TPU v7x, 32 devices: a whole 2x2x4 slice. The times are simulated.
32 devices in a mesh: dp: 4 (over x, core), context: 8 (over z, y).
Axes of the slice: x: 2, y: 2, z: 4, core: 2. Of those that a mesh axis runs over, the one named last changes fastest.
Arguments:
- queries: bfloat16 [4, 2560, 4096], P('dp', 'context'), may hold values from -6 to 6
- keys: bfloat16 [4, 2560, 4096], P('dp', 'context'), may hold values from -6 to 6
- values: bfloat16 [4, 2560, 4096], P('dp', 'context'), may hold values from -6 to 6
- gain: float32 [4096], replicated, may hold values from 0.1 to 1.9
- out_grad: bfloat16 [4, 2560, 4096], P('dp', 'context'), may hold values from -6 to 6
Outputs:
- output: bfloat16 [4, 2560, 4096], P('dp', 'context')
- query_grad: bfloat16 [4, 2560, 4096], P('dp', 'context')
- key_grad: bfloat16 [4, 2560, 4096], P('dp', 'context')
- value_grad: bfloat16 [4, 2560, 4096], P('dp', 'context')
- gain_grad: float32 [4096], replicated
All inputs are finite; a program needn't handle non-finite values.
Results may differ from a plain program's by a relative error of at most 0.0064.
Values may be sent and summed in bfloat16 or wider, within the bound.
No kernel may reach another device: no remote copies, remote signals or barrier semaphores. Data moves between devices by JAX's collectives and lax.ppermute only.
A program may use at most 192 MiB of HBM per device.

v0:
```python
import jax
import jax.numpy as jnp
from jax import lax
from jax.sharding import PartitionSpec as P

HEADS = 32
HD = 128


epsilon = 1e-06


def carried_in(array, axis, join, neutral):
    place = lax.axis_index(axis)
    gathered = lax.all_gather(array.astype(jnp.bfloat16), axis)
    state = jnp.zeros_like(array) + jnp.asarray(neutral, array.dtype)

    def one(hop, state):
        return join(state, lax.dynamic_index_in_dim(gathered, hop, 0, False).astype(array.dtype))

    return lax.fori_loop(0, place, one, state)


def add_states(earlier, later_one):
    return earlier + later_one


def masked_fold(my_index, shard_piece):
    index_rows = lax.broadcasted_iota(jnp.int32, (shard_piece.shape[0],), 0)
    keep = (index_rows > my_index).astype(jnp.float32)
    return jnp.tensordot(keep, shard_piece.astype(jnp.float32), axes=1)


def shards(queries, keys, values, gain, out_grad):
    tok_rows = queries.shape[1]
    local_query_rows = queries[0].reshape(tok_rows, HEADS, HD)
    local_key_rows = keys[0].reshape(tok_rows, HEADS, HD)
    local_value_rows = values[0].reshape(tok_rows, HEADS, HD)
    my_index = lax.axis_index("context")
    zero_state = jnp.zeros((HEADS, HD, HD), jnp.float32)
    causal = lax.broadcasted_iota(jnp.int32, (tok_rows, tok_rows), 0) >= lax.broadcasted_iota(
        jnp.int32, (tok_rows, tok_rows), 1
    )
    block_state = jnp.einsum(
        "uwc,uwg->wcg", local_key_rows, local_value_rows, preferred_element_type=jnp.float32
    ).astype(jnp.bfloat16)
    prior_state = carried_in(block_state.astype(jnp.float32), "context", add_states, zero_state)
    preceding_block = prior_state.astype(jnp.bfloat16)
    scores = jnp.einsum(
        "thk,shk->hts", local_query_rows, local_key_rows, preferred_element_type=jnp.float32
    )
    attn_weights = jnp.where(causal, scores, 0.0).astype(jnp.bfloat16)
    mixed_out = jnp.einsum(
        "hts,shv->thv", attn_weights, local_value_rows, preferred_element_type=jnp.float32
    )
    mixed_out = mixed_out + jnp.einsum(
        "lyq,yqd->lyd", local_query_rows, preceding_block, preferred_element_type=jnp.float32
    )
    mixed_out = mixed_out.reshape(tok_rows, HEADS * HD)
    inv_rms = lax.rsqrt(jnp.mean(mixed_out * mixed_out, -1, keepdims=True) + epsilon)
    normed = mixed_out * inv_rms
    output = (normed * gain).astype(jnp.bfloat16)
    grad_out = out_grad[0].astype(jnp.float32)
    gain_part = jnp.sum(grad_out * normed, 0)
    scaled = gain * grad_out
    centered_input = jnp.mean(scaled * mixed_out, -1, keepdims=True)
    mixed_gradient = (
        inv_rms * scaled - mixed_out * inv_rms * inv_rms * inv_rms * centered_input
    ).astype(jnp.bfloat16)
    mixed_gradient = mixed_gradient.reshape(tok_rows, HEADS, HD)
    state_grad = jnp.einsum(
        "uwc,uwg->wcg", local_query_rows, mixed_gradient, preferred_element_type=jnp.float32
    ).astype(jnp.bfloat16)
    later_state = masked_fold(
        my_index, lax.all_gather(state_grad[None], "context", axis=0, tiled=True)
    )
    following_block = later_state.astype(jnp.bfloat16)
    d_scores = jnp.einsum(
        "thv,shv->hts", mixed_gradient, local_value_rows, preferred_element_type=jnp.float32
    )
    d_weights = jnp.where(causal, d_scores, 0.0).astype(jnp.bfloat16)
    query_grad = jnp.einsum(
        "hts,shk->thk", d_weights, local_key_rows, preferred_element_type=jnp.float32
    )
    query_grad = query_grad + jnp.einsum(
        "mqy,qsy->mqs", mixed_gradient, preceding_block, preferred_element_type=jnp.float32
    )
    key_grad = jnp.einsum(
        "hts,thk->shk", d_weights, local_query_rows, preferred_element_type=jnp.float32
    )
    key_grad = key_grad + jnp.einsum(
        "mqy,qsy->mqs", local_value_rows, following_block, preferred_element_type=jnp.float32
    )
    value_grad = jnp.einsum(
        "hts,thv->shv", attn_weights, mixed_gradient, preferred_element_type=jnp.float32
    )
    value_grad = value_grad + jnp.einsum(
        "lyq,yqd->lyd", local_key_rows, following_block, preferred_element_type=jnp.float32
    )
    gain_grad = lax.psum(gain_part, ("dp", "context"))
    flat = (1, tok_rows, HEADS * HD)
    return (
        output[None],
        query_grad.reshape(flat).astype(jnp.bfloat16),
        key_grad.reshape(flat).astype(jnp.bfloat16),
        value_grad.reshape(flat).astype(jnp.bfloat16),
        gain_grad,
    )


def solution(mesh):
    in_specs = (
        P("dp", "context", None),
        P("dp", "context", None),
        P("dp", "context", None),
        P(),
        P("dp", "context", None),
    )
    out_specs = (
        P("dp", "context", None),
        P("dp", "context", None),
        P("dp", "context", None),
        P("dp", "context", None),
        P(),
    )
    return jax.shard_map(shards, mesh=mesh, in_specs=in_specs, out_specs=out_specs, check_vma=False)
```

profile of v0, /device:TPU:0, one launch (start us, length us, event | category | flops | bytes accessed | tf_op | source)
XLA Modules:
  0.0 348.8 jit_solution(7413628201742579282)
XLA Ops:
  7.2 0.0 all-gather.5.cloned.1.call-start
  7.2 2.5 copy.72
  9.7 0.0 copy-start.11
  9.7 0.0 copy-done.15
  9.7 0.6 copy.73
  10.4 0.8 copy-done.11
  11.2 4.7 %fusion.28 = bf16[32,128,128]{2,1,0:T(8,128)(2,1)} fusion(bf16[320,32,128]{2,1,0:T(8,128)(2,1)S(1)} %bitcast.77, bf16[320,32,128]{2,1,0:T(8,128)(2,1)S(1)} %bitcast.81), kind=kOutput, calls=%fused_computation.41 | convolution fusion | flops 336068608 | bytes 6291456 | tf_op jit(solution)/shard_map/uwc,uwg->wcg/dot_general | solution.py:44
  15.9 0.0 all-gather.5.cloned.1.call-update
  15.9 0.3 all-gather.7.cloned.1.call-start
  16.2 2.5 copy.71
  18.7 0.0 copy-done.14
  18.8 0.6 convert_bitcast_fusion.1
  19.4 3.3 copy.74
  22.7 9.2 %select_convert_fusion.1 = bf16[32,320,320]{2,1,0:T(8,128)(2,1)S(1)} fusion(pred[320,320]{1,0:T(8,128)(4,1)S(1)} %iota_compare_fusion, bf16[320,32,128]{2,1,0:T(8,128)(2,1)} %bitcast.82, bf16[320,32,128]{2,1,0:T(8,128)(2,1)S(1)} %bitcast.73), kind=kOutput, calls=%fused_computation.2 | convolution fusion | flops 845414400 | bytes 11898880 | tf_op jit(solution)/shard_map/thk,shk->hts/dot_general | solution.py:49
  31.9 3.1 copy-done.7
  35.0 5.4 %fusion.11 = f32[32,320,128]{2,1,0:T(8,128)} fusion(bf16[32,320,320]{2,1,0:T(8,128)(2,1)S(1)} %select_convert_fusion.1, bf16[320,32,128]{2,1,0:T(8,128)(2,1)S(1)} %bitcast.78), kind=kOutput, calls=%fused_computation.26 | convolution fusion | flops 838860800 | bytes 14417920 | tf_op jit(solution)/shard_map/hts,shv->thv/dot_general | solution.py:53
  40.4 103.3 %all-gather.5.cloned.1.call-done = bf16[256,128,128]{2,1,0:T(8,128)(2,1)} async-done(((bf16[32,128,128]{2,1,0:T(8,128)(2,1)}), bf16[256,128,128]{2,1,0:T(8,128)(2,1)}) %all-gather.5.cloned.1.call-update) | async-done | bytes 8388624 | tf_op jit(solution)/shard_map/all_gather | solution.py:15
  143.7 0.2 broadcast_in_dim.25
  144.0 0.3 while.10
  144.3 0.4 copy-done.16
  144.7 9.8 %multiply_reduce_fusion = (f32[320]{0:T(512)S(1)}, f32[320]{0:T(512)S(1)}, f32[320,32,128]{2,0,1:T(8,128)S(1)}) fusion(f32[320,32,128]{2,1,0:T(8,128)} %bitcast.69, f32[32,128]{1,0:T(8,128)S(1)} %bitcast.92, f32[32,128,128]{2,1,0:T(8,128)S(1)} %get-tuple-element.28, bf16[320,32,128]{2,1,0:T(8,128)(2,1)} %bitcast.74, f32[32,320,128]{2,1,0:T(8,128)} %fusion.11), kind=kOutput, calls=%fused_computation.18 | convolution fusion | flops 343932288 | bytes 20466176 | tf_op jit(solution)/shard_map/lyq,yqd->lyd/dot_general | solution.py:56
  154.5 4.1 %subtract_convert_fusion = bf16[320,32,128]{2,0,1:T(8,128)(2,1)S(1)} fusion(f32[320,32,128]{2,0,1:T(8,128)S(1)} %get-tuple-element.39, f32[320,32,128]{2,1,0:T(8,128)S(1)} %bitcast.72, f32[320]{0:T(512)S(1)} %broadcast_multiply_fusion, f32[32,128]{1,0:T(8,128)S(1)} %bitcast.93, f32[320]{0:T(512)S(1)} %add_rsqrt_fusion), kind=kLoop, calls=%fused_computation.17 | loop fusion | flops 10485760 | bytes 13126144 | tf_op jit(solution)/shard_map/convert_element_type | solution.py:69
  158.7 1.5 copy-done.1
  160.2 3.3 fusion.33
  163.5 1.3 copy.58
  164.8 0.0 all-gather.7.cloned.1.call-update
  164.8 7.8 %copy.50 = f32[320,32,128]{2,1,0:T(8,128)} copy(f32[320,32,128]{2,0,1:T(8,128)} %copy-done) | data formatting | bytes 10485760 | tf_op jit(solution)/shard_map/add | solution.py:56
  172.6 7.0 %reshape.168 = f32[1,320,4096]{2,1,0:T(8,128)} reshape(f32[320,32,128]{2,1,0:T(8,128)} %copy.50) | data formatting | bytes 10485760 | tf_op jit(solution)/shard_map/reshape | solution.py:59
  179.6 6.4 %select_convert_fusion = bf16[32,320,320]{2,1,0:T(8,128)(2,1)S(1)} fusion(bf16[320,32,128]{2,0,1:T(8,128)(2,1)} %copy-done.1, pred[320,320]{1,0:T(8,128)(4,1)S(1)} %iota_compare_fusion, bf16[320,32,128]{2,1,0:T(8,128)(2,1)} %bitcast.79), kind=kOutput, calls=%fused_computation.1 | convolution fusion | flops 845414400 | bytes 11898880 | tf_op jit(solution)/shard_map/thv,shv->hts/dot_general | solution.py:78
  186.0 3.4 fusion.15
  189.5 0.2 copy-done.8
  189.6 0.1 copy-done.2
  189.7 1.0 fusion.5
  190.7 1.7 copy.54
  192.4 3.1 convert_element_type.112
  195.5 4.4 %fusion.3 = f32[4096]{0:T(1024)S(1)} fusion(bf16[1,320,4096]{2,1,0:T(8,128)(2,1)} %param.11, f32[320]{0:T(512)S(1)} %add_rsqrt_fusion, f32[320,32,128]{2,0,1:T(8,128)} %copy-done), kind=kLoop, calls=%fused_computation.8 | loop fusion | flops 5238784 | bytes 7881984 | tf_op jit(solution)/shard_map/reduce_sum | solution.py:64
  199.9 53.4 %psum.7 = f32[4096]{0:T(1024)} all-reduce(f32[4096]{0:T(1024)S(1)} %fusion.3), channel_id=1, replica_groups=mesh['dp'=4,'context'=8] {'dp','context'}, use_global_device_ids=true, to_apply=%region_5.6 | all-reduce | flops 4096 | bytes 32768 | tf_op jit(solution)/shard_map/psum | solution.py:100
  253.2 9.5 %fusion.21 = f32[32,320,128]{2,1,0:T(8,128)} fusion(bf16[32,320,320]{2,1,0:T(8,128)(2,1)} %copy-done.8, bf16[320,32,128]{2,1,0:T(8,128)(2,1)S(1)} %bitcast.76), kind=kOutput, calls=%fused_computation.36 | convolution fusion | flops 838860800 | bytes 14417920 | tf_op jit(solution)/shard_map/hts,thk->shk/dot_general | solution.py:88
  262.8 4.8 %multiply_convert_fusion = bf16[1,320,4096]{2,1,0:T(8,128)(2,1)} fusion(f32[1,320,4096]{2,1,0:T(8,128)} %reshape.168, f32[4096]{0:T(1024)S(1)} %copy-done.16, f32[320]{0:T(512)S(1)} %add_rsqrt_fusion), kind=kLoop, calls=%fused_computation.19 | loop fusion | flops 3932160 | bytes 7881984 | tf_op jit(solution)/shard_map/convert_element_type | solution.py:62
  267.6 33.0 %all-gather.7.cloned.1.call-done = bf16[256,128,128]{2,1,0:T(8,128)(2,1)} async-done(((bf16[32,128,128]{2,1,0:T(8,128)(2,1)}), bf16[256,128,128]{2,1,0:T(8,128)(2,1)}) %all-gather.7.cloned.1.call-update) | async-done | bytes 8388624 | tf_op jit(solution)/shard_map/all_gather | solution.py:75
  300.6 10.3 %fusion = f32[1,32,128,128]{3,0,2,1:T(1,128)} fusion(bf16[8,32,128,128]{3,2,1,0:T(8,128)(2,1)} %bitcast.87, s32[]{:T(128)} %axis_index.16), kind=kOutput, calls=%fused_computation.3 | convolution fusion | flops 8388616 | bytes 10485764 | tf_op jit(solution)/shard_map/dot_general | solution.py:31
  310.9 3.2 fusion.13
  314.1 7.7 %fusion.6 = bf16[320,32,128]{2,0,1:T(8,128)(2,1)} fusion(f32[32,128,320]{1,2,0:T(8,128)S(1)} %fusion.13, bf16[320,32,128]{2,0,1:T(8,128)(2,1)S(1)} %copy-done.3, bf16[32,320,320]{2,1,0:T(8,128)(2,1)} %copy-done.7), kind=kOutput, calls=%fused_computation.21 | convolution fusion | flops 841482240 | bytes 17039360 | tf_op jit(solution)/shard_map/hts,thv->shv/dot_general | solution.py:94
  321.7 4.9 %copy.63 = bf16[320,32,128]{2,1,0:T(8,128)(2,1)} copy(bf16[320,32,128]{2,0,1:T(8,128)(2,1)} %fusion.6) | data formatting | bytes 5242880 | tf_op jit(solution)/shard_map/convert_element_type | solution.py:106
  326.7 5.3 %convert_element_type.120 = bf16[1,320,4096]{2,1,0:T(8,128)(2,1)} reshape(bf16[320,32,128]{2,1,0:T(8,128)(2,1)} %copy.63) | data formatting | bytes 5242880 | tf_op jit(solution)/shard_map/convert_element_type | solution.py:106
  332.0 4.8 %fusion.4 = bf16[320,32,128]{2,0,1:T(8,128)(2,1)S(1)} fusion(f32[32,320,128]{2,1,0:T(8,128)} %fusion.21, bf16[320,32,128]{2,1,0:T(8,128)(2,1)S(1)} %bitcast.80, f32[32,128,128]{2,1,0:T(8,128)} %bitcast.86), kind=kOutput, calls=%fused_computation.11 | convolution fusion | flops 338690048 | bytes 12582912 | tf_op jit(solution)/shard_map/mqy,qsy->mqs/dot_general | solution.py:91
  336.8 1.7 copy.60
  338.5 3.1 convert_element_type.117
  (33 shorter events, 0.1 us)
Async XLA Ops:
  7.2 136.6 %all-gather.5.cloned.1.call-start = ((), (), s32[]{:S(2)}) async-start(), calls=%async_computation | async-start | bytes 9437184 | tf_op jit(solution)/shard_map/all_gather | solution.py:15
  7.2 2.5 copy-start.15
  9.7 1.5 copy-start.11
  10.4 21.5 %copy-start.9 = (bf16[40,8,32,128]{3,2,1,0:T(8,128)(2,1)}, bf16[40,8,32,128]{3,2,1,0:T(8,128)(2,1)S(1)}, u32[]{:S(2)}) copy-start(bf16[40,8,32,128]{3,2,1,0:T(8,128)(2,1)S(1)} %copy.73) | copy-start | bytes 7864324
  15.9 284.6 %all-gather.7.cloned.1.call-start = ((), (), s32[]{:S(2)}) async-start(), calls=%async_computation.1 | async-start | bytes 9437184 | tf_op jit(solution)/shard_map/all_gather | solution.py:75
  16.2 2.5 copy-start.14
  18.7 4.0 %copy-start.4 = (bf16[40,8,32,128]{3,2,1,0:T(8,128)(2,1)}, bf16[40,8,32,128]{3,2,1,0:T(8,128)(2,1)S(1)}, u32[]{:S(2)}) copy-start(bf16[40,8,32,128]{3,2,1,0:T(8,128)(2,1)S(1)} %copy.71) | copy-start | bytes 7864324
  31.9 3.1 copy-start.7
  144.0 0.7 copy-start.16
  144.3 10.2 %slice-start = ((s8[5242880]{0:T(1024)(128)(4,1)}), s8[4194304]{0:T(1024)(128)(4,1)S(1)}, s32[]{:S(2)}) async-start(s8[5242880]{0:T(1024)(128)(4,1)} %bitcast.70), calls=%async_computation.2 | async-start | bytes 8388608
  144.7 9.8 %slice-start.1 = ((s8[5242880]{0:T(1024)(128)(4,1)}), s8[1048576]{0:T(1024)(128)(4,1)S(1)}, s32[]{:S(2)}) async-start(s8[5242880]{0:T(1024)(128)(4,1)} %bitcast.70), calls=%async_computation.3 | async-start | bytes 2097152
  154.5 4.2 %copy-start = (f32[320,32,128]{2,0,1:T(8,128)}, f32[320,32,128]{2,0,1:T(8,128)S(1)}, u32[]{:S(2)}) copy-start(f32[320,32,128]{2,0,1:T(8,128)S(1)} %get-tuple-element.39) | copy-start | bytes 15728644
  154.5 5.6 %copy-start.5 = (bf16[40,8,32,128]{3,2,1,0:T(8,128)(2,1)S(1)}, bf16[40,8,32,128]{3,2,1,0:T(8,128)(2,1)}, u32[]{:S(2)}) copy-start(bf16[40,8,32,128]{3,2,1,0:T(8,128)(2,1)} %copy-done.4) | copy-start | bytes 7864324
  158.7 1.5 copy-start.1
  179.6 6.4 %copy-start.12 = (bf16[40,8,32,128]{3,2,1,0:T(8,128)(2,1)S(1)}, bf16[40,8,32,128]{3,2,1,0:T(8,128)(2,1)}, u32[]{:S(2)}) copy-start(bf16[40,8,32,128]{3,2,1,0:T(8,128)(2,1)} %copy-done.11) | copy-start | bytes 7864324
  186.0 3.6 %copy-start.8 = (bf16[32,320,320]{2,1,0:T(8,128)(2,1)}, bf16[32,320,320]{2,1,0:T(8,128)(2,1)S(1)}, u32[]{:S(2)}) copy-start(bf16[32,320,320]{2,1,0:T(8,128)(2,1)S(1)} %select_convert_fusion) | copy-start | bytes 19660804
  186.0 3.7 %copy-start.2 = (bf16[320,32,128]{2,0,1:T(8,128)(2,1)S(1)}, bf16[320,32,128]{2,0,1:T(8,128)(2,1)}, u32[]{:S(2)}) copy-start(bf16[320,32,128]{2,0,1:T(8,128)(2,1)} %copy-done.1) | copy-start | bytes 7864324
  195.5 57.8 %copy-start.6 = (bf16[40,8,32,128]{3,2,1,0:T(8,128)(2,1)S(1)}, bf16[40,8,32,128]{3,2,1,0:T(8,128)(2,1)}, u32[]{:S(2)}) copy-start(bf16[40,8,32,128]{3,2,1,0:T(8,128)(2,1)} %copy-done.4) | copy-start | bytes 7864324
  300.5 10.3 %copy-start.13 = (bf16[40,8,32,128]{3,2,1,0:T(8,128)(2,1)S(1)}, bf16[40,8,32,128]{3,2,1,0:T(8,128)(2,1)}, u32[]{:S(2)}) copy-start(bf16[40,8,32,128]{3,2,1,0:T(8,128)(2,1)} %copy-done.11) | copy-start | bytes 7864324
  310.9 3.2 copy-start.3
  326.7 5.3 %copy-start.10 = (bf16[40,8,32,128]{3,2,1,0:T(8,128)(2,1)S(1)}, bf16[40,8,32,128]{3,2,1,0:T(8,128)(2,1)}, u32[]{:S(2)}) copy-start(bf16[40,8,32,128]{3,2,1,0:T(8,128)(2,1)} %copy-done.9) | copy-start | bytes 7864324
Sparse Core Ops, SparseCore 0:
  16.1 127.6 all-gather.4
  164.9 135.5 all-gather.6
where the time goes:
time: 353 us; the launch traced here: 349 us
  waiting for transfers between devices  136 us (39%)
  matrix products  78.6 us (22%)
  blocking collectives  53.4 us (15%)
  local copies, waits for them, and re-layouts  51.1 us (14%)
  between operations  14.8 us (4%)
  other arithmetic  14 us (4%)
    all_gather x1, waiting for transfers between devices, carried_in(): gathered = lax.all_gather(array.astype(jnp.bfloat16), axis)  103 us
    psum x1, blocking collectives, shards(): gain_grad = lax.psum(gain_part, ('dp', 'context'))  53.4 us
    all_gather x1, waiting for transfers between devices, shards(): lax.all_gather(state_grad[None], 'context', axis=0, tiled=True)  33 us
    unnamed x42, local copies, waits for them, and re-layouts  15 us
    dot_general x1, matrix products, masked_fold(): return jnp.tensordot(keep, shard_piece.astype(jnp.float32), axes=1)  10.3 us
    convert_element_type x2, local copies, waits for them, and re-layouts, shards(): value_grad.reshape(flat).astype(jnp.bfloat16)  10.2 us
    dot_general x1, matrix products, shards(): jnp.einsum('lyq,yqd->lyd', local_query_rows, preceding_block, preferred_e...  9.76 us
    dot_general x1, matrix products, shards(): jnp.einsum('hts,thk->shk', d_weights, local_query_rows, preferred_element...  9.53 us
  transfers between devices with their start and end apart: 2, of which 2 were waited for; matrix products, arithmetic and copies ran while one was open for 20% of the time, Pallas kernels for 0%

commit v1 on v0

v1 whole, which is shorter than its diff:
```python
import functools

import jax
import jax.numpy as jnp
from jax import lax
from jax.experimental import pallas as pl
from jax.experimental.pallas import tpu as pltpu
from jax.sharding import PartitionSpec as P

HD = 128
EPSILON = 1e-06
BF16 = jnp.bfloat16
F32 = jnp.float32
VMEM_LIMIT = 40 * 1024 * 1024


def dot(a, b, contract):
    return lax.dot_general(a, b, ((contract[:1], contract[1:]), ((), ())), preferred_element_type=F32)


def divisor(n, choices):
    return next(c for c in choices if n % c == 0)


def lanes(head):
    return slice(head * HD, (head + 1) * HD)


class Layout:
    def __init__(self, tokens, features, members):
        self.tokens = tokens
        self.heads = features // HD
        self.members = members
        self.per_piece = self.heads // members
        self.per_step = divisor(self.per_piece, (4, 2, 1))
        self.steps = self.per_piece // self.per_step
        self.grid = (members, self.steps)

    def natural(self):
        steps = self.steps
        return pl.BlockSpec((self.tokens, self.per_step * HD), lambda k, j, r: (0, (r[0] ^ k) * steps + j))

    def row(self):
        steps = self.steps
        return pl.BlockSpec((1, self.per_step * HD), lambda k, j, r: (0, (r[0] ^ k) * steps + j))

    def piece(self, mine):
        last = self.steps - 1
        return pl.BlockSpec(
            (self.per_step, HD, HD),
            lambda k, j, r: (jnp.where(k == mine, j, jnp.where(k > mine, last, 0)), 0, 0),
        )

    def pieces(self):
        return [self.piece(k) for k in range(self.members)]

    def whole(self):
        return pl.BlockSpec((self.tokens, HD), lambda k, j, r: (0, 0))

    def wide(self, kind):
        return jax.ShapeDtypeStruct((self.tokens, self.heads * HD), kind)

    def narrow(self):
        return jax.ShapeDtypeStruct((self.tokens, HD), F32)

    def piece_shapes(self):
        return [jax.ShapeDtypeStruct((self.per_piece, HD, HD), BF16)] * self.members

    def call(self, body, rank, operands, in_specs, out_specs, out_shape, macs, moved, scratch=()):
        return pl.pallas_call(
            body,
            grid_spec=pltpu.PrefetchScalarGridSpec(
                num_scalar_prefetch=1,
                grid=self.grid,
                in_specs=in_specs,
                out_specs=out_specs,
                scratch_shapes=list(scratch),
            ),
            out_shape=out_shape,
            compiler_params=pltpu.CompilerParams(vmem_limit_bytes=VMEM_LIMIT),
            cost_estimate=pl.CostEstimate(flops=2 * macs, bytes_accessed=moved, transcendentals=0),
        )(rank, *operands)


def for_piece(layout, refs, act):
    for k in range(layout.members):

        @pl.when(pl.program_id(0) == k)
        def _(k=k):
            act(refs[k])


def block_states(layout, rank, keys, values):
    def body(r, k_ref, v_ref, *outs):
        def act(out):
            for h in range(layout.per_step):
                out[h] = dot(k_ref[:, lanes(h)], v_ref[:, lanes(h)], (0, 0)).astype(BF16)

        for_piece(layout, outs, act)

    size = layout.tokens * layout.heads * HD
    return layout.call(
        body, rank, (keys, values), [layout.natural()] * 2, layout.pieces(), layout.piece_shapes(),
        size * HD, 4 * size,
    )


def causal_mask(tokens, upper):
    rows = lax.broadcasted_iota(jnp.int32, (tokens, tokens), 0)
    columns = lax.broadcasted_iota(jnp.int32, (tokens, tokens), 1)
    return rows <= columns if upper else rows >= columns


def within_block(layout, rank, queries, keys, values):
    def body(r, q_ref, k_ref, v_ref, o_ref):
        keep = causal_mask(layout.tokens, False)
        for h in range(layout.per_step):
            scores = dot(q_ref[:, lanes(h)], k_ref[:, lanes(h)], (1, 1))
            weights = jnp.where(keep, scores, 0.0).astype(BF16)
            o_ref[:, lanes(h)] = dot(weights, v_ref[:, lanes(h)], (1, 0))

    size = layout.tokens * layout.heads * HD
    return layout.call(
        body, rank, (queries, keys, values), [layout.natural()] * 3, layout.natural(), layout.wide(F32),
        2 * size * layout.tokens, 10 * size,
    )


def mix(layout, rank, inner, queries, out_grad, gain, prior):
    def body(r, o_ref, q_ref, g_ref, gain_ref, *refs):
        states, (m_ref, square_ref, cross_ref) = refs[: layout.members], refs[layout.members :]

        @pl.when((pl.program_id(0) == 0) & (pl.program_id(1) == 0))
        def _():
            square_ref[...] = jnp.zeros_like(square_ref)
            cross_ref[...] = jnp.zeros_like(cross_ref)

        def act(state):
            square, cross = square_ref[...], cross_ref[...]
            for h in range(layout.per_step):
                mixed = o_ref[:, lanes(h)] + dot(q_ref[:, lanes(h)], state[h], (1, 0))
                m_ref[:, lanes(h)] = mixed
                square = square + mixed * mixed
                cross = cross + gain_ref[:, lanes(h)] * g_ref[:, lanes(h)].astype(F32) * mixed
            square_ref[...] = square
            cross_ref[...] = cross

        for_piece(layout, states, act)

    size = layout.tokens * layout.heads * HD
    return layout.call(
        body, rank, (inner, queries, out_grad, gain, *prior),
        [layout.natural()] * 3 + [layout.row()] + layout.pieces(),
        [layout.natural(), layout.whole(), layout.whole()],
        [layout.wide(F32), layout.narrow(), layout.narrow()],
        size * HD, 12 * size,
    )


def mixed_gradients(layout, rank, mixed, queries, out_grad, gain, square, cross):
    features = layout.heads * HD

    def body(r, m_ref, q_ref, g_ref, gain_ref, square_ref, cross_ref, d_ref, inv_ref, *rest):
        outs, factor_ref = rest[:-1], rest[-1]

        @pl.when((pl.program_id(0) == 0) & (pl.program_id(1) == 0))
        def _():
            mean = jnp.sum(square_ref[...], -1, keepdims=True) / features
            inv = lax.rsqrt(mean + EPSILON)
            centered = jnp.sum(cross_ref[...], -1, keepdims=True) / features
            inv_ref[...] = jnp.broadcast_to(inv, inv_ref.shape)
            factor_ref[...] = jnp.broadcast_to(inv * inv * inv * centered, factor_ref.shape)

        def act(out):
            for h in range(layout.per_step):
                scaled = gain_ref[:, lanes(h)] * g_ref[:, lanes(h)].astype(F32)
                grad = (inv_ref[...] * scaled - m_ref[:, lanes(h)] * factor_ref[...]).astype(BF16)
                d_ref[:, lanes(h)] = grad
                out[h] = dot(q_ref[:, lanes(h)], grad, (0, 0)).astype(BF16)

        for_piece(layout, outs, act)

    size = layout.tokens * layout.heads * HD
    return layout.call(
        body, rank, (mixed, queries, out_grad, gain, square, cross),
        [layout.natural()] * 3 + [layout.row(), layout.whole(), layout.whole()],
        [layout.natural(), layout.whole()] + layout.pieces(),
        [layout.wide(BF16), layout.narrow()] + layout.piece_shapes(),
        size * HD, 10 * size, [pltpu.VMEM((layout.tokens, HD), F32)],
    )


def normed_output(layout, rank, mixed, out_grad, gain, inv):
    def body(r, m_ref, g_ref, gain_ref, inv_ref, o_ref, part_ref):
        for h in range(layout.per_step):
            normed = m_ref[:, lanes(h)] * inv_ref[...]
            o_ref[:, lanes(h)] = (normed * gain_ref[:, lanes(h)]).astype(BF16)
            part_ref[:, lanes(h)] = jnp.sum(g_ref[:, lanes(h)].astype(F32) * normed, 0, keepdims=True)

    size = layout.tokens * layout.heads * HD
    return layout.call(
        body, rank, (mixed, out_grad, gain, inv),
        [layout.natural()] * 2 + [layout.row(), layout.whole()],
        [layout.natural(), layout.row()],
        [layout.wide(BF16), jax.ShapeDtypeStruct((1, layout.heads * HD), F32)],
        0, 8 * size,
    )


def inner_gradients(layout, rank, queries, keys, values, d_mixed, prior):
    def body(r, q_ref, k_ref, v_ref, d_ref, *refs):
        states, (dq_ref, dk_ref, dv_ref) = refs[: layout.members], refs[layout.members :]
        lower = causal_mask(layout.tokens, False)
        upper = causal_mask(layout.tokens, True)

        def act(state):
            for h in range(layout.per_step):
                q, k, v, d = (ref[:, lanes(h)] for ref in (q_ref, k_ref, v_ref, d_ref))
                d_weights = jnp.where(lower, dot(d, v, (1, 1)), 0.0).astype(BF16)
                dq_ref[:, lanes(h)] = (dot(d_weights, k, (1, 0)) + dot(d, state[h], (1, 1))).astype(BF16)
                d_turned = jnp.where(upper, dot(v, d, (1, 1)), 0.0).astype(BF16)
                dk_ref[:, lanes(h)] = dot(d_turned, q, (1, 0))
                turned = jnp.where(upper, dot(k, q, (1, 1)), 0.0).astype(BF16)
                dv_ref[:, lanes(h)] = dot(turned, d, (1, 0))

        for_piece(layout, states, act)

    size = layout.tokens * layout.heads * HD
    return layout.call(
        body, rank, (queries, keys, values, d_mixed, *prior),
        [layout.natural()] * 4 + layout.pieces(),
        [layout.natural()] * 3,
        [layout.wide(BF16), layout.wide(F32), layout.wide(F32)],
        size * (6 * layout.tokens + HD), 18 * size,
    )


def outer_gradients(layout, rank, keys, values, dk_inner, dv_inner, later):
    def body(r, k_ref, v_ref, dki_ref, dvi_ref, *refs):
        states, (dk_ref, dv_ref) = refs[: layout.members], refs[layout.members :]

        def act(state):
            for h in range(layout.per_step):
                k, v = k_ref[:, lanes(h)], v_ref[:, lanes(h)]
                dk_ref[:, lanes(h)] = (dki_ref[:, lanes(h)] + dot(v, state[h], (1, 1))).astype(BF16)
                dv_ref[:, lanes(h)] = (dvi_ref[:, lanes(h)] + dot(k, state[h], (1, 0))).astype(BF16)

        for_piece(layout, states, act)

    size = layout.tokens * layout.heads * HD
    return layout.call(
        body, rank, (keys, values, dk_inner, dv_inner, *later),
        [layout.natural()] * 4 + layout.pieces(),
        [layout.natural()] * 2,
        [layout.wide(BF16)] * 2,
        2 * size * HD, 16 * size,
    )


def swap(array, axis, size, k):
    return lax.ppermute(array, axis, [(c, c ^ k) for c in range(size)])


def carried(pieces, rank, size, members, forward):
    order = [k for k in range(members - 1, 0, -1)]
    got = {k: swap(pieces[k], "context", size, k) for k in order}
    got = {k: array.astype(F32) for k, array in [(0, pieces[0]), *got.items()]}
    total = sum(got[k] for k in range(members)).astype(BF16)
    base = jnp.zeros(total.shape, F32)
    for far in range(1, size // members):
        hop = far * members
        if forward:
            pairs = [(c, c + hop) for c in range(size - hop)]
        else:
            pairs = [(c + hop, c) for c in range(size - hop)]
        base = base + lax.ppermute(total, "context", pairs).astype(F32)
    result = [None] * members
    for k in [*order, 0]:
        held = base
        for j in range(members):
            if j != k:
                ahead = (rank ^ j) < (rank ^ k) if forward else (rank ^ j) > (rank ^ k)
                held = held + jnp.where(ahead, got[j], 0.0)
        held = held.astype(BF16)
        result[k] = swap(held, "context", size, k) if k else held
    return result


def summed(part, axis, size):
    if size & (size - 1):
        return lax.psum(part, axis)
    stride = 1
    while stride < size:
        span = divisor(size // stride, (4, 2))
        part = sum((swap(part, axis, size, k * stride) for k in range(1, span)), part)
        stride *= span
    return part


def shards(dp, context, queries, keys, values, gain, out_grad):
    tokens, features = queries.shape[1:]
    members = divisor(context, (4, 2, 1))
    layout = Layout(tokens, features, members)
    rank = lax.axis_index("context") % members
    place = rank.astype(jnp.int32).reshape(1)
    q, k, v, g = (array[0] for array in (queries, keys, values, out_grad))
    gain_row = gain.reshape(1, features)

    states = block_states(layout, place, k, v)
    inner = within_block(layout, place, q, k, v)
    prior = carried(states, rank, context, members, True)
    mixed, square, cross = mix(layout, place, inner, q, g, gain_row, prior)
    d_mixed, inv, *state_grads = mixed_gradients(layout, place, mixed, q, g, gain_row, square, cross)
    later = carried(state_grads, rank, context, members, False)
    output, gain_part = normed_output(layout, place, mixed, g, gain_row, inv)
    gain_part = gain_part.reshape(features // HD, HD)
    gain_grad = summed(summed(gain_part, "dp", dp), "context", context)
    query_grad, dk_inner, dv_inner = inner_gradients(layout, place, q, k, v, d_mixed, prior)
    key_grad, value_grad = outer_gradients(layout, place, k, v, dk_inner, dv_inner, later)
    return output[None], query_grad[None], key_grad[None], value_grad[None], gain_grad.reshape(features)


def solution(mesh):
    sharded = P("dp", "context", None)
    return jax.shard_map(
        functools.partial(shards, mesh.shape["dp"], mesh.shape["context"]),
        mesh=mesh,
        in_specs=(sharded, sharded, sharded, P(), sharded),
        out_specs=(sharded, sharded, sharded, sharded, P()),
        check_vma=False,
    )
```

time: 353 us -> 152 us (0.43); the launches traced: 349 us -> 151 us
  waiting for transfers between devices: 136 us -> 26.7 us
  matrix products: 78.6 us -> 0 us
  Pallas kernels: 0 us -> 59.8 us
  blocking collectives: 53.4 us -> 0 us
  starting transfers between devices: 0.29 us -> 37.2 us
  local copies, waits for them, and re-layouts: 51.1 us -> 21.8 us
  between operations: 14.8 us -> 0.88 us
  other arithmetic: 14 us -> 5.03 us
    all_gather x2 -> x0, waiting for transfers between devices: 136 us -> none  [the longest x1 103 us: carried_in(): gathered = lax.all_gather(array.astype(jnp.bfloat16), axis)]
    dot_general x13 -> x0, matrix products: 78.6 us -> none  [the longest x1 10.3 us: masked_fold(): return jnp.tensordot(keep, shard_piece.astype(jnp.float32), axes=1)]
    pallas_call x0 -> x7, Pallas kernels: none -> 59.8 us  [call(): pl.pallas_call(body, grid_spec=pltpu.PrefetchScalarGridSpec(num_scalar_pr...]
    psum x1 -> x0, blocking collectives: 53.4 us -> none  [shards(): gain_grad = lax.psum(gain_part, ('dp', 'context'))]
    ppermute x0 -> x21, starting transfers between devices: none -> 37.2 us  [the longest x19 30.4 us: swap(): return lax.ppermute(array, axis, [(c, c ^ k) for c in range(size)])]
    ppermute x0 -> x21, waiting for transfers between devices: none -> 26.7 us  [the longest x19 19.8 us: swap(): return lax.ppermute(array, axis, [(c, c ^ k) for c in range(size)])]
    convert_element_type x7 -> x0, local copies, waits for them, and re-layouts: 21.1 us -> none  [the longest x2 10.2 us: shards(): value_grad.reshape(flat).astype(jnp.bfloat16)]
    add x1 -> x0, local copies, waits for them, and re-layouts: 7.8 us -> none  [shards(): mixed_out + jnp.einsum('lyq,yqd->lyd', local_query_rows, preceding_block,...]
  transfers between devices with their start and end apart: 2 -> 21, of which waited for: 2 -> 10; matrix products, arithmetic and copies ran while one was open for 20% -> 2% of each run, Pallas kernels for 0% -> 23%
where the time goes in v1:
time: 152 us; the launch traced here: 151 us
  Pallas kernels  59.8 us (39%)
  starting transfers between devices  37.2 us (24%)
  waiting for transfers between devices  26.7 us (18%)
  local copies, waits for them, and re-layouts  21.8 us (14%)
  other arithmetic  5.03 us (3%)
    pallas_call x7, Pallas kernels, call(): pl.pallas_call(body, grid_spec=pltpu.PrefetchScalarGridSpec(num_scalar_pr...  59.8 us
    ppermute x19, starting transfers between devices, swap(): return lax.ppermute(array, axis, [(c, c ^ k) for c in range(size)])  30.4 us
    unnamed x50, local copies, waits for them, and re-layouts  21.8 us
    ppermute x19, waiting for transfers between devices, swap(): return lax.ppermute(array, axis, [(c, c ^ k) for c in range(size)])  19.8 us
    ppermute x2, waiting for transfers between devices, carried(): base = base + lax.ppermute(total, 'context', pairs).astype(F32)  6.84 us
    ppermute x2, starting transfers between devices, carried(): base = base + lax.ppermute(total, 'context', pairs).astype(F32)  6.79 us
    convert_element_type x2, other arithmetic, carried(): held = held.astype(BF16)  3.42 us
  transfers between devices with their start and end apart: 21, of which 10 were waited for; matrix products, arithmetic and copies ran while one was open for 2% of the time, Pallas kernels for 23%

profile of v1, /device:TPU:0, one launch (start us, length us, event | category | flops | bytes accessed | tf_op | source)
XLA Modules:
  0.0 151.4 jit_solution(5390317965089932673)
XLA Ops:
  0.7 1.7 %copy-done = bf16[1,320,4096]{2,1,0:T(8,128)(2,1)S(1)} copy-done((bf16[1,320,4096]{2,1,0:T(8,128)(2,1)S(1)}, bf16[1,320,4096]{2,1,0:T(8,128)(2,1)}, u32[]{:S(2)}) %copy-start) | copy-done | bytes 2621464
  2.4 1.7 %copy-done.2 = bf16[1,320,4096]{2,1,0:T(8,128)(2,1)S(1)} copy-done((bf16[1,320,4096]{2,1,0:T(8,128)(2,1)S(1)}, bf16[1,320,4096]{2,1,0:T(8,128)(2,1)}, u32[]{:S(2)}) %copy-start.2) | copy-done | bytes 2621464
  4.1 3.2 %shard_map.93 = (bf16[8,128,128]{2,1,0:T(8,128)(2,1)S(1)}, bf16[8,128,128]{2,1,0:T(8,128)(2,1)S(1)}, bf16[8,128,128]{2,1,0:T(8,128)(2,1)S(1)}, bf16[8,128,128]{2,1,0:T(8,128)(2,1)S(1)}) custom-call(s32[1]{0:T(128)} %bitcast.r, bf16[320,4096]{1,0:T(8,128)(2,1)S(1)} %bitcast.13, bf16[320,4096]{1,0:T(8,128)(2,1)S(1)} %bitcast.17), custom_call_target="tpu_custom_call" | custom-call | flops 335544320 | bytes 5242880 | tf_op jit(solution)/shard_map/pallas_call | solution.py:70
  7.3 3.0 %collective-permute-start = (bf16[8,128,128]{2,1,0:T(8,128)(2,1)S(1)}, bf16[8,128,128]{2,1,0:T(8,128)(2,1)S(1)}, u32[]{:S(2)}, u32[]{:S(2)}) collective-permute-start(bf16[8,128,128]{2,1,0:T(8,128)(2,1)S(1)} %get-tuple-element.26), channel_id=1, source_target_pairs={{0,1},{1,0},{2,3},{3,2},{4,5},{5,4},{6,7},{7,6},{8,9},{9,8},{10,11... | collective-permute-start | bytes 786440 | tf_op jit(solution)/shard_map/ppermute | solution.py:261
  10.4 1.6 %collective-permute-start.1 = (bf16[8,128,128]{2,1,0:T(8,128)(2,1)S(1)}, bf16[8,128,128]{2,1,0:T(8,128)(2,1)S(1)}, u32[]{:S(2)}, u32[]{:S(2)}) collective-permute-start(bf16[8,128,128]{2,1,0:T(8,128)(2,1)S(1)} %get-tuple-element.27), channel_id=1, source_target_pairs={{0,2},{1,3},{2,0},{3,1},{4,6},{5,7},{6,4},{7,5},{8,10},{9,11},{10,... | collective-permute-start | bytes 786440 | tf_op jit(solution)/shard_map/ppermute | solution.py:261
  11.9 4.7 %collective-permute-done = bf16[8,128,128]{2,1,0:T(8,128)(2,1)S(1)} collective-permute-done((bf16[8,128,128]{2,1,0:T(8,128)(2,1)S(1)}, bf16[8,128,128]{2,1,0:T(8,128)(2,1)S(1)}, u32[]{:S(2)}, u32[]{:S(2)}) %collective-permute-start) | collective-permute-done | bytes 262176 | tf_op jit(solution)/shard_map/ppermute | solution.py:261
  16.7 2.9 %collective-permute-done.1 = bf16[8,128,128]{2,1,0:T(8,128)(2,1)S(1)} collective-permute-done((bf16[8,128,128]{2,1,0:T(8,128)(2,1)S(1)}, bf16[8,128,128]{2,1,0:T(8,128)(2,1)S(1)}, u32[]{:S(2)}, u32[]{:S(2)}) %collective-permute-start.1) | collective-permute-done | bytes 262176 | tf_op jit(solution)/shard_map/ppermute | solution.py:261
  19.6 3.9 %collective-permute-done.2 = bf16[8,128,128]{2,1,0:T(8,128)(2,1)S(1)} collective-permute-done((bf16[8,128,128]{2,1,0:T(8,128)(2,1)S(1)}, bf16[8,128,128]{2,1,0:T(8,128)(2,1)S(1)}, u32[]{:S(2)}, u32[]{:S(2)}) %collective-permute-start.2) | collective-permute-done | bytes 262176 | tf_op jit(solution)/shard_map/ppermute | solution.py:261
  23.7 0.6 copy-done.22
  24.2 5.3 %collective-permute-start.3 = (bf16[8,128,128]{2,1,0:T(8,128)(2,1)S(1)}, bf16[8,128,128]{2,1,0:T(8,128)(2,1)}, u32[]{:S(2)}, u32[]{:S(2)}) collective-permute-start(bf16[8,128,128]{2,1,0:T(8,128)(2,1)S(1)} %fusion.12), channel_id=1, source_target_pairs={{0,4},{1,5},{2,6},{3,7},{8,12},{9,13},{10,14},{11,15},{16,20},{17,... | collective-permute-start | bytes 786440 | tf_op jit(solution)/shard_map/ppermute | solution.py:276
  29.6 3.7 %collective-permute-done.3 = bf16[8,128,128]{2,1,0:T(8,128)(2,1)} collective-permute-done((bf16[8,128,128]{2,1,0:T(8,128)(2,1)S(1)}, bf16[8,128,128]{2,1,0:T(8,128)(2,1)}, u32[]{:S(2)}, u32[]{:S(2)}) %collective-permute-start.3) | collective-permute-done | bytes 262176 | tf_op jit(solution)/shard_map/ppermute | solution.py:276
  33.3 1.7 %fusion.5 = (bf16[8,128,128]{2,1,0:T(8,128)(2,1)S(1)}, bf16[8,128,128]{2,1,0:T(8,128)(2,1)S(1)}, bf16[8,128,128]{2,1,0:T(8,128)(2,1)S(1)}, bf16[8,128,128]{2,1,0:T(8,128)(2,1)S(1)}) fusion(bf16[8,128,128]{2,1,0:T(8,128)(2,1)S(1)} %collective-permute-done, bf16[8,128,128]{2,1,0:T(8,128)(2,1)} %copy-done.21, bf16[8,128,128]{2,1,0:T(8,128)(2,1)S(1)} %get-tuple-element.25, ...), kind=kLoop, calls=%fused_computation.43 | loop fusion | flops 4325376 | bytes 2359308 | tf_op jit(solution)/shard_map/convert_element_type | solution.py:284
  35.0 8.1 %collective-permute-start.6 = (bf16[8,128,128]{2,1,0:T(8,128)(2,1)S(1)}, bf16[8,128,128]{2,1,0:T(8,128)(2,1)S(1)}, u32[]{:S(2)}, u32[]{:S(2)}) collective-permute-start(bf16[8,128,128]{2,1,0:T(8,128)(2,1)S(1)} %get-tuple-element.49), channel_id=1, source_target_pairs={{0,3},{1,2},{2,1},{3,0},{4,7},{5,6},{6,5},{7,4},{8,11},{9,10},{10,... | collective-permute-start | bytes 786440 | tf_op jit(solution)/shard_map/ppermute | solution.py:261
  43.0 0.5 collective-permute-start.4
  43.7 1.7 %copy-done.3 = bf16[1,320,4096]{2,1,0:T(8,128)(2,1)S(1)} copy-done((bf16[1,320,4096]{2,1,0:T(8,128)(2,1)S(1)}, bf16[1,320,4096]{2,1,0:T(8,128)(2,1)}, u32[]{:S(2)}) %copy-start.3) | copy-done | bytes 2621464
  45.4 1.7 %copy-done.5 = bf16[1,320,4096]{2,1,0:T(8,128)(2,1)S(1)} copy-done((bf16[1,320,4096]{2,1,0:T(8,128)(2,1)S(1)}, bf16[1,320,4096]{2,1,0:T(8,128)(2,1)}, u32[]{:S(2)}) %copy-start.5) | copy-done | bytes 2621464
  47.1 8.5 %shard_map.92.o_ref = f32[320,4096]{1,0:T(8,128)S(1)} custom-call(s32[1]{0:T(128)} %bitcast.r, bf16[320,4096]{1,0:T(8,128)(2,1)S(1)} %bitcast.21, bf16[320,4096]{1,0:T(8,128)(2,1)S(1)} %bitcast.14, bf16[320,4096]{1,0:T(8,128)(2,1)S(1)} %bitcast.18), custom_call_target="tpu_custom_call" | custom-call | flops 1677721600 | bytes 13107200 | tf_op jit(solution)/shard_map/pallas_call | solution.py:70
  55.6 2.3 %copy-done.8 = f32[320,4096]{1,0:T(8,128)} copy-done((f32[320,4096]{1,0:T(8,128)}, f32[320,4096]{1,0:T(8,128)S(1)}, u32[]{:S(2)}) %copy-start.8) | copy-done | bytes 5242904
  58.0 6.6 %shard_map.94 = (f32[320,4096]{1,0:T(8,128)S(1)}, f32[320,128]{1,0:T(8,128)S(1)}, f32[320,128]{1,0:T(8,128)S(1)}) custom-call(s32[1]{0:T(128)} %bitcast.r, f32[320,4096]{1,0:T(8,128)} %copy-done.8, bf16[320,4096]{1,0:T(8,128)(2,1)S(1)} %bitcast.22, bf16[320,4096]{1,0:T(8,128)(2,1)S(1)} %bitcast.25, f32[1,4096]{1,0:T(1,128)S(1)} %bitcast.30, ...), custom_call_target="tpu_custom_call" | custom-call | flops 335544320 | bytes 15728640 | tf_op jit(solution)/shard_map/pallas_call | solution.py:70
  64.6 2.3 %copy-done.9 = f32[320,4096]{1,0:T(8,128)} copy-done((f32[320,4096]{1,0:T(8,128)}, f32[320,4096]{1,0:T(8,128)S(1)}, u32[]{:S(2)}) %copy-start.9) | copy-done | bytes 5242904
  67.0 7.0 %shard_map.95 = (bf16[320,4096]{1,0:T(8,128)(2,1)S(1)}, f32[320,128]{1,0:T(8,128)S(1)}, bf16[8,128,128]{2,1,0:T(8,128)(2,1)S(1)}, bf16[8,128,128]{2,1,0:T(8,128)...) custom-call(s32[1]{0:T(128)} %bitcast.r, f32[320,4096]{1,0:T(8,128)} %copy-done.9, ...), custom_call_target="tpu_custom_call" | custom-call | flops 335544320 | bytes 13107200 | tf_op jit(solution)/shard_map/pallas_call | solution.py:70
  73.9 1.4 collective-permute-start.7
  75.4 2.0 %collective-permute-start.8 = (bf16[8,128,128]{2,1,0:T(8,128)(2,1)S(1)}, bf16[8,128,128]{2,1,0:T(8,128)(2,1)S(1)}, u32[]{:S(2)}, u32[]{:S(2)}) collective-permute-start(bf16[8,128,128]{2,1,0:T(8,128)(2,1)S(1)} %get-tuple-element.40), channel_id=1, source_target_pairs={{0,2},{1,3},{2,0},{3,1},{4,6},{5,7},{6,4},{7,5},{8,10},{9,11},{10,... | collective-permute-start | bytes 786440 | tf_op jit(solution)/shard_map/ppermute | solution.py:261
  77.5 4.0 %shard_map.96 = (bf16[320,4096]{1,0:T(8,128)(2,1)}, f32[1,4096]{1,0:T(1,128)S(1)}) custom-call(s32[1]{0:T(128)} %bitcast.r, f32[320,4096]{1,0:T(8,128)S(1)} %bitcast.29, bf16[320,4096]{1,0:T(8,128)(2,1)S(1)} %bitcast.27, f32[1,4096]{1,0:T(1,128)S(1)} %bitcast.32, f32[320,128]{1,0:T(8,128)S(1)} %get-tuple-element.32.inv_ref), custom_call_target="tpu_custom_call" | custom-call | bytes 10485760 | tf_op jit(solution)/shard_map/pallas_call | solution.py:70
  81.5 1.5 %collective-permute-start.15 = (f32[32,128]{1,0:T(8,128)S(1)}, f32[32,128]{1,0:T(8,128)S(1)}, u32[]{:S(2)}, u32[]{:S(2)}) collective-permute-start(f32[32,128]{1,0:T(8,128)S(1)} %bitcast.34), channel_id=1, source_target_pairs={{0,16},{8,24},{16,0},{24,8},{1,17},{9,25},{17,1},{25,9},{2,18},{10... | collective-permute-start | bytes 49160 | tf_op jit(solution)/shard_map/ppermute | solution.py:261
  83.0 0.3 collective-permute-start.14
  83.4 1.3 collective-permute-done.8
  84.6 3.8 %collective-permute-done.9 = bf16[8,128,128]{2,1,0:T(8,128)(2,1)S(1)} collective-permute-done((bf16[8,128,128]{2,1,0:T(8,128)(2,1)S(1)}, bf16[8,128,128]{2,1,0:T(8,128)(2,1)S(1)}, u32[]{:S(2)}, u32[]{:S(2)}) %collective-permute-start.9) | collective-permute-done | bytes 262176 | tf_op jit(solution)/shard_map/ppermute | solution.py:261
  88.5 0.8 fusion.25
  89.3 1.5 collective-permute-start.10
  90.8 2.6 %collective-permute-start.19 = (f32[32,128]{1,0:T(8,128)S(1)}, f32[32,128]{1,0:T(8,128)S(1)}, u32[]{:S(2)}, u32[]{:S(2)}) collective-permute-start(f32[32,128]{1,0:T(8,128)S(1)} %add_add_fusion.1), channel_id=1, source_target_pairs={{0,3},{1,2},{2,1},{3,0},{4,7},{5,6},{6,5},{7,4},{8,11},{9,10},{10,... | collective-permute-start | bytes 49160 | tf_op jit(solution)/shard_map/ppermute | solution.py:261
  93.8 0.6 collective-permute-start.17
  94.4 1.1 collective-permute-done.19
  95.5 1.7 %collective-permute-done.18 = f32[32,128]{1,0:T(8,128)S(1)} collective-permute-done((f32[32,128]{1,0:T(8,128)S(1)}, f32[32,128]{1,0:T(8,128)S(1)}, u32[]{:S(2)}, u32[]{:S(2)}) %collective-permute-start.18) | collective-permute-done | bytes 16416 | tf_op jit(solution)/shard_map/ppermute | solution.py:261
  97.5 4.6 %collective-permute-start.20 = (f32[32,128]{1,0:T(8,128)S(1)}, f32[32,128]{1,0:T(8,128)S(1)}, u32[]{:S(2)}, u32[]{:S(2)}) collective-permute-start(f32[32,128]{1,0:T(8,128)S(1)} %add_add_fusion), channel_id=1, source_target_pairs={{0,4},{1,5},{2,6},{3,7},{4,0},{5,1},{6,2},{7,3},{8,12},{9,13},{10,... | collective-permute-start | bytes 49160 | tf_op jit(solution)/shard_map/ppermute | solution.py:261
  102.1 3.1 %collective-permute-done.10 = bf16[8,128,128]{2,1,0:T(8,128)(2,1)} collective-permute-done((bf16[8,128,128]{2,1,0:T(8,128)(2,1)}, bf16[8,128,128]{2,1,0:T(8,128)(2,1)}, u32[]{:S(2)}, u32[]{:S(2)}) %collective-permute-start.10) | collective-permute-done | bytes 262176 | tf_op jit(solution)/shard_map/ppermute | solution.py:276
  105.3 1.8 %fusion.18 = (bf16[8,128,128]{2,1,0:T(8,128)(2,1)S(1)}, bf16[8,128,128]{2,1,0:T(8,128)(2,1)S(1)}, bf16[8,128,128]{2,1,0:T(8,128)(2,1)S(1)}, bf16[8,128,128]{2,1,0:T(8,128)(2,1)S(1)}) fusion(bf16[8,128,128]{2,1,0:T(8,128)(2,1)} %copy-done.18, bf16[8,128,128]{2,1,0:T(8,128)(2,1)} %copy-done.19, bf16[8,128,128]{2,1,0:T(8,128)(2,1)S(1)} %get-tuple-element.38, ...), kind=kLoop, calls=%fused_computation.56 | loop fusion | flops 4325376 | bytes 2359308 | tf_op jit(solution)/shard_map/convert_element_type | solution.py:284
  107.1 1.5 collective-permute-start.11
  108.5 2.0 %collective-permute-start.12 = (bf16[8,128,128]{2,1,0:T(8,128)(2,1)S(1)}, bf16[8,128,128]{2,1,0:T(8,128)(2,1)S(1)}, u32[]{:S(2)}, u32[]{:S(2)}) collective-permute-start(bf16[8,128,128]{2,1,0:T(8,128)(2,1)S(1)} %get-tuple-element.48), channel_id=1, source_target_pairs={{0,2},{1,3},{2,0},{3,1},{4,6},{5,7},{6,4},{7,5},{8,10},{9,11},{10,... | collective-permute-start | bytes 786440 | tf_op jit(solution)/shard_map/ppermute | solution.py:261
  110.6 1.7 %copy-done.4 = bf16[1,320,4096]{2,1,0:T(8,128)(2,1)S(1)} copy-done((bf16[1,320,4096]{2,1,0:T(8,128)(2,1)S(1)}, bf16[1,320,4096]{2,1,0:T(8,128)(2,1)}, u32[]{:S(2)}) %copy-start.4) | copy-done | bytes 2621464
  112.3 1.7 %copy-done.6 = bf16[1,320,4096]{2,1,0:T(8,128)(2,1)S(1)} copy-done((bf16[1,320,4096]{2,1,0:T(8,128)(2,1)S(1)}, bf16[1,320,4096]{2,1,0:T(8,128)(2,1)}, u32[]{:S(2)}) %copy-start.6) | copy-done | bytes 2621464
  114.0 0.9 copy-done.12
  115.0 0.9 copy-done.14
  115.9 1.7 %copy-done.17 = bf16[320,4096]{1,0:T(8,128)(2,1)S(1)} copy-done((bf16[320,4096]{1,0:T(8,128)(2,1)S(1)}, bf16[320,4096]{1,0:T(8,128)(2,1)}, u32[]{:S(2)}) %copy-start.17) | copy-done | bytes 2621464
  117.7 22.4 %shard_map.97 = (bf16[320,4096]{1,0:T(8,128)(2,1)}, f32[320,4096]{1,0:T(8,128)}, f32[320,4096]{1,0:T(8,128)}) custom-call(s32[1]{0:T(128)} %bitcast.r, bf16[320,4096]{1,0:T(8,128)(2,1)S(1)} %bitcast.24, bf16[320,4096]{1,0:T(8,128)(2,1)S(1)} %bitcast.15, bf16[320,4096]{1,0:T(8,128)(2,1)S(1)} %bitcast.19, bf16[320,4096]{1,0:T(8,128)(2,1)S(1)} %copy-done.17, ...), custom_call_target="tpu_custom_call" | custom-call | flops 5368709120 | bytes 23592960 | tf_op jit(solution)/shard_map/pallas_call | solution.py:70
  140.1 0.6 add_bitcast_fusion
  140.7 2.5 %copy-done.10 = f32[320,4096]{1,0:T(8,128)S(1)} copy-done((f32[320,4096]{1,0:T(8,128)S(1)}, f32[320,4096]{1,0:T(8,128)}, u32[]{:S(2)}) %copy-start.10) | copy-done | bytes 5242904
  143.2 8.2 %shard_map.98 = (bf16[320,4096]{1,0:T(8,128)(2,1)}, bf16[320,4096]{1,0:T(8,128)(2,1)}) custom-call(s32[1]{0:T(128)} %bitcast.r, bf16[320,4096]{1,0:T(8,128)(2,1)S(1)} %bitcast.16, bf16[320,4096]{1,0:T(8,128)(2,1)S(1)} %bitcast.20, f32[320,4096]{1,0:T(8,128)S(1)} %copy-done.10, f32[320,4096]{1,0:T(8,128)} %get-tuple-element.37.dvi_ref, ...), custom_call_target="tpu_custom_call" | custom-call | flops 671088640 | bytes 20971520 | tf_op jit(solution)/shard_map/pallas_call | solution.py:70
  (59 shorter events, 1.1 us)
Async XLA Ops:
  0.6 1.7 %copy-start = (bf16[1,320,4096]{2,1,0:T(8,128)(2,1)S(1)}, bf16[1,320,4096]{2,1,0:T(8,128)(2,1)}, u32[]{:S(2)}) copy-start(bf16[1,320,4096]{2,1,0:T(8,128)(2,1)} %param.6) | copy-start | bytes 7864324
  2.4 1.7 %copy-start.2 = (bf16[1,320,4096]{2,1,0:T(8,128)(2,1)S(1)}, bf16[1,320,4096]{2,1,0:T(8,128)(2,1)}, u32[]{:S(2)}) copy-start(bf16[1,320,4096]{2,1,0:T(8,128)(2,1)} %param.7) | copy-start | bytes 7864324
  7.3 36.3 %copy-start.1 = (bf16[1,320,4096]{2,1,0:T(8,128)(2,1)S(1)}, bf16[1,320,4096]{2,1,0:T(8,128)(2,1)}, u32[]{:S(2)}) copy-start(bf16[1,320,4096]{2,1,0:T(8,128)(2,1)} %param.6) | copy-start | bytes 7864324
  7.3 9.3 %collective-permute-start = (bf16[8,128,128]{2,1,0:T(8,128)(2,1)S(1)}, bf16[8,128,128]{2,1,0:T(8,128)(2,1)S(1)}, u32[]{:S(2)}, u32[]{:S(2)}) collective-permute-start(bf16[8,128,128]{2,1,0:T(8,128)(2,1)S(1)} %get-tuple-element.26), channel_id=1, source_target_pairs={{0,1},{1,0},{2,3},{3,2},{4,5},{5,4},{6,7},{7,6},{8,9},{9,8},{10,11... | collective-permute-start | bytes 786440 | tf_op jit(solution)/shard_map/ppermute | solution.py:261
  10.4 9.2 %collective-permute-start.1 = (bf16[8,128,128]{2,1,0:T(8,128)(2,1)S(1)}, bf16[8,128,128]{2,1,0:T(8,128)(2,1)S(1)}, u32[]{:S(2)}, u32[]{:S(2)}) collective-permute-start(bf16[8,128,128]{2,1,0:T(8,128)(2,1)S(1)} %get-tuple-element.27), channel_id=1, source_target_pairs={{0,2},{1,3},{2,0},{3,1},{4,6},{5,7},{6,4},{7,5},{8,10},{9,11},{10,... | collective-permute-start | bytes 786440 | tf_op jit(solution)/shard_map/ppermute | solution.py:261
  11.9 11.6 %collective-permute-start.2 = (bf16[8,128,128]{2,1,0:T(8,128)(2,1)S(1)}, bf16[8,128,128]{2,1,0:T(8,128)(2,1)S(1)}, u32[]{:S(2)}, u32[]{:S(2)}) collective-permute-start(bf16[8,128,128]{2,1,0:T(8,128)(2,1)S(1)} %get-tuple-element.28), channel_id=1, source_target_pairs={{0,3},{1,2},{2,1},{3,0},{4,7},{5,6},{6,5},{7,4},{8,11},{9,10},{10,... | collective-permute-start | bytes 786440 | tf_op jit(solution)/shard_map/ppermute | solution.py:261
  19.6 3.9 %copy-start.21 = (bf16[8,128,128]{2,1,0:T(8,128)(2,1)}, bf16[8,128,128]{2,1,0:T(8,128)(2,1)S(1)}, u32[]{:S(2)}) copy-start(bf16[8,128,128]{2,1,0:T(8,128)(2,1)S(1)} %collective-permute-done.1) | copy-start | bytes 786436
  23.5 0.7 copy-start.22
  24.2 9.0 %collective-permute-start.3 = (bf16[8,128,128]{2,1,0:T(8,128)(2,1)S(1)}, bf16[8,128,128]{2,1,0:T(8,128)(2,1)}, u32[]{:S(2)}, u32[]{:S(2)}) collective-permute-start(bf16[8,128,128]{2,1,0:T(8,128)(2,1)S(1)} %fusion.12), channel_id=1, source_target_pairs={{0,4},{1,5},{2,6},{3,7},{8,12},{9,13},{10,14},{11,15},{16,20},{17,... | collective-permute-start | bytes 786440 | tf_op jit(solution)/shard_map/ppermute | solution.py:276
  35.0 23.0 %collective-permute-start.6 = (bf16[8,128,128]{2,1,0:T(8,128)(2,1)S(1)}, bf16[8,128,128]{2,1,0:T(8,128)(2,1)S(1)}, u32[]{:S(2)}, u32[]{:S(2)}) collective-permute-start(bf16[8,128,128]{2,1,0:T(8,128)(2,1)S(1)} %get-tuple-element.49), channel_id=1, source_target_pairs={{0,3},{1,2},{2,1},{3,0},{4,7},{5,6},{6,5},{7,4},{8,11},{9,10},{10,... | collective-permute-start | bytes 786440 | tf_op jit(solution)/shard_map/ppermute | solution.py:261
  43.0 14.9 %collective-permute-start.4 = (bf16[8,128,128]{2,1,0:T(8,128)(2,1)S(1)}, bf16[8,128,128]{2,1,0:T(8,128)(2,1)S(1)}, u32[]{:S(2)}, u32[]{:S(2)}) collective-permute-start(bf16[8,128,128]{2,1,0:T(8,128)(2,1)S(1)} %get-tuple-element.50), channel_id=1, source_target_pairs={{0,1},{1,0},{2,3},{3,2},{4,5},{5,4},{6,7},{7,6},{8,9},{9,8},{10,11... | collective-permute-start | bytes 786440 | tf_op jit(solution)/shard_map/ppermute | solution.py:261
  43.5 14.4 %collective-permute-start.5 = (bf16[8,128,128]{2,1,0:T(8,128)(2,1)S(1)}, bf16[8,128,128]{2,1,0:T(8,128)(2,1)S(1)}, u32[]{:S(2)}, u32[]{:S(2)}) collective-permute-start(bf16[8,128,128]{2,1,0:T(8,128)(2,1)S(1)} %get-tuple-element.52), channel_id=1, source_target_pairs={{0,2},{1,3},{2,0},{3,1},{4,6},{5,7},{6,4},{7,5},{8,10},{9,11},{10,... | collective-permute-start | bytes 786440 | tf_op jit(solution)/shard_map/ppermute | solution.py:261
  43.6 1.7 %copy-start.3 = (bf16[1,320,4096]{2,1,0:T(8,128)(2,1)S(1)}, bf16[1,320,4096]{2,1,0:T(8,128)(2,1)}, u32[]{:S(2)}) copy-start(bf16[1,320,4096]{2,1,0:T(8,128)(2,1)} %param.7) | copy-start | bytes 7864324
  45.4 1.7 %copy-start.5 = (bf16[1,320,4096]{2,1,0:T(8,128)(2,1)S(1)}, bf16[1,320,4096]{2,1,0:T(8,128)(2,1)}, u32[]{:S(2)}) copy-start(bf16[1,320,4096]{2,1,0:T(8,128)(2,1)} %param.5) | copy-start | bytes 7864324
  47.1 10.9 %copy-start.7 = (bf16[1,320,4096]{2,1,0:T(8,128)(2,1)S(1)}, bf16[1,320,4096]{2,1,0:T(8,128)(2,1)}, u32[]{:S(2)}) copy-start(bf16[1,320,4096]{2,1,0:T(8,128)(2,1)} %param.9) | copy-start | bytes 7864324
  47.1 10.9 %copy-start.15 = (f32[4096]{0:T(1024)S(1)}, f32[4096]{0:T(1024)}, u32[]{:S(2)}) copy-start(f32[4096]{0:T(1024)} %param.8) | copy-start | bytes 49156
  55.6 2.3 %copy-start.8 = (f32[320,4096]{1,0:T(8,128)}, f32[320,4096]{1,0:T(8,128)S(1)}, u32[]{:S(2)}) copy-start(f32[320,4096]{1,0:T(8,128)S(1)} %shard_map.92.o_ref) | copy-start | bytes 15728644
  58.0 6.7 %copy-start.11 = (bf16[8,128,128]{2,1,0:T(8,128)(2,1)}, bf16[8,128,128]{2,1,0:T(8,128)(2,1)S(1)}, u32[]{:S(2)}) copy-start(bf16[8,128,128]{2,1,0:T(8,128)(2,1)S(1)} %collective-permute-done.4.refs_1_) | copy-start | bytes 786436
  58.0 6.6 %copy-start.13 = (bf16[8,128,128]{2,1,0:T(8,128)(2,1)}, bf16[8,128,128]{2,1,0:T(8,128)(2,1)S(1)}, u32[]{:S(2)}) copy-start(bf16[8,128,128]{2,1,0:T(8,128)(2,1)S(1)} %collective-permute-done.5.refs_2_) | copy-start | bytes 786436
  64.6 2.3 %copy-start.9 = (f32[320,4096]{1,0:T(8,128)}, f32[320,4096]{1,0:T(8,128)S(1)}, u32[]{:S(2)}) copy-start(f32[320,4096]{1,0:T(8,128)S(1)} %get-tuple-element.29.m_ref) | copy-start | bytes 15728644
  67.0 10.5 %slice-start = ((s8[5242880]{0:T(1024)(128)(4,1)}), s8[4194304]{0:T(1024)(128)(4,1)S(1)}, s32[]{:S(2)}) async-start(s8[5242880]{0:T(1024)(128)(4,1)} %bitcast.28), calls=%async_computation | async-start | bytes 8388608
  67.0 10.5 %slice-start.1 = ((s8[5242880]{0:T(1024)(128)(4,1)}), s8[1048576]{0:T(1024)(128)(4,1)S(1)}, s32[]{:S(2)}) async-start(s8[5242880]{0:T(1024)(128)(4,1)} %bitcast.28), calls=%async_computation.1 | async-start | bytes 2097152
  73.9 7.6 %copy-start.16 = (bf16[320,4096]{1,0:T(8,128)(2,1)}, bf16[320,4096]{1,0:T(8,128)(2,1)S(1)}, u32[]{:S(2)}) copy-start(bf16[320,4096]{1,0:T(8,128)(2,1)S(1)} %get-tuple-element.34.d_ref) | copy-start | bytes 7864324
  73.9 9.1 %collective-permute-start.7 = (bf16[8,128,128]{2,1,0:T(8,128)(2,1)S(1)}, bf16[8,128,128]{2,1,0:T(8,128)(2,1)S(1)}, u32[]{:S(2)}, u32[]{:S(2)}) collective-permute-start(bf16[8,128,128]{2,1,0:T(8,128)(2,1)S(1)} %get-tuple-element.39), channel_id=1, source_target_pairs={{0,1},{1,0},{2,3},{3,2},{4,5},{5,4},{6,7},{7,6},{8,9},{9,8},{10,11... | collective-permute-start | bytes 786440 | tf_op jit(solution)/shard_map/ppermute | solution.py:261
  75.4 9.2 %collective-permute-start.8 = (bf16[8,128,128]{2,1,0:T(8,128)(2,1)S(1)}, bf16[8,128,128]{2,1,0:T(8,128)(2,1)S(1)}, u32[]{:S(2)}, u32[]{:S(2)}) collective-permute-start(bf16[8,128,128]{2,1,0:T(8,128)(2,1)S(1)} %get-tuple-element.40), channel_id=1, source_target_pairs={{0,2},{1,3},{2,0},{3,1},{4,6},{5,7},{6,4},{7,5},{8,10},{9,11},{10,... | collective-permute-start | bytes 786440 | tf_op jit(solution)/shard_map/ppermute | solution.py:261
  77.4 11.1 %collective-permute-start.9 = (bf16[8,128,128]{2,1,0:T(8,128)(2,1)S(1)}, bf16[8,128,128]{2,1,0:T(8,128)(2,1)S(1)}, u32[]{:S(2)}, u32[]{:S(2)}) collective-permute-start(bf16[8,128,128]{2,1,0:T(8,128)(2,1)S(1)} %get-tuple-element.41), channel_id=1, source_target_pairs={{0,3},{1,2},{2,1},{3,0},{4,7},{5,6},{6,5},{7,4},{8,11},{9,10},{10,... | collective-permute-start | bytes 786440 | tf_op jit(solution)/shard_map/ppermute | solution.py:261
  81.5 9.3 %collective-permute-start.16 = (f32[32,128]{1,0:T(8,128)S(1)}, f32[32,128]{1,0:T(8,128)S(1)}, u32[]{:S(2)}, u32[]{:S(2)}) collective-permute-start(f32[32,128]{1,0:T(8,128)S(1)} %bitcast.33), channel_id=1, source_target_pairs={{0,24},{8,16},{16,8},{24,0},{1,25},{9,17},{17,9},{25,1},{2,26},{10... | collective-permute-start | bytes 49160 | tf_op jit(solution)/shard_map/ppermute | solution.py:261
  81.5 9.3 %collective-permute-start.15 = (f32[32,128]{1,0:T(8,128)S(1)}, f32[32,128]{1,0:T(8,128)S(1)}, u32[]{:S(2)}, u32[]{:S(2)}) collective-permute-start(f32[32,128]{1,0:T(8,128)S(1)} %bitcast.34), channel_id=1, source_target_pairs={{0,16},{8,24},{16,0},{24,8},{1,17},{9,25},{17,1},{25,9},{2,18},{10... | collective-permute-start | bytes 49160 | tf_op jit(solution)/shard_map/ppermute | solution.py:261
  83.0 7.8 %copy-start.18 = (bf16[8,128,128]{2,1,0:T(8,128)(2,1)}, bf16[8,128,128]{2,1,0:T(8,128)(2,1)S(1)}, u32[]{:S(2)}) copy-start(bf16[8,128,128]{2,1,0:T(8,128)(2,1)S(1)} %collective-permute-done.7) | copy-start | bytes 786436
  83.0 7.8 %collective-permute-start.14 = (f32[32,128]{1,0:T(8,128)S(1)}, f32[32,128]{1,0:T(8,128)S(1)}, u32[]{:S(2)}, u32[]{:S(2)}) collective-permute-start(f32[32,128]{1,0:T(8,128)S(1)} %bitcast.35), channel_id=1, source_target_pairs={{0,8},{8,0},{16,24},{24,16},{1,9},{9,1},{17,25},{25,17},{2,10},{10... | collective-permute-start | bytes 49160 | tf_op jit(solution)/shard_map/ppermute | solution.py:261
  84.6 8.8 %copy-start.19 = (bf16[8,128,128]{2,1,0:T(8,128)(2,1)}, bf16[8,128,128]{2,1,0:T(8,128)(2,1)S(1)}, u32[]{:S(2)}) copy-start(bf16[8,128,128]{2,1,0:T(8,128)(2,1)S(1)} %collective-permute-done.8) | copy-start | bytes 786436
  88.5 5.3 %copy-start.20 = (bf16[8,128,128]{2,1,0:T(8,128)(2,1)}, bf16[8,128,128]{2,1,0:T(8,128)(2,1)S(1)}, u32[]{:S(2)}) copy-start(bf16[8,128,128]{2,1,0:T(8,128)(2,1)S(1)} %collective-permute-done.9) | copy-start | bytes 786436
  89.3 15.9 %collective-permute-start.10 = (bf16[8,128,128]{2,1,0:T(8,128)(2,1)}, bf16[8,128,128]{2,1,0:T(8,128)(2,1)}, u32[]{:S(2)}, u32[]{:S(2)}) collective-permute-start(bf16[8,128,128]{2,1,0:T(8,128)(2,1)} %fusion.25), channel_id=1, source_target_pairs={{4,0},{5,1},{6,2},{7,3},{12,8},{13,9},{14,10},{15,11},{20,16},{21,... | collective-permute-start | bytes 786440 | tf_op jit(solution)/shard_map/ppermute | solution.py:276
  90.8 4.7 %collective-permute-start.19 = (f32[32,128]{1,0:T(8,128)S(1)}, f32[32,128]{1,0:T(8,128)S(1)}, u32[]{:S(2)}, u32[]{:S(2)}) collective-permute-start(f32[32,128]{1,0:T(8,128)S(1)} %add_add_fusion.1), channel_id=1, source_target_pairs={{0,3},{1,2},{2,1},{3,0},{4,7},{5,6},{6,5},{7,4},{8,11},{9,10},{10,... | collective-permute-start | bytes 49160 | tf_op jit(solution)/shard_map/ppermute | solution.py:261
  93.5 3.8 %collective-permute-start.18 = (f32[32,128]{1,0:T(8,128)S(1)}, f32[32,128]{1,0:T(8,128)S(1)}, u32[]{:S(2)}, u32[]{:S(2)}) collective-permute-start(f32[32,128]{1,0:T(8,128)S(1)} %add_add_fusion.1), channel_id=1, source_target_pairs={{0,2},{1,3},{2,0},{3,1},{4,6},{5,7},{6,4},{7,5},{8,10},{9,11},{10,... | collective-permute-start | bytes 49160 | tf_op jit(solution)/shard_map/ppermute | solution.py:261
  93.8 3.7 %collective-permute-start.17 = (f32[32,128]{1,0:T(8,128)S(1)}, f32[32,128]{1,0:T(8,128)S(1)}, u32[]{:S(2)}, u32[]{:S(2)}) collective-permute-start(f32[32,128]{1,0:T(8,128)S(1)} %add_add_fusion.1), channel_id=1, source_target_pairs={{0,1},{1,0},{2,3},{3,2},{4,5},{5,4},{6,7},{7,6},{8,9},{9,8},{10,11... | collective-permute-start | bytes 49160 | tf_op jit(solution)/shard_map/ppermute | solution.py:261
  97.5 42.6 %collective-permute-start.20 = (f32[32,128]{1,0:T(8,128)S(1)}, f32[32,128]{1,0:T(8,128)S(1)}, u32[]{:S(2)}, u32[]{:S(2)}) collective-permute-start(f32[32,128]{1,0:T(8,128)S(1)} %add_add_fusion), channel_id=1, source_target_pairs={{0,4},{1,5},{2,6},{3,7},{4,0},{5,1},{6,2},{7,3},{8,12},{9,13},{10,... | collective-permute-start | bytes 49160 | tf_op jit(solution)/shard_map/ppermute | solution.py:261
  107.0 33.7 %collective-permute-start.13 = (bf16[8,128,128]{2,1,0:T(8,128)(2,1)S(1)}, bf16[8,128,128]{2,1,0:T(8,128)(2,1)S(1)}, u32[]{:S(2)}, u32[]{:S(2)}) collective-permute-start(bf16[8,128,128]{2,1,0:T(8,128)(2,1)S(1)} %get-tuple-element.45), channel_id=1, source_target_pairs={{0,3},{1,2},{2,1},{3,0},{4,7},{5,6},{6,5},{7,4},{8,11},{9,10},{10,... | collective-permute-start | bytes 786440 | tf_op jit(solution)/shard_map/ppermute | solution.py:261
  107.1 33.6 %collective-permute-start.11 = (bf16[8,128,128]{2,1,0:T(8,128)(2,1)S(1)}, bf16[8,128,128]{2,1,0:T(8,128)(2,1)S(1)}, u32[]{:S(2)}, u32[]{:S(2)}) collective-permute-start(bf16[8,128,128]{2,1,0:T(8,128)(2,1)S(1)} %get-tuple-element.46), channel_id=1, source_target_pairs={{0,1},{1,0},{2,3},{3,2},{4,5},{5,4},{6,7},{7,6},{8,9},{9,8},{10,11... | collective-permute-start | bytes 786440 | tf_op jit(solution)/shard_map/ppermute | solution.py:261
  108.5 32.2 %collective-permute-start.12 = (bf16[8,128,128]{2,1,0:T(8,128)(2,1)S(1)}, bf16[8,128,128]{2,1,0:T(8,128)(2,1)S(1)}, u32[]{:S(2)}, u32[]{:S(2)}) collective-permute-start(bf16[8,128,128]{2,1,0:T(8,128)(2,1)S(1)} %get-tuple-element.48), channel_id=1, source_target_pairs={{0,2},{1,3},{2,0},{3,1},{4,6},{5,7},{6,4},{7,5},{8,10},{9,11},{10,... | collective-permute-start | bytes 786440 | tf_op jit(solution)/shard_map/ppermute | solution.py:261
  110.6 1.7 %copy-start.4 = (bf16[1,320,4096]{2,1,0:T(8,128)(2,1)S(1)}, bf16[1,320,4096]{2,1,0:T(8,128)(2,1)}, u32[]{:S(2)}) copy-start(bf16[1,320,4096]{2,1,0:T(8,128)(2,1)} %param.7) | copy-start | bytes 7864324
  112.3 1.7 %copy-start.6 = (bf16[1,320,4096]{2,1,0:T(8,128)(2,1)S(1)}, bf16[1,320,4096]{2,1,0:T(8,128)(2,1)}, u32[]{:S(2)}) copy-start(bf16[1,320,4096]{2,1,0:T(8,128)(2,1)} %param.5) | copy-start | bytes 7864324
  114.0 0.9 copy-start.12
  115.0 0.9 copy-start.14
  115.9 1.7 %copy-start.17 = (bf16[320,4096]{1,0:T(8,128)(2,1)S(1)}, bf16[320,4096]{1,0:T(8,128)(2,1)}, u32[]{:S(2)}) copy-start(bf16[320,4096]{1,0:T(8,128)(2,1)} %copy-done.16) | copy-start | bytes 7864324
  140.7 2.5 %copy-start.10 = (f32[320,4096]{1,0:T(8,128)S(1)}, f32[320,4096]{1,0:T(8,128)}, u32[]{:S(2)}) copy-start(f32[320,4096]{1,0:T(8,128)} %get-tuple-element.36.dki_ref) | copy-start | bytes 15728644

commit v2 on v0

v2 whole, which is shorter than its diff:
```python
import functools

import jax
import jax.numpy as jnp
from jax import lax
from jax.experimental import pallas as pl
from jax.experimental.pallas import tpu as pltpu
from jax.sharding import PartitionSpec as P

HD = 128
EPSILON = 1e-06
BF16 = jnp.bfloat16
F32 = jnp.float32
CHUNKS = 2
HINTS = {"mix": 10, "outer_gradients": 10}
VMEM_LIMIT = 14 * 1024 * 1024


def dot(a, b, contract):
    return lax.dot_general(a, b, ((contract[:1], contract[1:]), ((), ())), preferred_element_type=F32)


def divisor(n, choices):
    return next(c for c in choices if n % c == 0)


def lanes(head):
    return slice(head * HD, (head + 1) * HD)


def resident(array):
    return pltpu.with_memory_space_constraint(array, pltpu.VMEM)


def pairs_of(count):
    step = 2 if count % 2 == 0 else 1
    return [range(h, h + step) for h in range(0, count, step)]


def rows_of(head, offset=0):
    return slice(offset + head * HD, offset + (head + 1) * HD)


def span(heads):
    return slice(heads[0] * HD, (heads[-1] + 1) * HD)


def diagonal(blocks):
    if len(blocks) == 1:
        return blocks[0]
    zero = jnp.zeros_like(blocks[0])
    return jnp.concatenate([jnp.concatenate([blocks[0], zero], 1), jnp.concatenate([zero, blocks[1]], 1)], 0)


HBM_WHOLE = pl.BlockSpec(memory_space=pl.ANY)


class Layout:
    def __init__(self, tokens, features, members, chunks):
        self.tokens = tokens
        self.features = features
        self.heads = features // HD
        self.members = members
        self.chunks = chunks
        self.count = self.heads // members // chunks
        self.width = self.count * HD
        self.size = self.count * members * tokens * HD

    def wide(self, chunk, first=0):
        chunks = self.chunks
        return pl.BlockSpec((self.tokens, self.width), lambda k, r: (0, (r[0] ^ (k + first)) * chunks + chunk))

    def columns(self, r, piece, chunk):
        return pl.ds(pl.multiple_of(((r[0] ^ piece) * self.chunks + chunk) * self.width, self.width), self.width)

    def wide_shape(self, kind=BF16):
        return jax.ShapeDtypeStruct((self.tokens, self.features), kind)

    def row_shape(self):
        return jax.ShapeDtypeStruct((1, self.features), F32)

    def kept(self, kind):
        return pltpu.VMEM((self.members, self.tokens, self.width), kind)

    def kept_row(self):
        return pltpu.VMEM((self.members, 1, self.width), F32)

    def narrow(self):
        return pltpu.VMEM((self.tokens, HD), F32)

    def piece(self, extra=0):
        return pltpu.VMEM((self.count * HD + extra, HD), BF16)

    def cut(self):
        return self.tokens // 256 * 256 if self.tokens > 256 and self.tokens % 256 % 16 == 0 else self.tokens

    def weights(self):
        cut, rest = self.cut(), max(self.tokens - self.cut(), 16)
        lead = (self.members, self.count)
        return [pltpu.VMEM((*lead, self.tokens, cut), BF16), pltpu.VMEM((*lead, rest, rest), BF16)]

    def token(self):
        return pltpu.VMEM((8, HD), F32)

    def call(self, name, body, rank, streamed, held, outs, after=(), into=(), macs=0, moved=0, scratch=(), grid=(1,)):
        whole = pl.BlockSpec(memory_space=pltpu.VMEM)
        unread = pl.BlockSpec(memory_space=pl.ANY)
        operands = [pltpu.with_memory_space_constraint(a, pltpu.HBM) for a in streamed]
        operands += [resident(a) for a in [*held, *after]]
        operands += [pltpu.with_memory_space_constraint(a, memory) for a, _, memory in into]
        first = 1 + len(streamed) + len(held) + len(after)
        used = len(streamed) + len(held)
        skipped = len(after) + len(into)

        def kernel(r, *refs):
            body(r, *refs[:used], *refs[used + skipped :])

        return pl.pallas_call(
            kernel,
            name=name,
            grid_spec=pltpu.PrefetchScalarGridSpec(
                num_scalar_prefetch=1,
                grid=grid,
                in_specs=[unread] * len(streamed) + [whole] * len(held) + [unread] * skipped,
                out_specs=[whole if s is None else s for _, s in outs],
                scratch_shapes=list(scratch),
            ),
            out_shape=[s for s, _ in outs],
            input_output_aliases={first + n: at for n, (_, at, _) in enumerate(into)},
            compiler_params=pltpu.CompilerParams(vmem_limit_bytes=VMEM_LIMIT),
            cost_estimate=pl.CostEstimate(
                flops=int(HINTS.get(name, 0) * 1e9) + 1, bytes_accessed=int(HINTS.get(name, 0) * 3.6e6) + 1, transcendentals=0
            ),
        )(rank, *operands)


def for_piece(refs, act):
    for k, ref in enumerate(refs):

        @pl.when(pl.program_id(0) == k)
        def _(ref=ref):
            act(ref)


def block_states(layout, rank, keys, values, chunk):
    members = layout.members

    def body(r, k_hbm, v_hbm, k_out, v_out, *refs):
        outs, sems = refs[:members], refs[members]
        copies = []
        for piece in range(members):
            at = layout.columns(r, piece, chunk)
            copies.append(pltpu.make_async_copy(k_hbm.at[:, at], k_out.at[piece], sems.at[0, piece]))
            copies.append(pltpu.make_async_copy(v_hbm.at[:, at], v_out.at[piece], sems.at[1, piece]))
        for copy in copies:
            copy.start()
        for piece in range(members):
            copies[2 * piece].wait()
            copies[2 * piece + 1].wait()
            states = [dot(k_out[piece, :, lanes(h)], v_out[piece, :, lanes(h)], (0, 0)) for h in range(layout.count)]
            for h, state in enumerate(states):
                outs[piece][lanes(h), :] = state.astype(BF16)

    k, v, *states = layout.call(
        "block_states", body, rank, [keys, values], [],
        [(layout.kept(BF16), None)] * 2 + [(layout.piece(), None)] * members,
        macs=layout.size * HD, moved=4 * layout.size, scratch=[pltpu.SemaphoreType.DMA((2, members))],
    )
    return k, v, states


def masked(product):
    rows = lax.broadcasted_iota(jnp.int32, product.shape, 0)
    columns = lax.broadcasted_iota(jnp.int32, product.shape, 1)
    return jnp.where(rows >= columns, product, 0.0).astype(BF16)


def masked_product(a, b, cut):
    blocks = [masked(dot(a, b[:cut], (1, 1)))]
    if cut < a.shape[0]:
        blocks.append(masked(dot(a[cut:], b[cut:], (1, 1))))
    return blocks


def store_product(out, at, blocks, b, cut, add=None):
    rows, columns = at[1:] if len(at) == 3 else at
    lead = at[:-2]
    full = dot(blocks[0], b[:cut], (1, 0))
    full = full if add is None else full + add
    out[(*lead, slice(0, cut), columns)] = full[:cut].astype(out.dtype)
    if len(blocks) > 1:
        out[(*lead, slice(cut, None), columns)] = (full[cut:] + dot(blocks[1], b[cut:], (1, 0))).astype(out.dtype)


def store_turned(out, at, blocks, b, cut):
    lead, columns = at[:-2], at[-1]
    out[(*lead, slice(0, cut), columns)] = dot(blocks[0], b, (0, 0))
    if len(blocks) > 1:
        out[(*lead, slice(cut, None), columns)] = dot(blocks[1], b[cut:], (0, 0))


def within_block(layout, rank, queries, out_grad, gain, keys, values, chunk, after):
    members = layout.members

    def body(r, q_hbm, g_hbm, gain_ref, k_ref, v_ref, q_out, g_out, gain_out, o_ref, *refs):
        w_refs, sems = refs[:-1], refs[-1]
        q_copies, g_copies = [], []
        for piece in range(members):
            at = layout.columns(r, piece, chunk)
            q_copies.append(pltpu.make_async_copy(q_hbm.at[:, at], q_out.at[piece], sems.at[0, piece]))
            g_copies.append(pltpu.make_async_copy(g_hbm.at[:, at], g_out.at[piece], sems.at[1, piece]))
        for copy in q_copies + g_copies:
            copy.start()
        for piece in range(members):
            gain_out[piece] = gain_ref[:, layout.columns(r, piece, chunk)]
            q_copies[piece].wait()
            weights = []
            for h in range(layout.count):
                weights.append(masked_product(q_out[piece, :, lanes(h)], k_ref[piece, :, lanes(h)], layout.cut()))
            for h in range(layout.count):
                for w_ref, block in zip(w_refs, weights[h]):
                    w_ref[piece, h] = block
                store_product(o_ref, (piece, slice(None), lanes(h)), weights[h], v_ref[piece, :, lanes(h)], layout.cut())
        for copy in g_copies:
            copy.wait()

    return layout.call(
        "within_block", body, rank, [queries, out_grad], [gain, keys, values],
        [(layout.kept(BF16), None)] * 2 + [(layout.kept_row(), None), (layout.kept(F32), None)]
        + [(shape, None) for shape in layout.weights()],
        after=after, macs=2 * layout.size * layout.tokens, moved=4 * layout.size, scratch=[pltpu.SemaphoreType.DMA((2, members))],
    )


def mix(layout, rank, kept, prior, jobs, mixed, sums):
    chunks = sorted({c for c, _ in jobs})
    fields = [kept[c][n] for c in chunks for n in (3, 0, 1, 2)]
    states = [prior[c][k][0] for c, k in jobs]
    old = [(n, mixed[c]) for n, c in enumerate(chunks) if c in mixed]

    def body(r, *refs):
        fields_in, refs = refs[: len(fields)], refs[len(fields) :]
        state_refs, refs = refs[: len(jobs)], refs[len(jobs) :]
        before, (*m_refs, square_ref, cross_ref) = refs[: len(sums)], refs[len(sums) :]
        square = before[0][...] if sums else jnp.zeros(square_ref.shape, F32)
        cross = before[1][...] if sums else jnp.zeros(cross_ref.shape, F32)
        for (c, piece), state in zip(jobs, state_refs, strict=True):
            n, offset = chunks.index(c), prior[c][piece][1]
            o_ref, q_ref, g_ref, gain_ref = fields_in[4 * n : 4 * n + 4]
            products = []
            for heads in pairs_of(layout.count):
                block = diagonal([state[rows_of(h, offset), :] for h in heads])
                both = dot(q_ref[piece, :, span(heads)], block, (1, 0))
                products += [both[:, lanes(m)] for m in range(len(heads))]
            for h in range(layout.count):
                at = (piece, slice(None), lanes(h))
                value = o_ref[at] + products[h]
                m_refs[n][at] = value
                square = square + value * value
                cross = cross + gain_ref[piece, :, lanes(h)] * g_ref[at].astype(F32) * value
        square_ref[...] = square
        cross_ref[...] = cross

    *outs, square, cross = layout.call(
        "mix", body, rank, [], [*fields, *states, *sums],
        [(layout.kept(F32), None)] * len(chunks) + [(layout.narrow(), None)] * 2,
        into=[(a, n, pltpu.VMEM) for n, a in old], macs=layout.size * HD, moved=layout.size,
    )
    return {**mixed, **dict(zip(chunks, outs, strict=True))}, [square, cross]


def norm_factors(layout, rank, square, cross):
    def body(r, square_ref, cross_ref, inv_ref, factor_ref):
        mean = jnp.sum(square_ref[...], -1, keepdims=True) / layout.features
        inv = lax.rsqrt(mean + EPSILON)
        centered = jnp.sum(cross_ref[...], -1, keepdims=True) / layout.features
        inv_ref[...] = jnp.broadcast_to(inv, inv_ref.shape)
        factor_ref[...] = jnp.broadcast_to(inv * inv * inv * centered, factor_ref.shape)

    return layout.call(
        "norm_factors", body, rank, [], [square, cross], [(layout.narrow(), None)] * 2, moved=layout.tokens * HD * 4
    )


def mixed_gradients(layout, rank, mixed, queries, out_grad, gain, inv, factor):
    def body(r, m_ref, q_ref, g_ref, gain_ref, inv_ref, factor_ref, d_ref, *outs):
        piece = pl.program_id(0)

        def act(out):
            for h in range(layout.count):
                at = (piece, slice(None), lanes(h))
                scaled = gain_ref[piece, :, lanes(h)] * g_ref[at].astype(F32)
                grad = (inv_ref[...] * scaled - m_ref[at] * factor_ref[...]).astype(BF16)
                d_ref[at] = grad
                out[lanes(h), :] = dot(q_ref[at], grad, (0, 0)).astype(BF16)

        for_piece(outs, act)

    d_mixed, *states = layout.call(
        "mixed_gradients", body, rank, [], [mixed, queries, out_grad, gain, inv, factor],
        [(layout.kept(BF16), None)] + [(layout.piece(), None)] * layout.members,
        macs=layout.size * HD, moved=layout.size, grid=(layout.members,),
    )
    return d_mixed, states


def normed_output(layout, rank, mixed, out_grad, gain, inv, chunk, into, after):
    members = layout.members

    def body(r, m_ref, g_ref, gain_ref, inv_ref, o_hbm, part_ref, buffer, sems):
        copies = []
        for piece in range(members):
            at = layout.columns(r, piece, chunk)
            for h in range(layout.count):
                here = (piece, slice(None), lanes(h))
                normed = m_ref[here] * inv_ref[...]
                buffer[here] = (normed * gain_ref[piece, :, lanes(h)]).astype(BF16)
                head = ((r[0] ^ piece) * layout.chunks + chunk) * layout.count + h
                part_ref[pl.ds(head, 1), :] = jnp.sum(g_ref[here].astype(F32) * normed, 0, keepdims=True)
            copies.append(pltpu.make_async_copy(buffer.at[piece], o_hbm.at[:, at], sems.at[piece]))
            copies[-1].start()
        for copy in copies:
            copy.wait()

    return layout.call(
        "normed_output", body, rank, [], [mixed, out_grad, gain, inv],
        [(layout.wide_shape(), HBM_WHOLE), (pltpu.VMEM((layout.heads, HD), F32), None)],
        into=[(a, n, m) for n, (a, m) in enumerate(zip(into, (pltpu.HBM, pltpu.VMEM)))], after=after, moved=2 * layout.size,
        scratch=[pltpu.VMEM((members, layout.tokens, layout.width), BF16), pltpu.SemaphoreType.DMA((members,))],
    )


def inner_gradients(layout, rank, weights, queries, keys, values, d_mixed, prior, chunk, part, dq, own, after):
    first, last = part

    def body(r, *refs):
        w_refs, (q_ref, k_ref, v_ref, d_ref, *refs) = refs[: len(weights)], refs[len(weights) :]
        states, (dq_ref, dk_ref, dv_ref, token_ref, state) = refs[: last - first], refs[last - first :]
        piece = pl.program_id(0) + first
        token_ref[...] = jnp.zeros_like(token_ref)

        for n, (ref, (_, offset)) in enumerate(zip(states, prior[first:last], strict=True)):

            @pl.when(pl.program_id(0) == n)
            def _(ref=ref, offset=offset):
                state[...] = ref[offset : offset + layout.count * HD, :]

        d_weights, from_prior = [], []
        for h in range(layout.count):
            at = (piece, slice(None), lanes(h))
            d_weights.append(masked_product(d_ref[at], v_ref[at], layout.cut()))
        for heads in pairs_of(layout.count):
            both = dot(d_ref[piece, :, span(heads)], diagonal([state[lanes(h), :] for h in heads]), (1, 1))
            from_prior += [both[:, lanes(n)] for n in range(len(heads))]
        for h in range(layout.count):
            at = (piece, slice(None), lanes(h))
            kept = [w_ref[piece, h] for w_ref in w_refs][: len(d_weights[h])]
            store_product(dq_ref, at[1:], d_weights[h], k_ref[at], layout.cut(), from_prior[h])
            store_turned(dk_ref, at, d_weights[h], q_ref[at], layout.cut())
            store_turned(dv_ref, at, kept, d_ref[at], layout.cut())

    return layout.call(
        "inner_gradients", body, rank, [], [*weights, queries, keys, values, d_mixed, *[a for a, _ in prior[first:last]]],
        [(layout.wide_shape(), layout.wide(chunk, first)), (layout.kept(F32), None), (layout.kept(F32), None), (layout.token(), None)],
        into=[(a, n, pltpu.HBM) for n, a in enumerate(dq)] + [(a, n + 1, pltpu.VMEM) for n, a in enumerate(own)], after=after,
        macs=layout.size * 4 * layout.tokens * (last - first) // layout.members, moved=layout.size,
        scratch=[pltpu.VMEM((layout.count * HD, HD), BF16)], grid=(last - first,),
    )


def pairwise(terms):
    while len(terms) > 1:
        terms = [a + b for a, b in zip(terms[::2], terms[1::2], strict=True)]
    return terms[0]


def outer_gradients(layout, rank, keys, values, own, later, jobs, into, extra):
    chunks = sorted({c for c, _ in jobs})
    fields = [a for c in chunks for a in (keys[c], values[c], *own[c])]
    states = [later[c][k][0] for c, k in jobs]
    count, heads_all = len(jobs), layout.heads
    gain_out = [(jax.ShapeDtypeStruct((heads_all, HD), F32), HBM_WHOLE)] if extra else []

    def body(r, *refs):
        fields_in, refs = refs[: len(fields)], refs[len(fields) :]
        state_refs, (dk_hbm, dv_hbm, *refs) = refs[:count], refs[count:]
        gain_hbm, (dk_buffer, dv_buffer, gain_buffer, sems) = refs[: len(gain_out)], refs[len(gain_out) :]
        copies = []
        if extra:
            parts = []
            for _, n in sorted((piece, n) for n, (c, piece) in enumerate(jobs) if c == chunks[-1]):
                rows = state_refs[n][-2 * heads_all :, :].astype(F32)
                parts.append(rows[:heads_all] + rows[heads_all:])
            gain_buffer[...] = pairwise(parts)
            copies.append(pltpu.make_async_copy(gain_buffer, gain_hbm[0], sems.at[2, 0]))
            copies[-1].start()
        for n, ((c, piece), state) in enumerate(zip(jobs, state_refs, strict=True)):
            at, offset = layout.columns(r, piece, c), later[c][piece][1]
            k_ref, v_ref, dki_ref, dvi_ref = fields_in[4 * chunks.index(c) : 4 * chunks.index(c) + 4]
            sums = []
            for heads in pairs_of(layout.count):
                here = (piece, slice(None), span(heads))
                block = diagonal([state[rows_of(h, offset), :] for h in heads])
                sums.append((heads, here, dot(v_ref[here], block, (1, 1)), dot(k_ref[here], block, (1, 0))))
            for heads, here, dk, dv in sums:
                dk_buffer[n, :, span(heads)] = (dki_ref[here] + dk).astype(BF16)
                dv_buffer[n, :, span(heads)] = (dvi_ref[here] + dv).astype(BF16)
            copies.append(pltpu.make_async_copy(dk_buffer.at[n], dk_hbm.at[:, at], sems.at[0, n]))
            copies.append(pltpu.make_async_copy(dv_buffer.at[n], dv_hbm.at[:, at], sems.at[1, n]))
            copies[-2].start()
            copies[-1].start()
        for copy in copies:
            copy.wait()

    return layout.call(
        "outer_gradients", body, rank, [], [*fields, *states],
        [(layout.wide_shape(), HBM_WHOLE)] * 2 + gain_out,
        into=[(a, n, pltpu.HBM) for n, a in enumerate(into)],
        macs=2 * layout.size * HD, moved=4 * layout.size,
        scratch=[pltpu.VMEM((count, layout.tokens, layout.width), BF16)] * 2
        + [pltpu.VMEM((heads_all, HD), F32), pltpu.SemaphoreType.DMA((3, count))],
    )


def swap(array, axis, size, k):
    return lax.ppermute(array, axis, [(c, c ^ k) for c in range(size)])


def gather_home(pieces, context):
    order = range(len(pieces) - 1, 0, -1)
    got = {k: swap(pieces[k], "context", context, k) for k in order}
    return [pieces[0]] + [got[k] for k in range(1, len(pieces))]


def group_total(layout, rank, got, after):
    def body(r, *refs):
        *gots, total = refs
        total[...] = sum(g[...].astype(F32) for g in gots).astype(BF16)

    return layout.call(
        "group_total", body, rank, [], got, [(layout.piece(), None)], after=after, moved=layout.count * HD * HD * 10
    )[0]


def cross_groups(total, members, context, forward):
    bases = []
    for far in range(1, context // members):
        hop = far * members
        up = [(c, c + hop) for c in range(context - hop)]
        bases.append(lax.ppermute(total, "context", up if forward else [(b, a) for a, b in up]))
    return bases


def spread(layout, rank, got, bases, forward, after, joined=(), gain=()):
    members, heads_all = layout.members, layout.heads
    extra = 2 * heads_all * len(gain)
    shift = layout.count * HD * len(joined)

    def body(r, *refs):
        gots, rest = refs[:members], refs[members:]
        lows, rest = rest[: len(bases)], rest[len(bases) :]
        joined_refs, rest = rest[: len(joined)], rest[len(joined) :]
        gains, outs = rest[: len(gain)], rest[len(gain) :]
        for n, ref in enumerate(joined_refs):
            outs[-1][n * layout.count * HD : (n + 1) * layout.count * HD, :] = ref[...]
        for h in range(layout.count):
            held = [g[rows_of(h), :].astype(F32) for g in gots]
            base = sum((low[rows_of(h), :].astype(F32) for low in lows), jnp.zeros((HD, HD), F32))
            for k in range(members):
                part = base
                for j in range(members):
                    if j != k:
                        one, other = r[0] ^ j, r[0] ^ k
                        ahead = one < other if forward else one > other
                        part = part + held[j] * ahead.astype(F32)
                outs[k][rows_of(h, shift if k == members - 1 else 0), :] = part.astype(BF16)
        for ref in gains:
            high = ref[...].astype(BF16)
            low = (ref[...] - high.astype(F32)).astype(BF16)
            for out in outs:
                rows = out.shape[0]
                out[rows - 2 * heads_all : rows - heads_all, :] = high
                out[rows - heads_all : rows, :] = low

    return layout.call(
        "spread", body, rank, [], [*got, *bases, *joined, *gain],
        [(layout.piece(extra), None)] * (members - 1) + [(layout.piece(extra + shift), None)], after=after,
        moved=layout.count * HD * HD * 18,
    )


def scatter_back(layout, rank, got, bases, context, forward, mark, between, gain=None):
    far, joined, pieces = layout.members - 1, [], []
    for c in range(layout.chunks):
        final = c == layout.chunks - 1
        mark = between(c, mark)
        rows = [gain()] if final and gain else []
        outs = spread(layout, rank, got[c], bases[c], forward, mark, joined if final else [], rows)
        mark = [outs[0]]
        joined.append(outs[far])
        order = range(far if final else far - 1, 0, -1)
        moved = {k: swap(outs[k], "context", context, k) for k in order}
        pieces.append([(moved.get(k, outs[k]), 0) for k in range(layout.members)])
    if far:
        last = pieces[-1][far][0]
        for c, chunk in enumerate(pieces):
            chunk[far] = (last, c * layout.count * HD)
    return pieces, mark


def xor_steps(axis, size, stride):
    steps = []
    while stride < size:
        steps.append((axis, size, stride))
        stride *= 2
    return steps


def added(layout, rank, one, other, after):
    def body(r, one_ref, other_ref, out_ref):
        out_ref[...] = one_ref[...] + other_ref[...]

    return layout.call(
        "gain_sum", body, rank, [], [one, other], [(pltpu.VMEM(one.shape, F32), None)], after=after, moved=one.size * 12
    )[0]


def shards(dp, context, queries, keys, values, gain, out_grad):
    tokens, features = queries.shape[1:]
    members = divisor(context, (4, 2, 1))
    layout = Layout(tokens, features, members, CHUNKS)
    chunks = range(CHUNKS)
    place = (lax.axis_index("context") % members).astype(jnp.int32).reshape(1)
    q, k, v, g = (array[0] for array in (queries, keys, values, out_grad))
    gain_row = gain.reshape(1, features)

    k_kept, v_kept, got = [], [], []
    for c in chunks:
        k_c, v_c, states = block_states(layout, place, k, v, c)
        k_kept.append(k_c)
        v_kept.append(v_c)
        got.append(gather_home(states, context))
    inner, bases, mark = [], [], []
    for c in chunks:
        total = group_total(layout, place, got[c], mark)
        bases.append(cross_groups(total, members, context, True))
        inner.append(within_block(layout, place, q, g, gain_row, k_kept[c], v_kept[c], c, [total]))
        mark = [inner[c][3]]
    prior, mark = scatter_back(layout, place, got, bases, context, True, mark, lambda c, mark: mark)
    far = members - 1
    early = [(c, k) for c in chunks[:-1] for k in range(far)]
    middle = [(CHUNKS - 1, k) for k in range(far)]
    late = [(c, far) for c in chunks]
    mixed, sums = {}, []
    for group in (early, middle, late):
        if group:
            mixed, sums = mix(layout, place, inner, prior, group, mixed, sums)
    inv, factor = norm_factors(layout, place, *sums)

    d_mixed, got = [], []
    for c in chunks:
        q_c, g_c, gain_c = inner[c][:3]
        d_c, states = mixed_gradients(layout, place, mixed[c], q_c, g_c, gain_c, inv, factor)
        d_mixed.append(d_c)
        got.append(gather_home(states, context))

    out, dq, own, gain_grad = [], [], [[] for _ in chunks], None
    regular = dp & (dp - 1) == 0 and context & (context - 1) == 0
    steps = xor_steps("dp", dp, 1) + xor_steps("context", context, members) if regular else []

    def inner_job(mark, c, part):
        nonlocal dq
        *dq, dk_c, dv_c, token = inner_gradients(
            layout, place, inner[c][4:], inner[c][0], k_kept[c], v_kept[c], d_mixed[c], prior[c], c, part, dq, own[c], mark
        )
        own[c] = [dk_c, dv_c]
        return [token]

    def gain_job(mark):
        nonlocal gain_grad
        if not steps:
            return mark
        axis, size, stride = steps.pop(0)
        gain_grad = added(layout, place, gain_grad, swap(gain_grad, axis, size, stride), mark)
        return [gain_grad]

    cuts = sorted({0, members // 4, members // 2, members})
    jobs = [(0, part) for part in zip(cuts[:-1], cuts[1:], strict=True)]
    bases, mark = [], [d_mixed[-1]]
    for c in chunks:
        _, g_c, gain_c = inner[c][:3]
        out = normed_output(layout, place, mixed[c], g_c, gain_c, inv, c, out, mark)
        output, gain_grad = out
        mark = [gain_grad]
        if c == CHUNKS - 1 and CHUNKS > 1:
            mark = inner_job(mark, *jobs.pop(0))
            mark = gain_job(mark)
        total = group_total(layout, place, got[c], mark)
        mark = [total]
        bases.append(cross_groups(total, members, context, False))

    def between(c, mark):
        if jobs:
            mark = inner_job(mark, *jobs.pop(0))
        mark = gain_job(mark)
        while c == CHUNKS - 1 and (jobs or steps):
            mark = inner_job(mark, *jobs.pop(0)) if jobs else mark
            mark = gain_job(mark)
        return mark

    gain = (lambda: gain_grad) if regular else None
    later, mark = scatter_back(layout, place, got, bases, context, False, mark, between, gain)
    for c in chunks[1:]:
        mark = inner_job(mark, c, (0, members))
    outer = []
    for group in (early, middle + late):
        if group:
            extra = regular and group != early
            *outer, total_gain = [*outer_gradients(layout, place, k_kept, v_kept, own, later, group, outer, extra), None][:3]
    if not regular:
        total_gain = lax.psum(gain_grad, ("dp", "context"))
    return output[None], dq[0][None], outer[0][None], outer[1][None], total_gain.reshape(features)


def solution(mesh):
    sharded = P("dp", "context", None)
    return jax.shard_map(
        functools.partial(shards, mesh.shape["dp"], mesh.shape["context"]),
        mesh=mesh,
        in_specs=(sharded, sharded, sharded, P(), sharded),
        out_specs=(sharded, sharded, sharded, sharded, P()),
        check_vma=False,
    )
```

time: 353 us -> 87.9 us (0.25); the launches traced: 349 us -> 87.6 us
  waiting for transfers between devices: 136 us -> 6.34 us
  matrix products: 78.6 us -> 0 us
  blocking collectives: 53.4 us -> 0 us
  local copies, waits for them, and re-layouts: 51.1 us -> 0.01 us
  starting transfers between devices: 0.29 us -> 43.3 us
  Pallas kernels: 0 us -> 36.9 us
  other arithmetic: 14 us -> 0 us
  between operations: 14.8 us -> 1.1 us
    all_gather x2 -> x0, waiting for transfers between devices: 136 us -> none  [the longest x1 103 us: carried_in(): gathered = lax.all_gather(array.astype(jnp.bfloat16), axis)]
    dot_general x13 -> x0, matrix products: 78.6 us -> none  [the longest x1 10.3 us: masked_fold(): return jnp.tensordot(keep, shard_piece.astype(jnp.float32), axes=1)]
    psum x1 -> x0, blocking collectives: 53.4 us -> none  [shards(): gain_grad = lax.psum(gain_part, ('dp', 'context'))]
    ppermute x0 -> x29, starting transfers between devices: none -> 43.3 us  [the longest x25 33.5 us: swap(): return lax.ppermute(array, axis, [(c, c ^ k) for c in range(size)])]
    pallas_call x0 -> x29, Pallas kernels: none -> 36.9 us  [call(): pl.pallas_call(kernel, name=name, grid_spec=pltpu.PrefetchScalarGridSpec(...]
    convert_element_type x7 -> x0, local copies, waits for them, and re-layouts: 21.1 us -> none  [the longest x2 10.2 us: shards(): value_grad.reshape(flat).astype(jnp.bfloat16)]
    unnamed x42 -> x2, local copies, waits for them, and re-layouts: 15 us -> 0.01 us
    convert_element_type x2 -> x0, other arithmetic: 8.93 us -> none  [the longest x1 4.8 us: shards(): output = (normed * gain).astype(jnp.bfloat16)]
  transfers between devices with their start and end apart: 2 -> 29, of which waited for: 2 -> 7; matrix products, arithmetic and copies ran while one was open for 20% -> 0% of each run, Pallas kernels for 0% -> 35%
where the time goes in v2:
time: 87.9 us; the launch traced here: 87.6 us
  starting transfers between devices  43.3 us (49%)
  Pallas kernels  36.9 us (42%)
  waiting for transfers between devices  6.34 us (7%)
  between operations  1.1 us (1%)
    pallas_call x29, Pallas kernels, call(): pl.pallas_call(kernel, name=name, grid_spec=pltpu.PrefetchScalarGridSpec(...  36.9 us
    ppermute x25, starting transfers between devices, swap(): return lax.ppermute(array, axis, [(c, c ^ k) for c in range(size)])  33.5 us
    ppermute x4, starting transfers between devices, cross_groups(): lax.ppermute(total, 'context', up if forward else [(b, a) for a, b in up])  9.79 us
    ppermute x25, waiting for transfers between devices, swap(): return lax.ppermute(array, axis, [(c, c ^ k) for c in range(size)])  6.33 us
  transfers between devices with their start and end apart: 29, of which 7 were waited for; matrix products, arithmetic and copies ran while one was open for 0% of the time, Pallas kernels for 35%

profile of v2, /device:TPU:0, one launch (start us, length us, event | category | flops | bytes accessed | tf_op | source)
XLA Modules:
  0.0 87.6 jit_solution(6679566724093306466)
XLA Ops:
  0.6 2.4 %block_states.2 = (bf16[4,320,512]{2,1,0:T(8,128)(2,1)S(1)}, bf16[4,320,512]{2,1,0:T(8,128)(2,1)S(1)}, bf16[512,128]{1,0:T(8,128)(2,1)S(1)}, bf16[512,128]{1,0:T...) custom-call(s32[1]{0:T(128)} %bitcast.r, bf16[320,4096]{1,0:T(8,128)(2,1)} %bitcast.18, ...), custom_call_target="tpu_custom_call" | custom-call | flops 1 | bytes 1 | tf_op jit(solution)/shard_map/block_states/pallas_call | solution.py:118
  3.0 3.0 %collective-permute-start = (bf16[512,128]{1,0:T(8,128)(2,1)S(1)}, bf16[512,128]{1,0:T(8,128)(2,1)S(1)}, u32[]{:S(2)}, u32[]{:S(2)}) collective-permute-start(bf16[512,128]{1,0:T(8,128)(2,1)S(1)} %get-tuple-element.94), channel_id=1, source_target_pairs={{0,1},{1,0},{2,3},{3,2},{4,5},{5,4},{6,7},{7,6},{8,9},{9,8},{10,11... | collective-permute-start | bytes 393224 | tf_op jit(solution)/shard_map/ppermute | solution.py:426
  6.0 1.6 %collective-permute-start.1 = (bf16[512,128]{1,0:T(8,128)(2,1)S(1)}, bf16[512,128]{1,0:T(8,128)(2,1)S(1)}, u32[]{:S(2)}, u32[]{:S(2)}) collective-permute-start(bf16[512,128]{1,0:T(8,128)(2,1)S(1)} %get-tuple-element.95), channel_id=1, source_target_pairs={{0,2},{1,3},{2,0},{3,1},{4,6},{5,7},{6,4},{7,5},{8,10},{9,11},{10,... | collective-permute-start | bytes 393224 | tf_op jit(solution)/shard_map/ppermute | solution.py:426
  7.6 2.4 %block_states.3 = (bf16[4,320,512]{2,1,0:T(8,128)(2,1)S(1)}, bf16[4,320,512]{2,1,0:T(8,128)(2,1)S(1)}, bf16[512,128]{1,0:T(8,128)(2,1)S(1)}, bf16[512,128]{1,0:T...) custom-call(s32[1]{0:T(128)} %bitcast.r, bf16[320,4096]{1,0:T(8,128)(2,1)} %bitcast.19, ...), custom_call_target="tpu_custom_call" | custom-call | flops 1 | bytes 1 | tf_op jit(solution)/shard_map/block_states/pallas_call | solution.py:118
  10.0 1.9 %collective-permute-start.3 = (bf16[512,128]{1,0:T(8,128)(2,1)S(1)}, bf16[512,128]{1,0:T(8,128)(2,1)S(1)}, u32[]{:S(2)}, u32[]{:S(2)}) collective-permute-start(bf16[512,128]{1,0:T(8,128)(2,1)S(1)} %get-tuple-element.104), channel_id=1, source_target_pairs={{0,1},{1,0},{2,3},{3,2},{4,5},{5,4},{6,7},{7,6},{8,9},{9,8},{10,11... | collective-permute-start | bytes 393224 | tf_op jit(solution)/shard_map/ppermute | solution.py:426
  12.0 1.6 %collective-permute-start.4 = (bf16[512,128]{1,0:T(8,128)(2,1)S(1)}, bf16[512,128]{1,0:T(8,128)(2,1)S(1)}, u32[]{:S(2)}, u32[]{:S(2)}) collective-permute-start(bf16[512,128]{1,0:T(8,128)(2,1)S(1)} %get-tuple-element.105), channel_id=1, source_target_pairs={{0,2},{1,3},{2,0},{3,1},{4,6},{5,7},{6,4},{7,5},{8,10},{9,11},{10,... | collective-permute-start | bytes 393224 | tf_op jit(solution)/shard_map/ppermute | solution.py:426
  13.6 0.5 collective-permute-done.2.refs_3_
  14.2 4.7 %collective-permute-start.7 = (bf16[512,128]{1,0:T(8,128)(2,1)S(1)}, bf16[512,128]{1,0:T(8,128)(2,1)S(1)}, u32[]{:S(2)}, u32[]{:S(2)}) collective-permute-start(bf16[512,128]{1,0:T(8,128)(2,1)S(1)} %group_total.4.refs_5_), channel_id=1, source_target_pairs={{0,4},{1,5},{2,6},{3,7},{8,12},{9,13},{10,14},{11,15},{16,20},{17,... | collective-permute-start | bytes 393224 | tf_op jit(solution)/shard_map/ppermute | solution.py:450
  18.9 3.5 %within_block.2 = (bf16[4,320,512]{2,1,0:T(8,128)(2,1)S(1)}, bf16[4,320,512]{2,1,0:T(8,128)(2,1)S(1)}, f32[4,1,512]{2,1,0:T(1,128)S(1)}, f32[4,320,512]{2,1,0:T(...) custom-call(s32[1]{0:T(128)} %bitcast.r, bf16[320,4096]{1,0:T(8,128)(2,1)} %bitcast.14, ...), custom_call_target="tpu_custom_call" | custom-call | flops 1 | bytes 1 | tf_op jit(solution)/shard_map/within_block/pallas_call | solution.py:118
  22.5 2.3 %collective-permute-start.6 = (bf16[512,128]{1,0:T(8,128)(2,1)S(1)}, bf16[512,128]{1,0:T(8,128)(2,1)S(1)}, u32[]{:S(2)}, u32[]{:S(2)}) collective-permute-start(bf16[512,128]{1,0:T(8,128)(2,1)S(1)} %group_total.5.refs_5_), channel_id=1, source_target_pairs={{0,4},{1,5},{2,6},{3,7},{8,12},{9,13},{10,14},{11,15},{16,20},{17,... | collective-permute-start | bytes 393224 | tf_op jit(solution)/shard_map/ppermute | solution.py:450
  24.8 3.5 %within_block.3 = (bf16[4,320,512]{2,1,0:T(8,128)(2,1)S(1)}, bf16[4,320,512]{2,1,0:T(8,128)(2,1)S(1)}, f32[4,1,512]{2,1,0:T(1,128)S(1)}, f32[4,320,512]{2,1,0:T(...) custom-call(s32[1]{0:T(128)} %bitcast.r, bf16[320,4096]{1,0:T(8,128)(2,1)} %bitcast.15, ...), custom_call_target="tpu_custom_call" | custom-call | flops 1 | bytes 1 | tf_op jit(solution)/shard_map/within_block/pallas_call | solution.py:118
  28.6 1.0 %collective-permute-start.11 = (bf16[512,128]{1,0:T(8,128)(2,1)S(1)}, bf16[512,128]{1,0:T(8,128)(2,1)S(1)}, u32[]{:S(2)}, u32[]{:S(2)}) collective-permute-start(bf16[512,128]{1,0:T(8,128)(2,1)S(1)} %get-tuple-element.117), channel_id=1, source_target_pairs={{0,1},{1,0},{2,3},{3,2},{4,5},{5,4},{6,7},{7,6},{8,9},{9,8},{10,11... | collective-permute-start | bytes 393224 | tf_op jit(solution)/shard_map/ppermute | solution.py:426
  29.5 3.0 %collective-permute-start.12 = (bf16[512,128]{1,0:T(8,128)(2,1)S(1)}, bf16[512,128]{1,0:T(8,128)(2,1)S(1)}, u32[]{:S(2)}, u32[]{:S(2)}) collective-permute-start(bf16[512,128]{1,0:T(8,128)(2,1)S(1)} %get-tuple-element.118), channel_id=1, source_target_pairs={{0,2},{1,3},{2,0},{3,1},{4,6},{5,7},{6,4},{7,5},{8,10},{9,11},{10,... | collective-permute-start | bytes 393224 | tf_op jit(solution)/shard_map/ppermute | solution.py:426
  33.0 3.3 %collective-permute-start.8 = (bf16[1024,128]{1,0:T(8,128)(2,1)S(1)}, bf16[1024,128]{1,0:T(8,128)(2,1)S(1)}, u32[]{:S(2)}, u32[]{:S(2)}) collective-permute-start(bf16[1024,128]{1,0:T(8,128)(2,1)S(1)} %get-tuple-element.113), channel_id=1, source_target_pairs={{0,3},{1,2},{2,1},{3,0},{4,7},{5,6},{6,5},{7,4},{8,11},{9,10},{10,... | collective-permute-start | bytes 786440 | tf_op jit(solution)/shard_map/ppermute | solution.py:426
  36.4 0.5 collective-permute-done.12.refs_6_
  36.9 0.6 mix.3
  37.5 0.8 collective-permute-done.10.refs_6_.refs_8_
  38.3 0.9 %collective-permute-done.9.refs_5_.refs_7_ = bf16[512,128]{1,0:T(8,128)(2,1)S(1)} collective-permute-done((bf16[512,128]{1,0:T(8,128)(2,1)S(1)}, bf16[512,128]{1,0:T(8,128)(2,1)S(1)}, u32[]{:S(2)}, u32[]{:S(2)}) %collective-permute-start.9) | collective-permute-done | bytes 131104 | tf_op jit(solution)/shard_map/ppermute | solution.py:426
  39.2 0.7 mix.4
  39.9 1.9 %collective-permute-done.8.refs_8_.refs_9_.refs_7_ = bf16[1024,128]{1,0:T(8,128)(2,1)S(1)} collective-permute-done((bf16[1024,128]{1,0:T(8,128)(2,1)S(1)}, bf16[1024,128]{1,0:T(8,128)(2,1)S(1)}, u32[]{:S(2)}, u32[]{:S(2)}) %collective-permute-start.8) | collective-permute-done | bytes 262176 | tf_op jit(solution)/shard_map/ppermute | solution.py:426
  41.8 0.5 mix.5
  42.5 1.4 %mixed_gradients.2 = (bf16[4,320,512]{2,1,0:T(8,128)(2,1)S(1)}, bf16[512,128]{1,0:T(8,128)(2,1)S(1)}, bf16[512,128]{1,0:T(8,128)(2,1)S(1)}, bf16[512,128]{1,0:T(8,128)(2,1)S(1)}, bf16[512,128]{1,0:T(8,128)(2,1)S(1)}) custom-call(s32[1]{0:T(128)} %bitcast.r, f32[4,320,512]{2,1,0:T(8,128)S(1)} %get-tuple-element.129.refs_0_, ...), custom_call_target="tpu_custom_call" | custom-call | flops 1 | bytes 1 | tf_op jit(solution)/shard_map/mixed_gradients/pallas_call | solution.py:118
  43.9 0.8 collective-permute-start.13
  44.7 1.6 %collective-permute-start.14 = (bf16[512,128]{1,0:T(8,128)(2,1)S(1)}, bf16[512,128]{1,0:T(8,128)(2,1)S(1)}, u32[]{:S(2)}, u32[]{:S(2)}) collective-permute-start(bf16[512,128]{1,0:T(8,128)(2,1)S(1)} %get-tuple-element.133), channel_id=1, source_target_pairs={{0,2},{1,3},{2,0},{3,1},{4,6},{5,7},{6,4},{7,5},{8,10},{9,11},{10,... | collective-permute-start | bytes 393224 | tf_op jit(solution)/shard_map/ppermute | solution.py:426
  46.4 1.1 %collective-permute-start.15 = (bf16[512,128]{1,0:T(8,128)(2,1)S(1)}, bf16[512,128]{1,0:T(8,128)(2,1)S(1)}, u32[]{:S(2)}, u32[]{:S(2)}) collective-permute-start(bf16[512,128]{1,0:T(8,128)(2,1)S(1)} %get-tuple-element.134), channel_id=1, source_target_pairs={{0,3},{1,2},{2,1},{3,0},{4,7},{5,6},{6,5},{7,4},{8,11},{9,10},{10,... | collective-permute-start | bytes 393224 | tf_op jit(solution)/shard_map/ppermute | solution.py:426
  47.4 1.4 %mixed_gradients.3 = (bf16[4,320,512]{2,1,0:T(8,128)(2,1)S(1)}, bf16[512,128]{1,0:T(8,128)(2,1)S(1)}, bf16[512,128]{1,0:T(8,128)(2,1)S(1)}, bf16[512,128]{1,0:T(8,128)(2,1)S(1)}, bf16[512,128]{1,0:T(8,128)(2,1)S(1)}) custom-call(s32[1]{0:T(128)} %bitcast.r, f32[4,320,512]{2,1,0:T(8,128)S(1)} %get-tuple-element.125.refs_0_, ...), custom_call_target="tpu_custom_call" | custom-call | flops 1 | bytes 1 | tf_op jit(solution)/shard_map/mixed_gradients/pallas_call | solution.py:118
  48.8 0.8 collective-permute-start.16
  49.7 1.6 %collective-permute-start.17 = (bf16[512,128]{1,0:T(8,128)(2,1)S(1)}, bf16[512,128]{1,0:T(8,128)(2,1)S(1)}, u32[]{:S(2)}, u32[]{:S(2)}) collective-permute-start(bf16[512,128]{1,0:T(8,128)(2,1)S(1)} %get-tuple-element.143), channel_id=1, source_target_pairs={{0,2},{1,3},{2,0},{3,1},{4,6},{5,7},{6,4},{7,5},{8,10},{9,11},{10,... | collective-permute-start | bytes 393224 | tf_op jit(solution)/shard_map/ppermute | solution.py:426
  51.3 1.1 %collective-permute-start.18 = (bf16[512,128]{1,0:T(8,128)(2,1)S(1)}, bf16[512,128]{1,0:T(8,128)(2,1)S(1)}, u32[]{:S(2)}, u32[]{:S(2)}) collective-permute-start(bf16[512,128]{1,0:T(8,128)(2,1)S(1)} %get-tuple-element.144), channel_id=1, source_target_pairs={{0,3},{1,2},{2,1},{3,0},{4,7},{5,6},{6,5},{7,4},{8,11},{9,10},{10,... | collective-permute-start | bytes 393224 | tf_op jit(solution)/shard_map/ppermute | solution.py:426
  52.4 1.3 %normed_output.2 = (bf16[320,4096]{1,0:T(8,128)(2,1)}, f32[32,128]{1,0:T(8,128)S(1)}) custom-call(s32[1]{0:T(128)} %bitcast.r, f32[4,320,512]{2,1,0:T(8,128)S(1)} %get-tuple-element.129.refs_0_, bf16[4,320,512]{2,1,0:T(8,128)(2,1)S(1)} %get-tuple-element.99.refs_2_.refs_1_, f32[4,1,512]{2,1,0:T(1,128)S(1)} %get-tuple-element.100.refs_3_.refs_2_, ...), custom_call_target="tpu_custom_call" | custom-call | flops 1 | bytes 1 | tf_op jit(solution)/shard_map/normed_output/pallas_call | solution.py:118
  53.7 0.5 collective-permute-done.15.refs_3_
  54.3 1.3 %collective-permute-start.21 = (bf16[512,128]{1,0:T(8,128)(2,1)S(1)}, bf16[512,128]{1,0:T(8,128)(2,1)S(1)}, u32[]{:S(2)}, u32[]{:S(2)}) collective-permute-start(bf16[512,128]{1,0:T(8,128)(2,1)S(1)} %group_total.6.refs_4_), channel_id=1, source_target_pairs={{4,0},{5,1},{6,2},{7,3},{12,8},{13,9},{14,10},{15,11},{20,16},{21,... | collective-permute-start | bytes 393224 | tf_op jit(solution)/shard_map/ppermute | solution.py:450
  55.6 1.3 %normed_output.3 = (bf16[320,4096]{1,0:T(8,128)(2,1)}, f32[32,128]{1,0:T(8,128)S(1)}) custom-call(s32[1]{0:T(128)} %bitcast.r, f32[4,320,512]{2,1,0:T(8,128)S(1)} %get-tuple-element.125.refs_0_, bf16[4,320,512]{2,1,0:T(8,128)(2,1)S(1)} %get-tuple-element.109.refs_2_.refs_6_.refs_1_, ...), custom_call_target="tpu_custom_call", output_to_operand_aliasing={{0}: (6, {}), {1}: (7, {})} | custom-call | flops 1 | bytes 1 | tf_op jit(solution)/shard_map/normed_output/pallas_call | solution.py:118
  57.0 1.9 %inner_gradients.4 = (bf16[320,4096]{1,0:T(8,128)(2,1)}, f32[4,320,512]{2,1,0:T(8,128)S(1)}, f32[4,320,512]{2,1,0:T(8,128)S(1)}, f32[8,128]{1,0:T(8,128)S(1)}) custom-call(s32[1]{0:T(128)} %bitcast.r, bf16[4,4,320,256]{3,2,1,0:T(8,128)(2,1)S(1)} %get-tuple-element.146.refs_0_, bf16[4,4,64,64]{3,2,1,0:T(8,128)(2,1)S(1)} %get-tuple-element.147.refs_1_, ...), custom_call_target="tpu_custom_call" | custom-call | flops 1 | bytes 1 | tf_op jit(solution)/shard_map/inner_gradients/pallas_call | solution.py:118
  58.9 1.5 %collective-permute-start.22 = (f32[32,128]{1,0:T(8,128)S(1)}, f32[32,128]{1,0:T(8,128)S(1)}, u32[]{:S(2)}, u32[]{:S(2)}) collective-permute-start(f32[32,128]{1,0:T(8,128)S(1)} %gain_sum.3.refs_4_.refs_0_), channel_id=1, source_target_pairs={{0,16},{8,24},{16,0},{24,8},{1,17},{9,25},{17,1},{25,9},{2,18},{10... | collective-permute-start | bytes 49160 | tf_op jit(solution)/shard_map/ppermute | solution.py:426
  60.5 1.5 %collective-permute-start.20 = (bf16[512,128]{1,0:T(8,128)(2,1)S(1)}, bf16[512,128]{1,0:T(8,128)(2,1)S(1)}, u32[]{:S(2)}, u32[]{:S(2)}) collective-permute-start(bf16[512,128]{1,0:T(8,128)(2,1)S(1)} %group_total.7.refs_7_), channel_id=1, source_target_pairs={{4,0},{5,1},{6,2},{7,3},{12,8},{13,9},{14,10},{15,11},{20,16},{21,... | collective-permute-start | bytes 393224 | tf_op jit(solution)/shard_map/ppermute | solution.py:450
  62.0 1.9 %inner_gradients.5 = (bf16[320,4096]{1,0:T(8,128)(2,1)}, f32[4,320,512]{2,1,0:T(8,128)S(1)}, f32[4,320,512]{2,1,0:T(8,128)S(1)}, f32[8,128]{1,0:T(8,128)S(1)}) custom-call(s32[1]{0:T(128)} %bitcast.r, bf16[4,4,320,256]{3,2,1,0:T(8,128)(2,1)S(1)} %get-tuple-element.146.refs_0_, ...), custom_call_target="tpu_custom_call", output_to_operand_aliasing={{0}: (9, {}), {1}: (10, {}), {2}: (11, {})} | custom-call | flops 1 | bytes 1 | tf_op jit(solution)/shard_map/inner_gradients/pallas_call | solution.py:118
  64.2 0.4 collective-permute-start.27
  64.6 1.6 %collective-permute-start.28 = (bf16[512,128]{1,0:T(8,128)(2,1)S(1)}, bf16[512,128]{1,0:T(8,128)(2,1)S(1)}, u32[]{:S(2)}, u32[]{:S(2)}) collective-permute-start(bf16[512,128]{1,0:T(8,128)(2,1)S(1)} %get-tuple-element.171), channel_id=1, source_target_pairs={{0,2},{1,3},{2,0},{3,1},{4,6},{5,7},{6,4},{7,5},{8,10},{9,11},{10,... | collective-permute-start | bytes 393224 | tf_op jit(solution)/shard_map/ppermute | solution.py:426
  66.2 3.5 %collective-permute-start.23 = (f32[32,128]{1,0:T(8,128)S(1)}, f32[32,128]{1,0:T(8,128)S(1)}, u32[]{:S(2)}, u32[]{:S(2)}) collective-permute-start(f32[32,128]{1,0:T(8,128)S(1)} %gain_sum.4.refs_5_.refs_0_), channel_id=1, source_target_pairs={{0,4},{1,5},{2,6},{3,7},{4,0},{5,1},{6,2},{7,3},{8,12},{9,13},{10,... | collective-permute-start | bytes 49160 | tf_op jit(solution)/shard_map/ppermute | solution.py:426
  69.7 3.1 %inner_gradients.6 = (bf16[320,4096]{1,0:T(8,128)(2,1)}, f32[4,320,512]{2,1,0:T(8,128)S(1)}, f32[4,320,512]{2,1,0:T(8,128)S(1)}, f32[8,128]{1,0:T(8,128)S(1)}) custom-call(s32[1]{0:T(128)} %bitcast.r, bf16[4,4,320,256]{3,2,1,0:T(8,128)(2,1)S(1)} %get-tuple-element.146.refs_0_, ...), custom_call_target="tpu_custom_call", output_to_operand_aliasing={{0}: (10, {}), {1}: (11, {}), {2}: (12, {})} | custom-call | flops 1 | bytes 1 | tf_op jit(solution)/shard_map/inner_gradients/pallas_call | solution.py:118
  73.2 2.1 %collective-permute-start.26 = (bf16[1088,128]{1,0:T(8,128)(2,1)S(1)}, bf16[1088,128]{1,0:T(8,128)(2,1)S(1)}, u32[]{:S(2)}, u32[]{:S(2)}) collective-permute-start(bf16[1088,128]{1,0:T(8,128)(2,1)S(1)} %get-tuple-element.169), channel_id=1, source_target_pairs={{0,3},{1,2},{2,1},{3,0},{4,7},{5,6},{6,5},{7,4},{8,11},{9,10},{10,... | collective-permute-start | bytes 835592 | tf_op jit(solution)/shard_map/ppermute | solution.py:426
  75.3 0.6 collective-permute-start.24
  75.9 0.9 collective-permute-start.25
  76.7 5.7 %inner_gradients.7 = (bf16[320,4096]{1,0:T(8,128)(2,1)}, f32[4,320,512]{2,1,0:T(8,128)S(1)}, f32[4,320,512]{2,1,0:T(8,128)S(1)}, f32[8,128]{1,0:T(8,128)}) custom-call(s32[1]{0:T(128)} %bitcast.r, bf16[4,4,320,256]{3,2,1,0:T(8,128)(2,1)S(1)} %get-tuple-element.139.refs_0_, ...), custom_call_target="tpu_custom_call", output_to_operand_aliasing={{0}: (12, {})} | custom-call | flops 1 | bytes 1 | tf_op jit(solution)/shard_map/inner_gradients/pallas_call | solution.py:118
  82.4 1.7 %outer_gradients.2 = (bf16[320,4096]{1,0:T(8,128)(2,1)}, bf16[320,4096]{1,0:T(8,128)(2,1)}) custom-call(s32[1]{0:T(128)} %bitcast.r, bf16[4,320,512]{2,1,0:T(8,128)(2,1)S(1)} %get-tuple-element.91.refs_3_.refs_0_, bf16[4,320,512]{2,1,0:T(8,128)(2,1)S(1)} %get-tuple-element.92.refs_4_.refs_1_, f32[4,320,512]{2,1,0:T(8,128)S(1)} %get-tuple-element.163.refs_2_, ...), custom_call_target="tpu_custom_call" | custom-call | flops 10000000000 | bytes 36000000 | tf_op jit(solution)/shard_map/outer_gradients/pallas_call | solution.py:118
  84.1 1.1 %collective-permute-done.24.refs_9_ = bf16[576,128]{1,0:T(8,128)(2,1)S(1)} collective-permute-done((bf16[576,128]{1,0:T(8,128)(2,1)S(1)}, bf16[576,128]{1,0:T(8,128)(2,1)S(1)}, u32[]{:S(2)}, u32[]{:S(2)}) %collective-permute-start.24) | collective-permute-done | bytes 147488 | tf_op jit(solution)/shard_map/ppermute | solution.py:426
  85.2 2.2 %outer_gradients.3 = (bf16[320,4096]{1,0:T(8,128)(2,1)}, bf16[320,4096]{1,0:T(8,128)(2,1)}, f32[32,128]{1,0:T(8,128)}) custom-call(s32[1]{0:T(128)} %bitcast.r, bf16[4,320,512]{2,1,0:T(8,128)(2,1)S(1)} %get-tuple-element.91.refs_3_.refs_0_, ...), custom_call_target="tpu_custom_call", output_to_operand_aliasing={{0}: (14, {}), {1}: (15, {})} | custom-call | flops 10000000000 | bytes 36000000 | tf_op jit(solution)/shard_map/outer_gradients/pallas_call | solution.py:118
  (41 shorter events, 1.9 us)
Async XLA Ops:
  3.0 10.6 %collective-permute-start = (bf16[512,128]{1,0:T(8,128)(2,1)S(1)}, bf16[512,128]{1,0:T(8,128)(2,1)S(1)}, u32[]{:S(2)}, u32[]{:S(2)}) collective-permute-start(bf16[512,128]{1,0:T(8,128)(2,1)S(1)} %get-tuple-element.94), channel_id=1, source_target_pairs={{0,1},{1,0},{2,3},{3,2},{4,5},{5,4},{6,7},{7,6},{8,9},{9,8},{10,11... | collective-permute-start | bytes 393224 | tf_op jit(solution)/shard_map/ppermute | solution.py:426
  6.0 7.6 %collective-permute-start.1 = (bf16[512,128]{1,0:T(8,128)(2,1)S(1)}, bf16[512,128]{1,0:T(8,128)(2,1)S(1)}, u32[]{:S(2)}, u32[]{:S(2)}) collective-permute-start(bf16[512,128]{1,0:T(8,128)(2,1)S(1)} %get-tuple-element.95), channel_id=1, source_target_pairs={{0,2},{1,3},{2,0},{3,1},{4,6},{5,7},{6,4},{7,5},{8,10},{9,11},{10,... | collective-permute-start | bytes 393224 | tf_op jit(solution)/shard_map/ppermute | solution.py:426
  7.6 11.3 %copy-start = (f32[4096]{0:T(1024)S(1)}, f32[4096]{0:T(1024)}, u32[]{:S(2)}) copy-start(f32[4096]{0:T(1024)} %param.8) | copy-start | bytes 49156
  7.6 6.4 %collective-permute-start.2 = (bf16[512,128]{1,0:T(8,128)(2,1)S(1)}, bf16[512,128]{1,0:T(8,128)(2,1)S(1)}, u32[]{:S(2)}, u32[]{:S(2)}) collective-permute-start(bf16[512,128]{1,0:T(8,128)(2,1)S(1)} %get-tuple-element.96), channel_id=1, source_target_pairs={{0,3},{1,2},{2,1},{3,0},{4,7},{5,6},{6,5},{7,4},{8,11},{9,10},{10,... | collective-permute-start | bytes 393224 | tf_op jit(solution)/shard_map/ppermute | solution.py:426
  10.0 12.4 %collective-permute-start.3 = (bf16[512,128]{1,0:T(8,128)(2,1)S(1)}, bf16[512,128]{1,0:T(8,128)(2,1)S(1)}, u32[]{:S(2)}, u32[]{:S(2)}) collective-permute-start(bf16[512,128]{1,0:T(8,128)(2,1)S(1)} %get-tuple-element.104), channel_id=1, source_target_pairs={{0,1},{1,0},{2,3},{3,2},{4,5},{5,4},{6,7},{7,6},{8,9},{9,8},{10,11... | collective-permute-start | bytes 393224 | tf_op jit(solution)/shard_map/ppermute | solution.py:426
  12.0 10.4 %collective-permute-start.4 = (bf16[512,128]{1,0:T(8,128)(2,1)S(1)}, bf16[512,128]{1,0:T(8,128)(2,1)S(1)}, u32[]{:S(2)}, u32[]{:S(2)}) collective-permute-start(bf16[512,128]{1,0:T(8,128)(2,1)S(1)} %get-tuple-element.105), channel_id=1, source_target_pairs={{0,2},{1,3},{2,0},{3,1},{4,6},{5,7},{6,4},{7,5},{8,10},{9,11},{10,... | collective-permute-start | bytes 393224 | tf_op jit(solution)/shard_map/ppermute | solution.py:426
  13.6 8.8 %collective-permute-start.5 = (bf16[512,128]{1,0:T(8,128)(2,1)S(1)}, bf16[512,128]{1,0:T(8,128)(2,1)S(1)}, u32[]{:S(2)}, u32[]{:S(2)}) collective-permute-start(bf16[512,128]{1,0:T(8,128)(2,1)S(1)} %get-tuple-element.106), channel_id=1, source_target_pairs={{0,3},{1,2},{2,1},{3,0},{4,7},{5,6},{6,5},{7,4},{8,11},{9,10},{10,... | collective-permute-start | bytes 393224 | tf_op jit(solution)/shard_map/ppermute | solution.py:426
  14.2 14.1 %collective-permute-start.7 = (bf16[512,128]{1,0:T(8,128)(2,1)S(1)}, bf16[512,128]{1,0:T(8,128)(2,1)S(1)}, u32[]{:S(2)}, u32[]{:S(2)}) collective-permute-start(bf16[512,128]{1,0:T(8,128)(2,1)S(1)} %group_total.4.refs_5_), channel_id=1, source_target_pairs={{0,4},{1,5},{2,6},{3,7},{8,12},{9,13},{10,14},{11,15},{16,20},{17,... | collective-permute-start | bytes 393224 | tf_op jit(solution)/shard_map/ppermute | solution.py:450
  22.5 10.0 %collective-permute-start.6 = (bf16[512,128]{1,0:T(8,128)(2,1)S(1)}, bf16[512,128]{1,0:T(8,128)(2,1)S(1)}, u32[]{:S(2)}, u32[]{:S(2)}) collective-permute-start(bf16[512,128]{1,0:T(8,128)(2,1)S(1)} %group_total.5.refs_5_), channel_id=1, source_target_pairs={{0,4},{1,5},{2,6},{3,7},{8,12},{9,13},{10,14},{11,15},{16,20},{17,... | collective-permute-start | bytes 393224 | tf_op jit(solution)/shard_map/ppermute | solution.py:450
  28.6 7.8 %collective-permute-start.11 = (bf16[512,128]{1,0:T(8,128)(2,1)S(1)}, bf16[512,128]{1,0:T(8,128)(2,1)S(1)}, u32[]{:S(2)}, u32[]{:S(2)}) collective-permute-start(bf16[512,128]{1,0:T(8,128)(2,1)S(1)} %get-tuple-element.117), channel_id=1, source_target_pairs={{0,1},{1,0},{2,3},{3,2},{4,5},{5,4},{6,7},{7,6},{8,9},{9,8},{10,11... | collective-permute-start | bytes 393224 | tf_op jit(solution)/shard_map/ppermute | solution.py:426
  29.5 7.4 %collective-permute-start.12 = (bf16[512,128]{1,0:T(8,128)(2,1)S(1)}, bf16[512,128]{1,0:T(8,128)(2,1)S(1)}, u32[]{:S(2)}, u32[]{:S(2)}) collective-permute-start(bf16[512,128]{1,0:T(8,128)(2,1)S(1)} %get-tuple-element.118), channel_id=1, source_target_pairs={{0,2},{1,3},{2,0},{3,1},{4,6},{5,7},{6,4},{7,5},{8,10},{9,11},{10,... | collective-permute-start | bytes 393224 | tf_op jit(solution)/shard_map/ppermute | solution.py:426
  32.8 5.5 %collective-permute-start.10 = (bf16[512,128]{1,0:T(8,128)(2,1)S(1)}, bf16[512,128]{1,0:T(8,128)(2,1)S(1)}, u32[]{:S(2)}, u32[]{:S(2)}) collective-permute-start(bf16[512,128]{1,0:T(8,128)(2,1)S(1)} %get-tuple-element.116), channel_id=1, source_target_pairs={{0,2},{1,3},{2,0},{3,1},{4,6},{5,7},{6,4},{7,5},{8,10},{9,11},{10,... | collective-permute-start | bytes 393224 | tf_op jit(solution)/shard_map/ppermute | solution.py:426
  32.9 6.3 %collective-permute-start.9 = (bf16[512,128]{1,0:T(8,128)(2,1)S(1)}, bf16[512,128]{1,0:T(8,128)(2,1)S(1)}, u32[]{:S(2)}, u32[]{:S(2)}) collective-permute-start(bf16[512,128]{1,0:T(8,128)(2,1)S(1)} %get-tuple-element.115), channel_id=1, source_target_pairs={{0,1},{1,0},{2,3},{3,2},{4,5},{5,4},{6,7},{7,6},{8,9},{9,8},{10,11... | collective-permute-start | bytes 393224 | tf_op jit(solution)/shard_map/ppermute | solution.py:426
  33.0 8.8 %collective-permute-start.8 = (bf16[1024,128]{1,0:T(8,128)(2,1)S(1)}, bf16[1024,128]{1,0:T(8,128)(2,1)S(1)}, u32[]{:S(2)}, u32[]{:S(2)}) collective-permute-start(bf16[1024,128]{1,0:T(8,128)(2,1)S(1)} %get-tuple-element.113), channel_id=1, source_target_pairs={{0,3},{1,2},{2,1},{3,0},{4,7},{5,6},{6,5},{7,4},{8,11},{9,10},{10,... | collective-permute-start | bytes 786440 | tf_op jit(solution)/shard_map/ppermute | solution.py:426
  43.9 7.4 %collective-permute-start.13 = (bf16[512,128]{1,0:T(8,128)(2,1)S(1)}, bf16[512,128]{1,0:T(8,128)(2,1)S(1)}, u32[]{:S(2)}, u32[]{:S(2)}) collective-permute-start(bf16[512,128]{1,0:T(8,128)(2,1)S(1)} %get-tuple-element.132), channel_id=1, source_target_pairs={{0,1},{1,0},{2,3},{3,2},{4,5},{5,4},{6,7},{7,6},{8,9},{9,8},{10,11... | collective-permute-start | bytes 393224 | tf_op jit(solution)/shard_map/ppermute | solution.py:426
  44.7 9.0 %collective-permute-start.14 = (bf16[512,128]{1,0:T(8,128)(2,1)S(1)}, bf16[512,128]{1,0:T(8,128)(2,1)S(1)}, u32[]{:S(2)}, u32[]{:S(2)}) collective-permute-start(bf16[512,128]{1,0:T(8,128)(2,1)S(1)} %get-tuple-element.133), channel_id=1, source_target_pairs={{0,2},{1,3},{2,0},{3,1},{4,6},{5,7},{6,4},{7,5},{8,10},{9,11},{10,... | collective-permute-start | bytes 393224 | tf_op jit(solution)/shard_map/ppermute | solution.py:426
  46.4 7.9 %collective-permute-start.15 = (bf16[512,128]{1,0:T(8,128)(2,1)S(1)}, bf16[512,128]{1,0:T(8,128)(2,1)S(1)}, u32[]{:S(2)}, u32[]{:S(2)}) collective-permute-start(bf16[512,128]{1,0:T(8,128)(2,1)S(1)} %get-tuple-element.134), channel_id=1, source_target_pairs={{0,3},{1,2},{2,1},{3,0},{4,7},{5,6},{6,5},{7,4},{8,11},{9,10},{10,... | collective-permute-start | bytes 393224 | tf_op jit(solution)/shard_map/ppermute | solution.py:426
  48.8 11.6 %collective-permute-start.16 = (bf16[512,128]{1,0:T(8,128)(2,1)S(1)}, bf16[512,128]{1,0:T(8,128)(2,1)S(1)}, u32[]{:S(2)}, u32[]{:S(2)}) collective-permute-start(bf16[512,128]{1,0:T(8,128)(2,1)S(1)} %get-tuple-element.142), channel_id=1, source_target_pairs={{0,1},{1,0},{2,3},{3,2},{4,5},{5,4},{6,7},{7,6},{8,9},{9,8},{10,11... | collective-permute-start | bytes 393224 | tf_op jit(solution)/shard_map/ppermute | solution.py:426
  49.7 10.7 %collective-permute-start.17 = (bf16[512,128]{1,0:T(8,128)(2,1)S(1)}, bf16[512,128]{1,0:T(8,128)(2,1)S(1)}, u32[]{:S(2)}, u32[]{:S(2)}) collective-permute-start(bf16[512,128]{1,0:T(8,128)(2,1)S(1)} %get-tuple-element.143), channel_id=1, source_target_pairs={{0,2},{1,3},{2,0},{3,1},{4,6},{5,7},{6,4},{7,5},{8,10},{9,11},{10,... | collective-permute-start | bytes 393224 | tf_op jit(solution)/shard_map/ppermute | solution.py:426
  51.3 9.1 %collective-permute-start.18 = (bf16[512,128]{1,0:T(8,128)(2,1)S(1)}, bf16[512,128]{1,0:T(8,128)(2,1)S(1)}, u32[]{:S(2)}, u32[]{:S(2)}) collective-permute-start(bf16[512,128]{1,0:T(8,128)(2,1)S(1)} %get-tuple-element.144), channel_id=1, source_target_pairs={{0,3},{1,2},{2,1},{3,0},{4,7},{5,6},{6,5},{7,4},{8,11},{9,10},{10,... | collective-permute-start | bytes 393224 | tf_op jit(solution)/shard_map/ppermute | solution.py:426
  54.3 9.6 %collective-permute-start.21 = (bf16[512,128]{1,0:T(8,128)(2,1)S(1)}, bf16[512,128]{1,0:T(8,128)(2,1)S(1)}, u32[]{:S(2)}, u32[]{:S(2)}) collective-permute-start(bf16[512,128]{1,0:T(8,128)(2,1)S(1)} %group_total.6.refs_4_), channel_id=1, source_target_pairs={{4,0},{5,1},{6,2},{7,3},{12,8},{13,9},{14,10},{15,11},{20,16},{21,... | collective-permute-start | bytes 393224 | tf_op jit(solution)/shard_map/ppermute | solution.py:450
  56.9 1.9 %collective-permute-start.19 = (f32[32,128]{1,0:T(8,128)S(1)}, f32[32,128]{1,0:T(8,128)S(1)}, u32[]{:S(2)}, u32[]{:S(2)}) collective-permute-start(f32[32,128]{1,0:T(8,128)S(1)} %get-tuple-element.145.refs_7_.refs_0_), channel_id=1, source_target_pairs={{0,8},{8,0},{16,24},{24,16},{1,9},{9,1},{17,25},{25,17},{2,10},{10... | collective-permute-start | bytes 49160 | tf_op jit(solution)/shard_map/ppermute | solution.py:426
  58.9 5.0 %collective-permute-start.22 = (f32[32,128]{1,0:T(8,128)S(1)}, f32[32,128]{1,0:T(8,128)S(1)}, u32[]{:S(2)}, u32[]{:S(2)}) collective-permute-start(f32[32,128]{1,0:T(8,128)S(1)} %gain_sum.3.refs_4_.refs_0_), channel_id=1, source_target_pairs={{0,16},{8,24},{16,0},{24,8},{1,17},{9,25},{17,1},{25,9},{2,18},{10... | collective-permute-start | bytes 49160 | tf_op jit(solution)/shard_map/ppermute | solution.py:426
  60.5 12.4 %collective-permute-start.20 = (bf16[512,128]{1,0:T(8,128)(2,1)S(1)}, bf16[512,128]{1,0:T(8,128)(2,1)S(1)}, u32[]{:S(2)}, u32[]{:S(2)}) collective-permute-start(bf16[512,128]{1,0:T(8,128)(2,1)S(1)} %group_total.7.refs_7_), channel_id=1, source_target_pairs={{4,0},{5,1},{6,2},{7,3},{12,8},{13,9},{14,10},{15,11},{20,16},{21,... | collective-permute-start | bytes 393224 | tf_op jit(solution)/shard_map/ppermute | solution.py:450
  64.2 18.2 %collective-permute-start.27 = (bf16[512,128]{1,0:T(8,128)(2,1)S(1)}, bf16[512,128]{1,0:T(8,128)(2,1)S(1)}, u32[]{:S(2)}, u32[]{:S(2)}) collective-permute-start(bf16[512,128]{1,0:T(8,128)(2,1)S(1)} %get-tuple-element.170), channel_id=1, source_target_pairs={{0,1},{1,0},{2,3},{3,2},{4,5},{5,4},{6,7},{7,6},{8,9},{9,8},{10,11... | collective-permute-start | bytes 393224 | tf_op jit(solution)/shard_map/ppermute | solution.py:426
  64.6 17.8 %collective-permute-start.28 = (bf16[512,128]{1,0:T(8,128)(2,1)S(1)}, bf16[512,128]{1,0:T(8,128)(2,1)S(1)}, u32[]{:S(2)}, u32[]{:S(2)}) collective-permute-start(bf16[512,128]{1,0:T(8,128)(2,1)S(1)} %get-tuple-element.171), channel_id=1, source_target_pairs={{0,2},{1,3},{2,0},{3,1},{4,6},{5,7},{6,4},{7,5},{8,10},{9,11},{10,... | collective-permute-start | bytes 393224 | tf_op jit(solution)/shard_map/ppermute | solution.py:426
  66.2 6.7 %collective-permute-start.23 = (f32[32,128]{1,0:T(8,128)S(1)}, f32[32,128]{1,0:T(8,128)S(1)}, u32[]{:S(2)}, u32[]{:S(2)}) collective-permute-start(f32[32,128]{1,0:T(8,128)S(1)} %gain_sum.4.refs_5_.refs_0_), channel_id=1, source_target_pairs={{0,4},{1,5},{2,6},{3,7},{4,0},{5,1},{6,2},{7,3},{8,12},{9,13},{10,... | collective-permute-start | bytes 49160 | tf_op jit(solution)/shard_map/ppermute | solution.py:426
  73.2 12.1 %collective-permute-start.26 = (bf16[1088,128]{1,0:T(8,128)(2,1)S(1)}, bf16[1088,128]{1,0:T(8,128)(2,1)S(1)}, u32[]{:S(2)}, u32[]{:S(2)}) collective-permute-start(bf16[1088,128]{1,0:T(8,128)(2,1)S(1)} %get-tuple-element.169), channel_id=1, source_target_pairs={{0,3},{1,2},{2,1},{3,0},{4,7},{5,6},{6,5},{7,4},{8,11},{9,10},{10,... | collective-permute-start | bytes 835592 | tf_op jit(solution)/shard_map/ppermute | solution.py:426
  75.3 9.9 %collective-permute-start.24 = (bf16[576,128]{1,0:T(8,128)(2,1)S(1)}, bf16[576,128]{1,0:T(8,128)(2,1)S(1)}, u32[]{:S(2)}, u32[]{:S(2)}) collective-permute-start(bf16[576,128]{1,0:T(8,128)(2,1)S(1)} %get-tuple-element.167), channel_id=1, source_target_pairs={{0,1},{1,0},{2,3},{3,2},{4,5},{5,4},{6,7},{7,6},{8,9},{9,8},{10,11... | collective-permute-start | bytes 442376 | tf_op jit(solution)/shard_map/ppermute | solution.py:426
  75.9 9.4 %collective-permute-start.25 = (bf16[576,128]{1,0:T(8,128)(2,1)S(1)}, bf16[576,128]{1,0:T(8,128)(2,1)S(1)}, u32[]{:S(2)}, u32[]{:S(2)}) collective-permute-start(bf16[576,128]{1,0:T(8,128)(2,1)S(1)} %get-tuple-element.168), channel_id=1, source_target_pairs={{0,2},{1,3},{2,0},{3,1},{4,6},{5,7},{6,4},{7,5},{8,10},{9,11},{10,... | collective-permute-start | bytes 442376 | tf_op jit(solution)/shard_map/ppermute | solution.py:426

commit v3 on v2

--- a/solution.py
+++ b/solution.py
@@ -12,7 +12,11 @@
 BF16 = jnp.bfloat16
 F32 = jnp.float32
 CHUNKS = 2
-HINTS = {"mix": 10, "outer_gradients": 10}
+MIX_HINTS = (2, 0, 0)
+OUTER_HINTS = (2, 0)
+SPREAD_HINT = 0
+JOB_HINTS = (0, 0, 0, 0)
+NORM_HINTS = (0, 0)
 VMEM_LIMIT = 14 * 1024 * 1024
 
 
@@ -102,7 +106,7 @@
     def token(self):
         return pltpu.VMEM((8, HD), F32)
 
-    def call(self, name, body, rank, streamed, held, outs, after=(), into=(), macs=0, moved=0, scratch=(), grid=(1,)):
+    def call(self, name, body, rank, streamed, held, outs, after=(), into=(), macs=0, moved=0, scratch=(), grid=(1,), hint=0):
         whole = pl.BlockSpec(memory_space=pltpu.VMEM)
         unread = pl.BlockSpec(memory_space=pl.ANY)
         operands = [pltpu.with_memory_space_constraint(a, pltpu.HBM) for a in streamed]
@@ -129,7 +133,7 @@
             input_output_aliases={first + n: at for n, (_, at, _) in enumerate(into)},
             compiler_params=pltpu.CompilerParams(vmem_limit_bytes=VMEM_LIMIT),
             cost_estimate=pl.CostEstimate(
-                flops=int(HINTS.get(name, 0) * 1e9) + 1, bytes_accessed=int(HINTS.get(name, 0) * 3.6e6) + 1, transcendentals=0
+                flops=int(hint * 1e9) + 1, bytes_accessed=int(hint * 3.6e6) + 1, transcendentals=0
             ),
         )(rank, *operands)
 
@@ -232,7 +236,7 @@
     )
 
 
-def mix(layout, rank, kept, prior, jobs, mixed, sums):
+def mix(layout, rank, kept, prior, jobs, mixed, sums, hint):
     chunks = sorted({c for c, _ in jobs})
     fields = [kept[c][n] for c in chunks for n in (3, 0, 1, 2)]
     states = [prior[c][k][0] for c, k in jobs]
@@ -264,7 +268,7 @@
     *outs, square, cross = layout.call(
         "mix", body, rank, [], [*fields, *states, *sums],
         [(layout.kept(F32), None)] * len(chunks) + [(layout.narrow(), None)] * 2,
-        into=[(a, n, pltpu.VMEM) for n, a in old], macs=layout.size * HD, moved=layout.size,
+        into=[(a, n, pltpu.VMEM) for n, a in old], hint=hint,
     )
     return {**mixed, **dict(zip(chunks, outs, strict=True))}, [square, cross]
 
@@ -304,44 +308,55 @@
     return d_mixed, states
 
 
-def normed_output(layout, rank, mixed, out_grad, gain, inv, chunk, into, after):
-    members = layout.members
-
-    def body(r, m_ref, g_ref, gain_ref, inv_ref, o_hbm, part_ref, buffer, sems):
-        copies = []
-        for piece in range(members):
-            at = layout.columns(r, piece, chunk)
+def normed_output(layout, rank, mixed, out_grad, gain, inv, chunk, gain_grad, after, hint):
+    def body(r, m_ref, g_ref, gain_ref, inv_ref, o_ref, part_ref):
+        for piece in range(layout.members):
             for h in range(layout.count):
                 here = (piece, slice(None), lanes(h))
                 normed = m_ref[here] * inv_ref[...]
-                buffer[here] = (normed * gain_ref[piece, :, lanes(h)]).astype(BF16)
+                o_ref[here] = (normed * gain_ref[piece, :, lanes(h)]).astype(BF16)
                 head = ((r[0] ^ piece) * layout.chunks + chunk) * layout.count + h
                 part_ref[pl.ds(head, 1), :] = jnp.sum(g_ref[here].astype(F32) * normed, 0, keepdims=True)
-            copies.append(pltpu.make_async_copy(buffer.at[piece], o_hbm.at[:, at], sems.at[piece]))
-            copies[-1].start()
-        for copy in copies:
-            copy.wait()
 
     return layout.call(
         "normed_output", body, rank, [], [mixed, out_grad, gain, inv],
-        [(layout.wide_shape(), HBM_WHOLE), (pltpu.VMEM((layout.heads, HD), F32), None)],
-        into=[(a, n, m) for n, (a, m) in enumerate(zip(into, (pltpu.HBM, pltpu.VMEM)))], after=after, moved=2 * layout.size,
-        scratch=[pltpu.VMEM((members, layout.tokens, layout.width), BF16), pltpu.SemaphoreType.DMA((members,))],
-    )
-
-
-def inner_gradients(layout, rank, weights, queries, keys, values, d_mixed, prior, chunk, part, dq, own, after):
+        [(layout.kept(BF16), None), (pltpu.VMEM((layout.heads, HD), F32), None)],
+        into=[(a, 1, pltpu.VMEM) for a in gain_grad], after=after, hint=hint,
+    )
+
+
+def inner_gradients(layout, rank, weights, queries, keys, values, d_mixed, prior, chunk, part, own, after, ready=(), stream=(), hint=0):
     first, last = part
+    hbm = [(layout.wide_shape(), HBM_WHOLE)] * 2 if ready else []
 
     def body(r, *refs):
         w_refs, (q_ref, k_ref, v_ref, d_ref, *refs) = refs[: len(weights)], refs[len(weights) :]
-        states, (dq_ref, dk_ref, dv_ref, token_ref, state) = refs[: last - first], refs[last - first :]
-        piece = pl.program_id(0) + first
+        states, refs = refs[: last - first], refs[last - first :]
+        ready_refs, (dq_ref, dk_ref, dv_ref, token_ref, *refs) = refs[: len(ready)], refs[len(ready) :]
+        hbm_refs, (state, sems) = refs[: len(hbm)], refs[len(hbm) :]
+        step = pl.program_id(0)
+        piece = step + first
         token_ref[...] = jnp.zeros_like(token_ref)
 
+        def write(n, c, source, at):
+            target = hbm_refs[n].at[:, layout.columns(r, at, c)]
+            return pltpu.make_async_copy(source.at[at], target, sems.at[n * layout.chunks + c, at])
+
+        def kept_copies(members):
+            for (c, _), ref in zip(ready, ready_refs, strict=True):
+                for at in range(layout.members):
+                    yield write(0, c, ref, at)
+            for at in range(members if ready else 0):
+                yield write(1, chunk, dq_ref, at)
+
+        @pl.when(step == 0)
+        def _():
+            for copy in kept_copies(first):
+                copy.start()
+
         for n, (ref, (_, offset)) in enumerate(zip(states, prior[first:last], strict=True)):
 
-            @pl.when(pl.program_id(0) == n)
+            @pl.when(step == n)
             def _(ref=ref, offset=offset):
                 state[...] = ref[offset : offset + layout.count * HD, :]
 
@@ -355,16 +370,25 @@
         for h in range(layout.count):
             at = (piece, slice(None), lanes(h))
             kept = [w_ref[piece, h] for w_ref in w_refs][: len(d_weights[h])]
-            store_product(dq_ref, at[1:], d_weights[h], k_ref[at], layout.cut(), from_prior[h])
+            store_product(dq_ref, at[1:] if stream else at, d_weights[h], k_ref[at], layout.cut(), from_prior[h])
             store_turned(dk_ref, at, d_weights[h], q_ref[at], layout.cut())
             store_turned(dv_ref, at, kept, d_ref[at], layout.cut())
-
-    return layout.call(
-        "inner_gradients", body, rank, [], [*weights, queries, keys, values, d_mixed, *[a for a, _ in prior[first:last]]],
-        [(layout.wide_shape(), layout.wide(chunk, first)), (layout.kept(F32), None), (layout.kept(F32), None), (layout.token(), None)],
-        into=[(a, n, pltpu.HBM) for n, a in enumerate(dq)] + [(a, n + 1, pltpu.VMEM) for n, a in enumerate(own)], after=after,
-        macs=layout.size * 4 * layout.tokens * (last - first) // layout.members, moved=layout.size,
-        scratch=[pltpu.VMEM((layout.count * HD, HD), BF16)], grid=(last - first,),
+        if ready:
+            write(1, chunk, dq_ref, piece).start()
+
+        @pl.when(step == last - first - 1)
+        def _():
+            for copy in kept_copies(layout.members):
+                copy.wait()
+
+    dq = (layout.wide_shape(), layout.wide(chunk, first)) if stream else (layout.kept(BF16), None)
+    return layout.call(
+        "inner_gradients", body, rank, [],
+        [*weights, queries, keys, values, d_mixed, *[a for a, _ in prior[first:last]], *[a for _, a in ready]],
+        [dq, (layout.kept(F32), None), (layout.kept(F32), None), (layout.token(), None)] + hbm,
+        into=[(a, n, pltpu.VMEM) for n, a in enumerate(own)] + [(a, 0, pltpu.HBM) for a in stream], after=after,
+        scratch=[pltpu.VMEM((layout.count * HD, HD), BF16), pltpu.SemaphoreType.DMA((2 * layout.chunks, layout.members))],
+        grid=(last - first,), hint=hint,
     )
 
 
@@ -374,9 +398,9 @@
     return terms[0]
 
 
-def outer_gradients(layout, rank, keys, values, own, later, jobs, into, extra):
+def outer_gradients(layout, rank, keys, values, own, later, jobs, into, extra, hint):
     chunks = sorted({c for c, _ in jobs})
-    fields = [a for c in chunks for a in (keys[c], values[c], *own[c])]
+    fields = [a for c in chunks for a in (keys[c], values[c], *own[c][1:])]
     states = [later[c][k][0] for c, k in jobs]
     count, heads_all = len(jobs), layout.heads
     gain_out = [(jax.ShapeDtypeStruct((heads_all, HD), F32), HBM_WHOLE)] if extra else []
@@ -416,7 +440,7 @@
         "outer_gradients", body, rank, [], [*fields, *states],
         [(layout.wide_shape(), HBM_WHOLE)] * 2 + gain_out,
         into=[(a, n, pltpu.HBM) for n, a in enumerate(into)],
-        macs=2 * layout.size * HD, moved=4 * layout.size,
+        macs=2 * layout.size * HD, moved=4 * layout.size, hint=hint,
         scratch=[pltpu.VMEM((count, layout.tokens, layout.width), BF16)] * 2
         + [pltpu.VMEM((heads_all, HD), F32), pltpu.SemaphoreType.DMA((3, count))],
     )
@@ -451,7 +475,7 @@
     return bases
 
 
-def spread(layout, rank, got, bases, forward, after, joined=(), gain=()):
+def spread(layout, rank, got, bases, forward, after, joined=(), gain=(), hint=0):
     members, heads_all = layout.members, layout.heads
     extra = 2 * heads_all * len(gain)
     shift = layout.count * HD * len(joined)
@@ -485,17 +509,17 @@
     return layout.call(
         "spread", body, rank, [], [*got, *bases, *joined, *gain],
         [(layout.piece(extra), None)] * (members - 1) + [(layout.piece(extra + shift), None)], after=after,
-        moved=layout.count * HD * HD * 18,
-    )
-
-
-def scatter_back(layout, rank, got, bases, context, forward, mark, between, gain=None):
+        hint=hint,
+    )
+
+
+def scatter_back(layout, rank, got, bases, context, forward, mark, between, gain=None, hint=0):
     far, joined, pieces = layout.members - 1, [], []
     for c in range(layout.chunks):
         final = c == layout.chunks - 1
         mark = between(c, mark)
         rows = [gain()] if final and gain else []
-        outs = spread(layout, rank, got[c], bases[c], forward, mark, joined if final else [], rows)
+        outs = spread(layout, rank, got[c], bases[c], forward, mark, joined if final else [], rows, hint)
         mark = [outs[0]]
         joined.append(outs[far])
         order = range(far if final else far - 1, 0, -1)
@@ -552,9 +576,9 @@
     middle = [(CHUNKS - 1, k) for k in range(far)]
     late = [(c, far) for c in chunks]
     mixed, sums = {}, []
-    for group in (early, middle, late):
+    for group, hint in zip((early, middle, late), MIX_HINTS, strict=True):
         if group:
-            mixed, sums = mix(layout, place, inner, prior, group, mixed, sums)
+            mixed, sums = mix(layout, place, inner, prior, group, mixed, sums, hint)
     inv, factor = norm_factors(layout, place, *sums)
 
     d_mixed, got = [], []
@@ -564,62 +588,66 @@
         d_mixed.append(d_c)
         got.append(gather_home(states, context))
 
-    out, dq, own, gain_grad = [], [], [[] for _ in chunks], None
+    normed, own, gain_grad = {}, [[] for _ in chunks], []
     regular = dp & (dp - 1) == 0 and context & (context - 1) == 0
     steps = xor_steps("dp", dp, 1) + xor_steps("context", context, members) if regular else []
 
-    def inner_job(mark, c, part):
-        nonlocal dq
-        *dq, dk_c, dv_c, token = inner_gradients(
-            layout, place, inner[c][4:], inner[c][0], k_kept[c], v_kept[c], d_mixed[c], prior[c], c, part, dq, own[c], mark
+    def inner_job(mark, c, part, ready=(), stream=(), hint=0):
+        result = inner_gradients(
+            layout, place, inner[c][4:], inner[c][0], k_kept[c], v_kept[c], d_mixed[c], prior[c], c, part, own[c], mark, ready, stream, hint
         )
-        own[c] = [dk_c, dv_c]
-        return [token]
+        *own[c], token = result[:4]
+        return [token], result[4:]
 
     def gain_job(mark):
         nonlocal gain_grad
         if not steps:
             return mark
         axis, size, stride = steps.pop(0)
-        gain_grad = added(layout, place, gain_grad, swap(gain_grad, axis, size, stride), mark)
-        return [gain_grad]
+        gain_grad = [added(layout, place, *gain_grad, swap(*gain_grad, axis, size, stride), mark)]
+        return gain_grad
 
     cuts = sorted({0, members // 4, members // 2, members})
     jobs = [(0, part) for part in zip(cuts[:-1], cuts[1:], strict=True)]
     bases, mark = [], [d_mixed[-1]]
     for c in chunks:
         _, g_c, gain_c = inner[c][:3]
-        out = normed_output(layout, place, mixed[c], g_c, gain_c, inv, c, out, mark)
-        output, gain_grad = out
-        mark = [gain_grad]
-        if c == CHUNKS - 1 and CHUNKS > 1:
-            mark = inner_job(mark, *jobs.pop(0))
+        normed[c], *gain_grad = normed_output(layout, place, mixed[c], g_c, gain_c, inv, c, gain_grad, mark, NORM_HINTS[c])
+        mark = gain_grad
+        if c == CHUNKS - 1:
+            mark, _ = inner_job(mark, *jobs.pop(0), hint=JOB_HINTS[0])
             mark = gain_job(mark)
         total = group_total(layout, place, got[c], mark)
         mark = [total]
         bases.append(cross_groups(total, members, context, False))
 
+    written = []
+
     def between(c, mark):
+        nonlocal written
         if jobs:
-            mark = inner_job(mark, *jobs.pop(0))
+            job = jobs.pop(0)
+            mark, written = inner_job(mark, *job, () if jobs else [*normed.items()], hint=JOB_HINTS[1 + c])
         mark = gain_job(mark)
-        while c == CHUNKS - 1 and (jobs or steps):
-            mark = inner_job(mark, *jobs.pop(0)) if jobs else mark
+        while c == CHUNKS - 1 and steps:
             mark = gain_job(mark)
         return mark
 
-    gain = (lambda: gain_grad) if regular else None
-    later, mark = scatter_back(layout, place, got, bases, context, False, mark, between, gain)
+    gain = (lambda: gain_grad[0]) if regular else None
+    later, mark = scatter_back(layout, place, got, bases, context, False, mark, between, gain, SPREAD_HINT)
     for c in chunks[1:]:
-        mark = inner_job(mark, c, (0, members))
+        output, query_grad = written
+        mark, _ = inner_job(mark, c, (0, members), (), [query_grad], JOB_HINTS[3])
+        written = [output, own[c][0]]
+    output, query_grad = written
     outer = []
-    for group in (early, middle + late):
+    for group, hint in zip((early, middle + late), OUTER_HINTS, strict=True):
         if group:
             extra = regular and group != early
-            *outer, total_gain = [*outer_gradients(layout, place, k_kept, v_kept, own, later, group, outer, extra), None][:3]
+            *outer, total_gain = [*outer_gradients(layout, place, k_kept, v_kept, own, later, group, outer, extra, hint), None][:3]
     if not regular:
-        total_gain = lax.psum(gain_grad, ("dp", "context"))
-    return output[None], dq[0][None], outer[0][None], outer[1][None], total_gain.reshape(features)
+        total_gain = lax.psum(gain_grad[0], ("dp", "context"))
+    return output[None], query_grad[None], outer[0][None], outer[1][None], total_gain.reshape(features)
 
 
 def solution(mesh):

time: 87.9 us -> 87 us (0.990)
  waiting for transfers between devices: 6.34 us -> 7.65 us
  Pallas kernels: 36.9 us -> 35.6 us
  starting transfers between devices: 43.3 us -> 42.3 us
    ppermute x25, waiting for transfers between devices: 6.33 us -> 7.64 us  [swap(): return lax.ppermute(array, axis, [(c, c ^ k) for c in range(size)])]
    pallas_call x29, Pallas kernels: 36.9 us -> 35.6 us  [call(): pl.pallas_call(kernel, name=name, grid_spec=pltpu.PrefetchScalarGridSpec(...]
    ppermute x25, starting transfers between devices: 33.5 us -> 32.4 us  [swap(): return lax.ppermute(array, axis, [(c, c ^ k) for c in range(size)])]
  transfers between devices with their start and end apart: 29 -> 29, of which waited for: 7 -> 7; matrix products, arithmetic and copies ran while one was open for 0% -> 0% of each run, Pallas kernels for 35% -> 33%
where the time goes in v3:
time: 87 us; the launch traced here: 86.7 us
  starting transfers between devices  42.3 us (49%)
  Pallas kernels  35.6 us (41%)
  waiting for transfers between devices  7.65 us (9%)
  between operations  1.17 us (1%)
    pallas_call x29, Pallas kernels, call(): pl.pallas_call(kernel, name=name, grid_spec=pltpu.PrefetchScalarGridSpec(...  35.6 us
    ppermute x25, starting transfers between devices, swap(): return lax.ppermute(array, axis, [(c, c ^ k) for c in range(size)])  32.4 us
    ppermute x4, starting transfers between devices, cross_groups(): lax.ppermute(total, 'context', up if forward else [(b, a) for a, b in up])  9.86 us
    ppermute x25, waiting for transfers between devices, swap(): return lax.ppermute(array, axis, [(c, c ^ k) for c in range(size)])  7.64 us
  transfers between devices with their start and end apart: 29, of which 7 were waited for; matrix products, arithmetic and copies ran while one was open for 0% of the time, Pallas kernels for 33%

profile of v3, /device:TPU:0, one launch (start us, length us, event | category | flops | bytes accessed | tf_op | source)
XLA Modules:
  0.0 86.7 jit_solution(6103233646473453070)
XLA Ops:
  0.6 2.4 %block_states.2 = (bf16[4,320,512]{2,1,0:T(8,128)(2,1)S(1)}, bf16[4,320,512]{2,1,0:T(8,128)(2,1)S(1)}, bf16[512,128]{1,0:T(8,128)(2,1)S(1)}, bf16[512,128]{1,0:T...) custom-call(s32[1]{0:T(128)} %bitcast.r, bf16[320,4096]{1,0:T(8,128)(2,1)} %bitcast.17, ...), custom_call_target="tpu_custom_call" | custom-call | flops 1 | bytes 1 | tf_op jit(solution)/shard_map/block_states/pallas_call | solution.py:122
  3.0 3.0 %collective-permute-start = (bf16[512,128]{1,0:T(8,128)(2,1)S(1)}, bf16[512,128]{1,0:T(8,128)(2,1)S(1)}, u32[]{:S(2)}, u32[]{:S(2)}) collective-permute-start(bf16[512,128]{1,0:T(8,128)(2,1)S(1)} %get-tuple-element.95), channel_id=1, source_target_pairs={{0,1},{1,0},{2,3},{3,2},{4,5},{5,4},{6,7},{7,6},{8,9},{9,8},{10,11... | collective-permute-start | bytes 393224 | tf_op jit(solution)/shard_map/ppermute | solution.py:450
  6.1 1.6 %collective-permute-start.1 = (bf16[512,128]{1,0:T(8,128)(2,1)S(1)}, bf16[512,128]{1,0:T(8,128)(2,1)S(1)}, u32[]{:S(2)}, u32[]{:S(2)}) collective-permute-start(bf16[512,128]{1,0:T(8,128)(2,1)S(1)} %get-tuple-element.96), channel_id=1, source_target_pairs={{0,2},{1,3},{2,0},{3,1},{4,6},{5,7},{6,4},{7,5},{8,10},{9,11},{10,... | collective-permute-start | bytes 393224 | tf_op jit(solution)/shard_map/ppermute | solution.py:450
  7.6 2.4 %block_states.3 = (bf16[4,320,512]{2,1,0:T(8,128)(2,1)S(1)}, bf16[4,320,512]{2,1,0:T(8,128)(2,1)S(1)}, bf16[512,128]{1,0:T(8,128)(2,1)S(1)}, bf16[512,128]{1,0:T...) custom-call(s32[1]{0:T(128)} %bitcast.r, bf16[320,4096]{1,0:T(8,128)(2,1)} %bitcast.18, ...), custom_call_target="tpu_custom_call" | custom-call | flops 1 | bytes 1 | tf_op jit(solution)/shard_map/block_states/pallas_call | solution.py:122
  10.0 2.0 %collective-permute-start.3 = (bf16[512,128]{1,0:T(8,128)(2,1)S(1)}, bf16[512,128]{1,0:T(8,128)(2,1)S(1)}, u32[]{:S(2)}, u32[]{:S(2)}) collective-permute-start(bf16[512,128]{1,0:T(8,128)(2,1)S(1)} %get-tuple-element.107), channel_id=1, source_target_pairs={{0,1},{1,0},{2,3},{3,2},{4,5},{5,4},{6,7},{7,6},{8,9},{9,8},{10,11... | collective-permute-start | bytes 393224 | tf_op jit(solution)/shard_map/ppermute | solution.py:450
  12.0 1.6 %collective-permute-start.4 = (bf16[512,128]{1,0:T(8,128)(2,1)S(1)}, bf16[512,128]{1,0:T(8,128)(2,1)S(1)}, u32[]{:S(2)}, u32[]{:S(2)}) collective-permute-start(bf16[512,128]{1,0:T(8,128)(2,1)S(1)} %get-tuple-element.108), channel_id=1, source_target_pairs={{0,2},{1,3},{2,0},{3,1},{4,6},{5,7},{6,4},{7,5},{8,10},{9,11},{10,... | collective-permute-start | bytes 393224 | tf_op jit(solution)/shard_map/ppermute | solution.py:450
  13.6 0.5 collective-permute-done.2.refs_3_
  14.1 4.7 %collective-permute-start.7 = (bf16[512,128]{1,0:T(8,128)(2,1)S(1)}, bf16[512,128]{1,0:T(8,128)(2,1)S(1)}, u32[]{:S(2)}, u32[]{:S(2)}) collective-permute-start(bf16[512,128]{1,0:T(8,128)(2,1)S(1)} %group_total.4.refs_5_), channel_id=1, source_target_pairs={{0,4},{1,5},{2,6},{3,7},{8,12},{9,13},{10,14},{11,15},{16,20},{17,... | collective-permute-start | bytes 393224 | tf_op jit(solution)/shard_map/ppermute | solution.py:474
  18.9 3.4 %within_block.2 = (bf16[4,320,512]{2,1,0:T(8,128)(2,1)S(1)}, bf16[4,320,512]{2,1,0:T(8,128)(2,1)S(1)}, f32[4,1,512]{2,1,0:T(1,128)S(1)}, f32[4,320,512]{2,1,0:T(...) custom-call(s32[1]{0:T(128)} %bitcast.r, bf16[320,4096]{1,0:T(8,128)(2,1)} %bitcast.13, ...), custom_call_target="tpu_custom_call" | custom-call | flops 1 | bytes 1 | tf_op jit(solution)/shard_map/within_block/pallas_call | solution.py:122
  22.4 2.3 %collective-permute-start.6 = (bf16[512,128]{1,0:T(8,128)(2,1)S(1)}, bf16[512,128]{1,0:T(8,128)(2,1)S(1)}, u32[]{:S(2)}, u32[]{:S(2)}) collective-permute-start(bf16[512,128]{1,0:T(8,128)(2,1)S(1)} %group_total.5.refs_5_), channel_id=1, source_target_pairs={{0,4},{1,5},{2,6},{3,7},{8,12},{9,13},{10,14},{11,15},{16,20},{17,... | collective-permute-start | bytes 393224 | tf_op jit(solution)/shard_map/ppermute | solution.py:474
  24.8 3.5 %within_block.3 = (bf16[4,320,512]{2,1,0:T(8,128)(2,1)S(1)}, bf16[4,320,512]{2,1,0:T(8,128)(2,1)S(1)}, f32[4,1,512]{2,1,0:T(1,128)S(1)}, f32[4,320,512]{2,1,0:T(...) custom-call(s32[1]{0:T(128)} %bitcast.r, bf16[320,4096]{1,0:T(8,128)(2,1)} %bitcast.14, ...), custom_call_target="tpu_custom_call" | custom-call | flops 1 | bytes 1 | tf_op jit(solution)/shard_map/within_block/pallas_call | solution.py:122
  28.6 0.9 %collective-permute-start.11 = (bf16[512,128]{1,0:T(8,128)(2,1)S(1)}, bf16[512,128]{1,0:T(8,128)(2,1)S(1)}, u32[]{:S(2)}, u32[]{:S(2)}) collective-permute-start(bf16[512,128]{1,0:T(8,128)(2,1)S(1)} %get-tuple-element.120), channel_id=1, source_target_pairs={{0,1},{1,0},{2,3},{3,2},{4,5},{5,4},{6,7},{7,6},{8,9},{9,8},{10,11... | collective-permute-start | bytes 393224 | tf_op jit(solution)/shard_map/ppermute | solution.py:450
  29.5 3.0 %collective-permute-start.12 = (bf16[512,128]{1,0:T(8,128)(2,1)S(1)}, bf16[512,128]{1,0:T(8,128)(2,1)S(1)}, u32[]{:S(2)}, u32[]{:S(2)}) collective-permute-start(bf16[512,128]{1,0:T(8,128)(2,1)S(1)} %get-tuple-element.121), channel_id=1, source_target_pairs={{0,2},{1,3},{2,0},{3,1},{4,6},{5,7},{6,4},{7,5},{8,10},{9,11},{10,... | collective-permute-start | bytes 393224 | tf_op jit(solution)/shard_map/ppermute | solution.py:450
  32.9 1.5 %collective-permute-start.9 = (bf16[512,128]{1,0:T(8,128)(2,1)S(1)}, bf16[512,128]{1,0:T(8,128)(2,1)S(1)}, u32[]{:S(2)}, u32[]{:S(2)}) collective-permute-start(bf16[512,128]{1,0:T(8,128)(2,1)S(1)} %get-tuple-element.118), channel_id=1, source_target_pairs={{0,1},{1,0},{2,3},{3,2},{4,5},{5,4},{6,7},{7,6},{8,9},{9,8},{10,11... | collective-permute-start | bytes 393224 | tf_op jit(solution)/shard_map/ppermute | solution.py:450
  34.3 2.0 %collective-permute-start.10 = (bf16[512,128]{1,0:T(8,128)(2,1)S(1)}, bf16[512,128]{1,0:T(8,128)(2,1)S(1)}, u32[]{:S(2)}, u32[]{:S(2)}) collective-permute-start(bf16[512,128]{1,0:T(8,128)(2,1)S(1)} %get-tuple-element.119), channel_id=1, source_target_pairs={{0,2},{1,3},{2,0},{3,1},{4,6},{5,7},{6,4},{7,5},{8,10},{9,11},{10,... | collective-permute-start | bytes 393224 | tf_op jit(solution)/shard_map/ppermute | solution.py:450
  36.3 1.8 %collective-permute-done.11.refs_5_.refs_6_ = bf16[512,128]{1,0:T(8,128)(2,1)S(1)} collective-permute-done((bf16[512,128]{1,0:T(8,128)(2,1)S(1)}, bf16[512,128]{1,0:T(8,128)(2,1)S(1)}, u32[]{:S(2)}, u32[]{:S(2)}) %collective-permute-start.11) | collective-permute-done | bytes 131104 | tf_op jit(solution)/shard_map/ppermute | solution.py:450
  38.1 0.7 mix.3
  38.8 3.2 %collective-permute-done.9.refs_5_.refs_7_ = bf16[512,128]{1,0:T(8,128)(2,1)S(1)} collective-permute-done((bf16[512,128]{1,0:T(8,128)(2,1)S(1)}, bf16[512,128]{1,0:T(8,128)(2,1)S(1)}, u32[]{:S(2)}, u32[]{:S(2)}) %collective-permute-start.9) | collective-permute-done | bytes 131104 | tf_op jit(solution)/shard_map/ppermute | solution.py:450
  42.0 0.7 mix.4
  42.7 0.5 mix.5
  43.3 1.6 %mixed_gradients.2 = (bf16[4,320,512]{2,1,0:T(8,128)(2,1)S(1)}, bf16[512,128]{1,0:T(8,128)(2,1)S(1)}, bf16[512,128]{1,0:T(8,128)(2,1)S(1)}, bf16[512,128]{1,0:T(8,128)(2,1)S(1)}, bf16[512,128]{1,0:T(8,128)(2,1)S(1)}) custom-call(s32[1]{0:T(128)} %bitcast.r, f32[4,320,512]{2,1,0:T(8,128)S(1)} %get-tuple-element.128.refs_0_, ...), custom_call_target="tpu_custom_call" | custom-call | flops 1 | bytes 1 | tf_op jit(solution)/shard_map/mixed_gradients/pallas_call | solution.py:122
  44.9 0.7 collective-permute-start.13
  45.6 1.3 %collective-permute-start.14 = (bf16[512,128]{1,0:T(8,128)(2,1)S(1)}, bf16[512,128]{1,0:T(8,128)(2,1)S(1)}, u32[]{:S(2)}, u32[]{:S(2)}) collective-permute-start(bf16[512,128]{1,0:T(8,128)(2,1)S(1)} %get-tuple-element.139), channel_id=1, source_target_pairs={{0,2},{1,3},{2,0},{3,1},{4,6},{5,7},{6,4},{7,5},{8,10},{9,11},{10,... | collective-permute-start | bytes 393224 | tf_op jit(solution)/shard_map/ppermute | solution.py:450
  46.9 1.6 %collective-permute-start.15 = (bf16[512,128]{1,0:T(8,128)(2,1)S(1)}, bf16[512,128]{1,0:T(8,128)(2,1)S(1)}, u32[]{:S(2)}, u32[]{:S(2)}) collective-permute-start(bf16[512,128]{1,0:T(8,128)(2,1)S(1)} %get-tuple-element.140), channel_id=1, source_target_pairs={{0,3},{1,2},{2,1},{3,0},{4,7},{5,6},{6,5},{7,4},{8,11},{9,10},{10,... | collective-permute-start | bytes 393224 | tf_op jit(solution)/shard_map/ppermute | solution.py:450
  48.5 1.5 %mixed_gradients.3 = (bf16[4,320,512]{2,1,0:T(8,128)(2,1)S(1)}, bf16[512,128]{1,0:T(8,128)(2,1)S(1)}, bf16[512,128]{1,0:T(8,128)(2,1)S(1)}, bf16[512,128]{1,0:T(8,128)(2,1)S(1)}, bf16[512,128]{1,0:T(8,128)(2,1)S(1)}) custom-call(s32[1]{0:T(128)} %bitcast.r, f32[4,320,512]{2,1,0:T(8,128)S(1)} %get-tuple-element.134.refs_0_, ...), custom_call_target="tpu_custom_call" | custom-call | flops 1 | bytes 1 | tf_op jit(solution)/shard_map/mixed_gradients/pallas_call | solution.py:122
  50.0 0.7 collective-permute-start.19
  50.6 1.3 %collective-permute-start.20 = (bf16[512,128]{1,0:T(8,128)(2,1)S(1)}, bf16[512,128]{1,0:T(8,128)(2,1)S(1)}, u32[]{:S(2)}, u32[]{:S(2)}) collective-permute-start(bf16[512,128]{1,0:T(8,128)(2,1)S(1)} %get-tuple-element.147), channel_id=1, source_target_pairs={{0,2},{1,3},{2,0},{3,1},{4,6},{5,7},{6,4},{7,5},{8,10},{9,11},{10,... | collective-permute-start | bytes 393224 | tf_op jit(solution)/shard_map/ppermute | solution.py:450
  52.0 1.6 %collective-permute-start.21 = (bf16[512,128]{1,0:T(8,128)(2,1)S(1)}, bf16[512,128]{1,0:T(8,128)(2,1)S(1)}, u32[]{:S(2)}, u32[]{:S(2)}) collective-permute-start(bf16[512,128]{1,0:T(8,128)(2,1)S(1)} %get-tuple-element.148), channel_id=1, source_target_pairs={{0,3},{1,2},{2,1},{3,0},{4,7},{5,6},{6,5},{7,4},{8,11},{9,10},{10,... | collective-permute-start | bytes 393224 | tf_op jit(solution)/shard_map/ppermute | solution.py:450
  53.5 0.9 %normed_output.2 = (bf16[4,320,512]{2,1,0:T(8,128)(2,1)S(1)}, f32[32,128]{1,0:T(8,128)S(1)}) custom-call(s32[1]{0:T(128)} %bitcast.r, f32[4,320,512]{2,1,0:T(8,128)S(1)} %get-tuple-element.128.refs_0_, bf16[4,320,512]{2,1,0:T(8,128)(2,1)S(1)} %get-tuple-element.102.refs_2_.refs_1_, f32[4,1,512]{2,1,0:T(1,128)S(1)} %get-tuple-element.103.refs_3_.refs_2_, ...), custom_call_target="tpu_custom_call" | custom-call | flops 1 | bytes 1 | tf_op jit(solution)/shard_map/normed_output/pallas_call | solution.py:122
  54.5 0.5 collective-permute-done.15.refs_3_
  55.0 1.3 %collective-permute-start.16 = (bf16[512,128]{1,0:T(8,128)(2,1)S(1)}, bf16[512,128]{1,0:T(8,128)(2,1)S(1)}, u32[]{:S(2)}, u32[]{:S(2)}) collective-permute-start(bf16[512,128]{1,0:T(8,128)(2,1)S(1)} %group_total.6.refs_4_), channel_id=1, source_target_pairs={{4,0},{5,1},{6,2},{7,3},{12,8},{13,9},{14,10},{15,11},{20,16},{21,... | collective-permute-start | bytes 393224 | tf_op jit(solution)/shard_map/ppermute | solution.py:474
  56.3 0.9 %normed_output.3 = (bf16[4,320,512]{2,1,0:T(8,128)(2,1)S(1)}, f32[32,128]{1,0:T(8,128)S(1)}) custom-call(s32[1]{0:T(128)} %bitcast.r, f32[4,320,512]{2,1,0:T(8,128)S(1)} %get-tuple-element.134.refs_0_, bf16[4,320,512]{2,1,0:T(8,128)(2,1)S(1)} %get-tuple-element.112.refs_2_.refs_6_.refs_1_, ...), custom_call_target="tpu_custom_call", output_to_operand_aliasing={{1}: (6, {})} | custom-call | flops 1 | bytes 1 | tf_op jit(solution)/shard_map/normed_output/pallas_call | solution.py:122
  57.3 1.4 %inner_gradients.4 = (bf16[4,320,512]{2,1,0:T(8,128)(2,1)S(1)}, f32[4,320,512]{2,1,0:T(8,128)S(1)}, f32[4,320,512]{2,1,0:T(8,128)S(1)}, f32[8,128]{1,0:T(8,128)S(1)}) custom-call(s32[1]{0:T(128)} %bitcast.r, bf16[4,4,320,256]{3,2,1,0:T(8,128)(2,1)S(1)} %get-tuple-element.98.refs_0_, bf16[4,4,64,64]{3,2,1,0:T(8,128)(2,1)S(1)} %get-tuple-element.99.refs_1_, ...), custom_call_target="tpu_custom_call" | custom-call | flops 1 | bytes 1 | tf_op jit(solution)/shard_map/inner_gradients/pallas_call | solution.py:122
  58.7 0.6 collective-permute-done.21.refs_3_
  59.3 1.5 %collective-permute-start.22 = (bf16[512,128]{1,0:T(8,128)(2,1)S(1)}, bf16[512,128]{1,0:T(8,128)(2,1)S(1)}, u32[]{:S(2)}, u32[]{:S(2)}) collective-permute-start(bf16[512,128]{1,0:T(8,128)(2,1)S(1)} %group_total.7.refs_7_), channel_id=1, source_target_pairs={{4,0},{5,1},{6,2},{7,3},{12,8},{13,9},{14,10},{15,11},{20,16},{21,... | collective-permute-start | bytes 393224 | tf_op jit(solution)/shard_map/ppermute | solution.py:474
  60.9 1.5 %collective-permute-start.18 = (f32[32,128]{1,0:T(8,128)S(1)}, f32[32,128]{1,0:T(8,128)S(1)}, u32[]{:S(2)}, u32[]{:S(2)}) collective-permute-start(f32[32,128]{1,0:T(8,128)S(1)} %gain_sum.3.refs_4_.refs_0_), channel_id=1, source_target_pairs={{0,16},{8,24},{16,0},{24,8},{1,17},{9,25},{17,1},{25,9},{2,18},{10... | collective-permute-start | bytes 49160 | tf_op jit(solution)/shard_map/ppermute | solution.py:450
  62.4 1.4 %inner_gradients.5 = (bf16[4,320,512]{2,1,0:T(8,128)(2,1)S(1)}, f32[4,320,512]{2,1,0:T(8,128)S(1)}, f32[4,320,512]{2,1,0:T(8,128)S(1)}, f32[8,128]{1,0:T(8,128)S(1)}) custom-call(s32[1]{0:T(128)} %bitcast.r, bf16[4,4,320,256]{3,2,1,0:T(8,128)(2,1)S(1)} %get-tuple-element.98.refs_0_, ...), custom_call_target="tpu_custom_call", output_to_operand_aliasing={{0}: (9, {}), {1}: (10, {}), {2}: (11, {})} | custom-call | flops 1 | bytes 1 | tf_op jit(solution)/shard_map/inner_gradients/pallas_call | solution.py:122
  63.8 0.9 %collective-permute-done.18.refs_1_ = f32[32,128]{1,0:T(8,128)S(1)} collective-permute-done((f32[32,128]{1,0:T(8,128)S(1)}, f32[32,128]{1,0:T(8,128)S(1)}, u32[]{:S(2)}, u32[]{:S(2)}) %collective-permute-start.18) | collective-permute-done | bytes 16416 | tf_op jit(solution)/shard_map/ppermute | solution.py:450
  65.0 0.7 collective-permute-start.27
  65.6 0.3 collective-permute-start.28
  66.0 3.6 %collective-permute-start.23 = (f32[32,128]{1,0:T(8,128)S(1)}, f32[32,128]{1,0:T(8,128)S(1)}, u32[]{:S(2)}, u32[]{:S(2)}) collective-permute-start(f32[32,128]{1,0:T(8,128)S(1)} %gain_sum.4.refs_5_.refs_0_), channel_id=1, source_target_pairs={{0,4},{1,5},{2,6},{3,7},{4,0},{5,1},{6,2},{7,3},{8,12},{9,13},{10,... | collective-permute-start | bytes 49160 | tf_op jit(solution)/shard_map/ppermute | solution.py:450
  69.5 3.3 %inner_gradients.6 = (bf16[4,320,512]{2,1,0:T(8,128)(2,1)S(1)}, f32[4,320,512]{2,1,0:T(8,128)S(1)}, f32[4,320,512]{2,1,0:T(8,128)S(1)}, f32[8,128]{1,0:T(8,128)S...) custom-call(s32[1]{0:T(128)} %bitcast.r, ...), custom_call_target="tpu_custom_call", output_to_operand_aliasing={{0}: (12, {}), {1}: (13, {}), {2}: (14, {})} | custom-call | flops 1 | bytes 1 | tf_op jit(solution)/shard_map/inner_gradients/pallas_call | solution.py:122
  73.2 2.6 %collective-permute-start.26 = (bf16[1088,128]{1,0:T(8,128)(2,1)S(1)}, bf16[1088,128]{1,0:T(8,128)(2,1)S(1)}, u32[]{:S(2)}, u32[]{:S(2)}) collective-permute-start(bf16[1088,128]{1,0:T(8,128)(2,1)S(1)} %get-tuple-element.171), channel_id=1, source_target_pairs={{0,3},{1,2},{2,1},{3,0},{4,7},{5,6},{6,5},{7,4},{8,11},{9,10},{10,... | collective-permute-start | bytes 835592 | tf_op jit(solution)/shard_map/ppermute | solution.py:450
  75.8 0.6 collective-permute-start.24
  76.4 0.3 collective-permute-start.25
  76.7 5.7 %inner_gradients.7 = (bf16[320,4096]{1,0:T(8,128)(2,1)}, f32[4,320,512]{2,1,0:T(8,128)S(1)}, f32[4,320,512]{2,1,0:T(8,128)S(1)}, f32[8,128]{1,0:T(8,128)}) custom-call(s32[1]{0:T(128)} %bitcast.r, bf16[4,4,320,256]{3,2,1,0:T(8,128)(2,1)S(1)} %get-tuple-element.158.refs_0_, ...), custom_call_target="tpu_custom_call", output_to_operand_aliasing={{0}: (12, {})} | custom-call | flops 1 | bytes 1 | tf_op jit(solution)/shard_map/inner_gradients/pallas_call | solution.py:122
  82.5 1.7 %outer_gradients.2 = (bf16[320,4096]{1,0:T(8,128)(2,1)}, bf16[320,4096]{1,0:T(8,128)(2,1)}) custom-call(s32[1]{0:T(128)} %bitcast.r, bf16[4,320,512]{2,1,0:T(8,128)(2,1)S(1)} %get-tuple-element.92.refs_3_.refs_0_, bf16[4,320,512]{2,1,0:T(8,128)(2,1)S(1)} %get-tuple-element.93.refs_4_.refs_1_, f32[4,320,512]{2,1,0:T(8,128)S(1)} %get-tuple-element.165.refs_2_, ...), custom_call_target="tpu_custom_call" | custom-call | flops 2000000000 | bytes 7200001 | tf_op jit(solution)/shard_map/outer_gradients/pallas_call | solution.py:122
  84.4 2.2 %outer_gradients.3 = (bf16[320,4096]{1,0:T(8,128)(2,1)}, bf16[320,4096]{1,0:T(8,128)(2,1)}, f32[32,128]{1,0:T(8,128)}) custom-call(s32[1]{0:T(128)} %bitcast.r, bf16[4,320,512]{2,1,0:T(8,128)(2,1)S(1)} %get-tuple-element.92.refs_3_.refs_0_, ...), custom_call_target="tpu_custom_call", output_to_operand_aliasing={{0}: (14, {}), {1}: (15, {})} | custom-call | flops 1 | bytes 1 | tf_op jit(solution)/shard_map/outer_gradients/pallas_call | solution.py:122
  (41 shorter events, 2.0 us)
Async XLA Ops:
  3.0 10.5 %collective-permute-start = (bf16[512,128]{1,0:T(8,128)(2,1)S(1)}, bf16[512,128]{1,0:T(8,128)(2,1)S(1)}, u32[]{:S(2)}, u32[]{:S(2)}) collective-permute-start(bf16[512,128]{1,0:T(8,128)(2,1)S(1)} %get-tuple-element.95), channel_id=1, source_target_pairs={{0,1},{1,0},{2,3},{3,2},{4,5},{5,4},{6,7},{7,6},{8,9},{9,8},{10,11... | collective-permute-start | bytes 393224 | tf_op jit(solution)/shard_map/ppermute | solution.py:450
  6.1 7.5 %collective-permute-start.1 = (bf16[512,128]{1,0:T(8,128)(2,1)S(1)}, bf16[512,128]{1,0:T(8,128)(2,1)S(1)}, u32[]{:S(2)}, u32[]{:S(2)}) collective-permute-start(bf16[512,128]{1,0:T(8,128)(2,1)S(1)} %get-tuple-element.96), channel_id=1, source_target_pairs={{0,2},{1,3},{2,0},{3,1},{4,6},{5,7},{6,4},{7,5},{8,10},{9,11},{10,... | collective-permute-start | bytes 393224 | tf_op jit(solution)/shard_map/ppermute | solution.py:450
  7.6 11.2 %copy-start = (f32[4096]{0:T(1024)S(1)}, f32[4096]{0:T(1024)}, u32[]{:S(2)}) copy-start(f32[4096]{0:T(1024)} %param.8) | copy-start | bytes 49156
  7.6 6.4 %collective-permute-start.2 = (bf16[512,128]{1,0:T(8,128)(2,1)S(1)}, bf16[512,128]{1,0:T(8,128)(2,1)S(1)}, u32[]{:S(2)}, u32[]{:S(2)}) collective-permute-start(bf16[512,128]{1,0:T(8,128)(2,1)S(1)} %get-tuple-element.97), channel_id=1, source_target_pairs={{0,3},{1,2},{2,1},{3,0},{4,7},{5,6},{6,5},{7,4},{8,11},{9,10},{10,... | collective-permute-start | bytes 393224 | tf_op jit(solution)/shard_map/ppermute | solution.py:450
  10.0 12.3 %collective-permute-start.3 = (bf16[512,128]{1,0:T(8,128)(2,1)S(1)}, bf16[512,128]{1,0:T(8,128)(2,1)S(1)}, u32[]{:S(2)}, u32[]{:S(2)}) collective-permute-start(bf16[512,128]{1,0:T(8,128)(2,1)S(1)} %get-tuple-element.107), channel_id=1, source_target_pairs={{0,1},{1,0},{2,3},{3,2},{4,5},{5,4},{6,7},{7,6},{8,9},{9,8},{10,11... | collective-permute-start | bytes 393224 | tf_op jit(solution)/shard_map/ppermute | solution.py:450
  12.0 10.4 %collective-permute-start.4 = (bf16[512,128]{1,0:T(8,128)(2,1)S(1)}, bf16[512,128]{1,0:T(8,128)(2,1)S(1)}, u32[]{:S(2)}, u32[]{:S(2)}) collective-permute-start(bf16[512,128]{1,0:T(8,128)(2,1)S(1)} %get-tuple-element.108), channel_id=1, source_target_pairs={{0,2},{1,3},{2,0},{3,1},{4,6},{5,7},{6,4},{7,5},{8,10},{9,11},{10,... | collective-permute-start | bytes 393224 | tf_op jit(solution)/shard_map/ppermute | solution.py:450
  13.6 8.8 %collective-permute-start.5 = (bf16[512,128]{1,0:T(8,128)(2,1)S(1)}, bf16[512,128]{1,0:T(8,128)(2,1)S(1)}, u32[]{:S(2)}, u32[]{:S(2)}) collective-permute-start(bf16[512,128]{1,0:T(8,128)(2,1)S(1)} %get-tuple-element.109), channel_id=1, source_target_pairs={{0,3},{1,2},{2,1},{3,0},{4,7},{5,6},{6,5},{7,4},{8,11},{9,10},{10,... | collective-permute-start | bytes 393224 | tf_op jit(solution)/shard_map/ppermute | solution.py:450
  14.1 14.1 %collective-permute-start.7 = (bf16[512,128]{1,0:T(8,128)(2,1)S(1)}, bf16[512,128]{1,0:T(8,128)(2,1)S(1)}, u32[]{:S(2)}, u32[]{:S(2)}) collective-permute-start(bf16[512,128]{1,0:T(8,128)(2,1)S(1)} %group_total.4.refs_5_), channel_id=1, source_target_pairs={{0,4},{1,5},{2,6},{3,7},{8,12},{9,13},{10,14},{11,15},{16,20},{17,... | collective-permute-start | bytes 393224 | tf_op jit(solution)/shard_map/ppermute | solution.py:474
  22.4 10.1 %collective-permute-start.6 = (bf16[512,128]{1,0:T(8,128)(2,1)S(1)}, bf16[512,128]{1,0:T(8,128)(2,1)S(1)}, u32[]{:S(2)}, u32[]{:S(2)}) collective-permute-start(bf16[512,128]{1,0:T(8,128)(2,1)S(1)} %group_total.5.refs_5_), channel_id=1, source_target_pairs={{0,4},{1,5},{2,6},{3,7},{8,12},{9,13},{10,14},{11,15},{16,20},{17,... | collective-permute-start | bytes 393224 | tf_op jit(solution)/shard_map/ppermute | solution.py:474
  28.6 9.5 %collective-permute-start.11 = (bf16[512,128]{1,0:T(8,128)(2,1)S(1)}, bf16[512,128]{1,0:T(8,128)(2,1)S(1)}, u32[]{:S(2)}, u32[]{:S(2)}) collective-permute-start(bf16[512,128]{1,0:T(8,128)(2,1)S(1)} %get-tuple-element.120), channel_id=1, source_target_pairs={{0,1},{1,0},{2,3},{3,2},{4,5},{5,4},{6,7},{7,6},{8,9},{9,8},{10,11... | collective-permute-start | bytes 393224 | tf_op jit(solution)/shard_map/ppermute | solution.py:450
  29.5 8.6 %collective-permute-start.12 = (bf16[512,128]{1,0:T(8,128)(2,1)S(1)}, bf16[512,128]{1,0:T(8,128)(2,1)S(1)}, u32[]{:S(2)}, u32[]{:S(2)}) collective-permute-start(bf16[512,128]{1,0:T(8,128)(2,1)S(1)} %get-tuple-element.121), channel_id=1, source_target_pairs={{0,2},{1,3},{2,0},{3,1},{4,6},{5,7},{6,4},{7,5},{8,10},{9,11},{10,... | collective-permute-start | bytes 393224 | tf_op jit(solution)/shard_map/ppermute | solution.py:450
  32.8 9.9 %collective-permute-start.8 = (bf16[1024,128]{1,0:T(8,128)(2,1)S(1)}, bf16[1024,128]{1,0:T(8,128)(2,1)S(1)}, u32[]{:S(2)}, u32[]{:S(2)}) collective-permute-start(bf16[1024,128]{1,0:T(8,128)(2,1)S(1)} %get-tuple-element.116), channel_id=1, source_target_pairs={{0,3},{1,2},{2,1},{3,0},{4,7},{5,6},{6,5},{7,4},{8,11},{9,10},{10,... | collective-permute-start | bytes 786440 | tf_op jit(solution)/shard_map/ppermute | solution.py:450
  32.9 9.1 %collective-permute-start.9 = (bf16[512,128]{1,0:T(8,128)(2,1)S(1)}, bf16[512,128]{1,0:T(8,128)(2,1)S(1)}, u32[]{:S(2)}, u32[]{:S(2)}) collective-permute-start(bf16[512,128]{1,0:T(8,128)(2,1)S(1)} %get-tuple-element.118), channel_id=1, source_target_pairs={{0,1},{1,0},{2,3},{3,2},{4,5},{5,4},{6,7},{7,6},{8,9},{9,8},{10,11... | collective-permute-start | bytes 393224 | tf_op jit(solution)/shard_map/ppermute | solution.py:450
  34.3 7.6 %collective-permute-start.10 = (bf16[512,128]{1,0:T(8,128)(2,1)S(1)}, bf16[512,128]{1,0:T(8,128)(2,1)S(1)}, u32[]{:S(2)}, u32[]{:S(2)}) collective-permute-start(bf16[512,128]{1,0:T(8,128)(2,1)S(1)} %get-tuple-element.119), channel_id=1, source_target_pairs={{0,2},{1,3},{2,0},{3,1},{4,6},{5,7},{6,4},{7,5},{8,10},{9,11},{10,... | collective-permute-start | bytes 393224 | tf_op jit(solution)/shard_map/ppermute | solution.py:450
  44.9 7.1 %collective-permute-start.13 = (bf16[512,128]{1,0:T(8,128)(2,1)S(1)}, bf16[512,128]{1,0:T(8,128)(2,1)S(1)}, u32[]{:S(2)}, u32[]{:S(2)}) collective-permute-start(bf16[512,128]{1,0:T(8,128)(2,1)S(1)} %get-tuple-element.138), channel_id=1, source_target_pairs={{0,1},{1,0},{2,3},{3,2},{4,5},{5,4},{6,7},{7,6},{8,9},{9,8},{10,11... | collective-permute-start | bytes 393224 | tf_op jit(solution)/shard_map/ppermute | solution.py:450
  45.6 8.9 %collective-permute-start.14 = (bf16[512,128]{1,0:T(8,128)(2,1)S(1)}, bf16[512,128]{1,0:T(8,128)(2,1)S(1)}, u32[]{:S(2)}, u32[]{:S(2)}) collective-permute-start(bf16[512,128]{1,0:T(8,128)(2,1)S(1)} %get-tuple-element.139), channel_id=1, source_target_pairs={{0,2},{1,3},{2,0},{3,1},{4,6},{5,7},{6,4},{7,5},{8,10},{9,11},{10,... | collective-permute-start | bytes 393224 | tf_op jit(solution)/shard_map/ppermute | solution.py:450
  46.9 8.0 %collective-permute-start.15 = (bf16[512,128]{1,0:T(8,128)(2,1)S(1)}, bf16[512,128]{1,0:T(8,128)(2,1)S(1)}, u32[]{:S(2)}, u32[]{:S(2)}) collective-permute-start(bf16[512,128]{1,0:T(8,128)(2,1)S(1)} %get-tuple-element.140), channel_id=1, source_target_pairs={{0,3},{1,2},{2,1},{3,0},{4,7},{5,6},{6,5},{7,4},{8,11},{9,10},{10,... | collective-permute-start | bytes 393224 | tf_op jit(solution)/shard_map/ppermute | solution.py:450
  50.0 8.7 %collective-permute-start.19 = (bf16[512,128]{1,0:T(8,128)(2,1)S(1)}, bf16[512,128]{1,0:T(8,128)(2,1)S(1)}, u32[]{:S(2)}, u32[]{:S(2)}) collective-permute-start(bf16[512,128]{1,0:T(8,128)(2,1)S(1)} %get-tuple-element.146), channel_id=1, source_target_pairs={{0,1},{1,0},{2,3},{3,2},{4,5},{5,4},{6,7},{7,6},{8,9},{9,8},{10,11... | collective-permute-start | bytes 393224 | tf_op jit(solution)/shard_map/ppermute | solution.py:450
  50.6 8.1 %collective-permute-start.20 = (bf16[512,128]{1,0:T(8,128)(2,1)S(1)}, bf16[512,128]{1,0:T(8,128)(2,1)S(1)}, u32[]{:S(2)}, u32[]{:S(2)}) collective-permute-start(bf16[512,128]{1,0:T(8,128)(2,1)S(1)} %get-tuple-element.147), channel_id=1, source_target_pairs={{0,2},{1,3},{2,0},{3,1},{4,6},{5,7},{6,4},{7,5},{8,10},{9,11},{10,... | collective-permute-start | bytes 393224 | tf_op jit(solution)/shard_map/ppermute | solution.py:450
  52.0 7.3 %collective-permute-start.21 = (bf16[512,128]{1,0:T(8,128)(2,1)S(1)}, bf16[512,128]{1,0:T(8,128)(2,1)S(1)}, u32[]{:S(2)}, u32[]{:S(2)}) collective-permute-start(bf16[512,128]{1,0:T(8,128)(2,1)S(1)} %get-tuple-element.148), channel_id=1, source_target_pairs={{0,3},{1,2},{2,1},{3,0},{4,7},{5,6},{6,5},{7,4},{8,11},{9,10},{10,... | collective-permute-start | bytes 393224 | tf_op jit(solution)/shard_map/ppermute | solution.py:450
  55.0 9.7 %collective-permute-start.16 = (bf16[512,128]{1,0:T(8,128)(2,1)S(1)}, bf16[512,128]{1,0:T(8,128)(2,1)S(1)}, u32[]{:S(2)}, u32[]{:S(2)}) collective-permute-start(bf16[512,128]{1,0:T(8,128)(2,1)S(1)} %group_total.6.refs_4_), channel_id=1, source_target_pairs={{4,0},{5,1},{6,2},{7,3},{12,8},{13,9},{14,10},{15,11},{20,16},{21,... | collective-permute-start | bytes 393224 | tf_op jit(solution)/shard_map/ppermute | solution.py:474
  57.2 1.4 %collective-permute-start.17 = (f32[32,128]{1,0:T(8,128)S(1)}, f32[32,128]{1,0:T(8,128)S(1)}, u32[]{:S(2)}, u32[]{:S(2)}) collective-permute-start(f32[32,128]{1,0:T(8,128)S(1)} %get-tuple-element.143.refs_7_.refs_0_), channel_id=1, source_target_pairs={{0,8},{8,0},{16,24},{24,16},{1,9},{9,1},{17,25},{25,17},{2,10},{10... | collective-permute-start | bytes 49160 | tf_op jit(solution)/shard_map/ppermute | solution.py:450
  59.3 13.5 %collective-permute-start.22 = (bf16[512,128]{1,0:T(8,128)(2,1)S(1)}, bf16[512,128]{1,0:T(8,128)(2,1)S(1)}, u32[]{:S(2)}, u32[]{:S(2)}) collective-permute-start(bf16[512,128]{1,0:T(8,128)(2,1)S(1)} %group_total.7.refs_7_), channel_id=1, source_target_pairs={{4,0},{5,1},{6,2},{7,3},{12,8},{13,9},{14,10},{15,11},{20,16},{21,... | collective-permute-start | bytes 393224 | tf_op jit(solution)/shard_map/ppermute | solution.py:474
  60.9 3.8 %collective-permute-start.18 = (f32[32,128]{1,0:T(8,128)S(1)}, f32[32,128]{1,0:T(8,128)S(1)}, u32[]{:S(2)}, u32[]{:S(2)}) collective-permute-start(f32[32,128]{1,0:T(8,128)S(1)} %gain_sum.3.refs_4_.refs_0_), channel_id=1, source_target_pairs={{0,16},{8,24},{16,0},{24,8},{1,17},{9,25},{17,1},{25,9},{2,18},{10... | collective-permute-start | bytes 49160 | tf_op jit(solution)/shard_map/ppermute | solution.py:450
  65.0 17.5 %collective-permute-start.27 = (bf16[512,128]{1,0:T(8,128)(2,1)S(1)}, bf16[512,128]{1,0:T(8,128)(2,1)S(1)}, u32[]{:S(2)}, u32[]{:S(2)}) collective-permute-start(bf16[512,128]{1,0:T(8,128)(2,1)S(1)} %get-tuple-element.172), channel_id=1, source_target_pairs={{0,1},{1,0},{2,3},{3,2},{4,5},{5,4},{6,7},{7,6},{8,9},{9,8},{10,11... | collective-permute-start | bytes 393224 | tf_op jit(solution)/shard_map/ppermute | solution.py:450
  65.6 16.8 %collective-permute-start.28 = (bf16[512,128]{1,0:T(8,128)(2,1)S(1)}, bf16[512,128]{1,0:T(8,128)(2,1)S(1)}, u32[]{:S(2)}, u32[]{:S(2)}) collective-permute-start(bf16[512,128]{1,0:T(8,128)(2,1)S(1)} %get-tuple-element.173), channel_id=1, source_target_pairs={{0,2},{1,3},{2,0},{3,1},{4,6},{5,7},{6,4},{7,5},{8,10},{9,11},{10,... | collective-permute-start | bytes 393224 | tf_op jit(solution)/shard_map/ppermute | solution.py:450
  66.0 6.9 %collective-permute-start.23 = (f32[32,128]{1,0:T(8,128)S(1)}, f32[32,128]{1,0:T(8,128)S(1)}, u32[]{:S(2)}, u32[]{:S(2)}) collective-permute-start(f32[32,128]{1,0:T(8,128)S(1)} %gain_sum.4.refs_5_.refs_0_), channel_id=1, source_target_pairs={{0,4},{1,5},{2,6},{3,7},{4,0},{5,1},{6,2},{7,3},{8,12},{9,13},{10,... | collective-permute-start | bytes 49160 | tf_op jit(solution)/shard_map/ppermute | solution.py:450
  73.2 11.2 %collective-permute-start.26 = (bf16[1088,128]{1,0:T(8,128)(2,1)S(1)}, bf16[1088,128]{1,0:T(8,128)(2,1)S(1)}, u32[]{:S(2)}, u32[]{:S(2)}) collective-permute-start(bf16[1088,128]{1,0:T(8,128)(2,1)S(1)} %get-tuple-element.171), channel_id=1, source_target_pairs={{0,3},{1,2},{2,1},{3,0},{4,7},{5,6},{6,5},{7,4},{8,11},{9,10},{10,... | collective-permute-start | bytes 835592 | tf_op jit(solution)/shard_map/ppermute | solution.py:450
  75.8 8.6 %collective-permute-start.24 = (bf16[576,128]{1,0:T(8,128)(2,1)S(1)}, bf16[576,128]{1,0:T(8,128)(2,1)S(1)}, u32[]{:S(2)}, u32[]{:S(2)}) collective-permute-start(bf16[576,128]{1,0:T(8,128)(2,1)S(1)} %get-tuple-element.169), channel_id=1, source_target_pairs={{0,1},{1,0},{2,3},{3,2},{4,5},{5,4},{6,7},{7,6},{8,9},{9,8},{10,11... | collective-permute-start | bytes 442376 | tf_op jit(solution)/shard_map/ppermute | solution.py:450
  76.4 8.0 %collective-permute-start.25 = (bf16[576,128]{1,0:T(8,128)(2,1)S(1)}, bf16[576,128]{1,0:T(8,128)(2,1)S(1)}, u32[]{:S(2)}, u32[]{:S(2)}) collective-permute-start(bf16[576,128]{1,0:T(8,128)(2,1)S(1)} %get-tuple-element.170), channel_id=1, source_target_pairs={{0,2},{1,3},{2,0},{3,1},{4,6},{5,7},{6,4},{7,5},{8,10},{9,11},{10,... | collective-permute-start | bytes 442376 | tf_op jit(solution)/shard_map/ppermute | solution.py:450

commit v4 on v3

--- a/solution.py
+++ b/solution.py
@@ -12,11 +12,9 @@
 BF16 = jnp.bfloat16
 F32 = jnp.float32
 CHUNKS = 2
-MIX_HINTS = (2, 0, 0)
-OUTER_HINTS = (2, 0)
+MIX_HINTS = (10, 10, 10)
+OUTER_HINT = 2
 SPREAD_HINT = 0
-JOB_HINTS = (0, 0, 0, 0)
-NORM_HINTS = (0, 0)
 VMEM_LIMIT = 14 * 1024 * 1024
 
 
@@ -308,7 +306,7 @@
     return d_mixed, states
 
 
-def normed_output(layout, rank, mixed, out_grad, gain, inv, chunk, gain_grad, after, hint):
+def normed_output(layout, rank, mixed, out_grad, gain, inv, chunk, gain_grad, after):
     def body(r, m_ref, g_ref, gain_ref, inv_ref, o_ref, part_ref):
         for piece in range(layout.members):
             for h in range(layout.count):
@@ -321,19 +319,25 @@
     return layout.call(
         "normed_output", body, rank, [], [mixed, out_grad, gain, inv],
         [(layout.kept(BF16), None), (pltpu.VMEM((layout.heads, HD), F32), None)],
-        into=[(a, 1, pltpu.VMEM) for a in gain_grad], after=after, hint=hint,
-    )
-
-
-def inner_gradients(layout, rank, weights, queries, keys, values, d_mixed, prior, chunk, part, own, after, ready=(), stream=(), hint=0):
+        into=[(a, 1, pltpu.VMEM) for a in gain_grad], after=after,
+    )
+
+
+def inner_gradients(
+    layout, rank, weights, queries, keys, values, d_mixed, prior, chunk, part, own, after, ready=(), others=(), also=(), hint=0
+):
     first, last = part
-    hbm = [(layout.wide_shape(), HBM_WHOLE)] * 2 if ready else []
+    targets = ([0] if ready else []) + ([1] if others else []) + ([2, 3] if also else [])
+    hbm = [(layout.wide_shape(), HBM_WHOLE)] * len(targets)
+    lists = [*((0, c, a) for c, a in ready), *((1, c, a) for c, a in others)]
+    extra = max(len(also) - 4, 0)
 
     def body(r, *refs):
         w_refs, (q_ref, k_ref, v_ref, d_ref, *refs) = refs[: len(weights)], refs[len(weights) :]
         states, refs = refs[: last - first], refs[last - first :]
-        ready_refs, (dq_ref, dk_ref, dv_ref, token_ref, *refs) = refs[: len(ready)], refs[len(ready) :]
-        hbm_refs, (state, sems) = refs[: len(hbm)], refs[len(hbm) :]
+        list_refs, refs = refs[: len(lists)], refs[len(lists) :]
+        also_refs, (dq_ref, dk_ref, dv_ref, token_ref, *refs) = refs[: len(also)], refs[len(also) :]
+        hbm_refs, (state, dk_buffer, dv_buffer, sems) = dict(zip(targets, refs)), refs[len(hbm) :]
         step = pl.program_id(0)
         piece = step + first
         token_ref[...] = jnp.zeros_like(token_ref)
@@ -342,16 +346,17 @@
             target = hbm_refs[n].at[:, layout.columns(r, at, c)]
             return pltpu.make_async_copy(source.at[at], target, sems.at[n * layout.chunks + c, at])
 
-        def kept_copies(members):
-            for (c, _), ref in zip(ready, ready_refs, strict=True):
+        def list_copies():
+            for (n, c, _), ref in zip(lists, list_refs, strict=True):
                 for at in range(layout.members):
-                    yield write(0, c, ref, at)
-            for at in range(members if ready else 0):
-                yield write(1, chunk, dq_ref, at)
+                    yield write(n, c, ref, at)
+
+        def outer_copies(at):
+            return [write(n, 0, ref, at) for n, ref in ((2, dk_buffer), (3, dv_buffer))]
 
         @pl.when(step == 0)
         def _():
-            for copy in kept_copies(first):
+            for copy in list_copies():
                 copy.start()
 
         for n, (ref, (_, offset)) in enumerate(zip(states, prior[first:last], strict=True)):
@@ -359,6 +364,14 @@
             @pl.when(step == n)
             def _(ref=ref, offset=offset):
                 state[...] = ref[offset : offset + layout.count * HD, :]
+
+        for n in range(extra):
+
+            @pl.when(step == n)
+            def _(n=n):
+                store_outer(layout, also_refs[:4], also_refs[4 + n], 0, n, dk_buffer, dv_buffer, n)
+                for copy in outer_copies(n):
+                    copy.start()
 
         d_weights, from_prior = [], []
         for h in range(layout.count):
@@ -370,26 +383,49 @@
         for h in range(layout.count):
             at = (piece, slice(None), lanes(h))
             kept = [w_ref[piece, h] for w_ref in w_refs][: len(d_weights[h])]
-            store_product(dq_ref, at[1:] if stream else at, d_weights[h], k_ref[at], layout.cut(), from_prior[h])
+            store_product(dq_ref, at, d_weights[h], k_ref[at], layout.cut(), from_prior[h])
             store_turned(dk_ref, at, d_weights[h], q_ref[at], layout.cut())
             store_turned(dv_ref, at, kept, d_ref[at], layout.cut())
-        if ready:
-            write(1, chunk, dq_ref, piece).start()
+        if others:
+
+            @pl.when(step < last - first - 1)
+            def _():
+                write(1, chunk, dq_ref, piece).start()
 
         @pl.when(step == last - first - 1)
         def _():
-            for copy in kept_copies(layout.members):
+            for copy in list_copies():
                 copy.wait()
-
-    dq = (layout.wide_shape(), layout.wide(chunk, first)) if stream else (layout.kept(BF16), None)
+            for at in range(first, last - 1 if others else first):
+                write(1, chunk, dq_ref, at).wait()
+            for n in range(extra):
+                for copy in outer_copies(n):
+                    copy.wait()
+
+    buffer = pltpu.VMEM((max(extra, 1), layout.tokens, layout.width), BF16)
     return layout.call(
         "inner_gradients", body, rank, [],
-        [*weights, queries, keys, values, d_mixed, *[a for a, _ in prior[first:last]], *[a for _, a in ready]],
-        [dq, (layout.kept(F32), None), (layout.kept(F32), None), (layout.token(), None)] + hbm,
-        into=[(a, n, pltpu.VMEM) for n, a in enumerate(own)] + [(a, 0, pltpu.HBM) for a in stream], after=after,
-        scratch=[pltpu.VMEM((layout.count * HD, HD), BF16), pltpu.SemaphoreType.DMA((2 * layout.chunks, layout.members))],
-        grid=(last - first,), hint=hint,
-    )
+        [*weights, queries, keys, values, d_mixed, *[a for a, _ in prior[first:last]], *[a for _, _, a in lists], *also],
+        [(layout.kept(BF16), None), (layout.kept(F32), None), (layout.kept(F32), None), (layout.token(), None)] + hbm,
+        into=[(a, n, pltpu.VMEM) for n, a in enumerate(own)], after=after, hint=hint,
+        scratch=[
+            pltpu.VMEM((layout.count * HD, HD), BF16), buffer, buffer,
+            pltpu.SemaphoreType.DMA((4 * layout.chunks, layout.members)),
+        ],
+        grid=(last - first,),
+    )
+
+
+def store_outer(layout, fields, state, offset, piece, dk_buffer, dv_buffer, slot):
+    k_ref, v_ref, dki_ref, dvi_ref = fields
+    sums = []
+    for heads in pairs_of(layout.count):
+        here = (piece, slice(None), span(heads))
+        block = diagonal([state[rows_of(h, offset), :] for h in heads])
+        sums.append((heads, here, dot(v_ref[here], block, (1, 1)), dot(k_ref[here], block, (1, 0))))
+    for heads, here, dk, dv in sums:
+        dk_buffer[slot, :, span(heads)] = (dki_ref[here] + dk).astype(BF16)
+        dv_buffer[slot, :, span(heads)] = (dvi_ref[here] + dv).astype(BF16)
 
 
 def pairwise(terms):
@@ -398,7 +434,7 @@
     return terms[0]
 
 
-def outer_gradients(layout, rank, keys, values, own, later, jobs, into, extra, hint):
+def outer_gradients(layout, rank, keys, values, own, later, jobs, into, extra, queries, query_grad):
     chunks = sorted({c for c, _ in jobs})
     fields = [a for c in chunks for a in (keys[c], values[c], *own[c][1:])]
     states = [later[c][k][0] for c, k in jobs]
@@ -407,9 +443,11 @@
 
     def body(r, *refs):
         fields_in, refs = refs[: len(fields)], refs[len(fields) :]
-        state_refs, (dk_hbm, dv_hbm, *refs) = refs[:count], refs[count:]
+        state_refs, (q_ref, dk_hbm, dv_hbm, dq_hbm, *refs) = refs[:count], refs[count:]
         gain_hbm, (dk_buffer, dv_buffer, gain_buffer, sems) = refs[: len(gain_out)], refs[len(gain_out) :]
-        copies = []
+        at = layout.columns(r, layout.members - 1, layout.chunks - 1)
+        copies = [pltpu.make_async_copy(q_ref.at[layout.members - 1], dq_hbm.at[:, at], sems.at[3, 0])]
+        copies[0].start()
         if extra:
             parts = []
             for _, n in sorted((piece, n) for n, (c, piece) in enumerate(jobs) if c == chunks[-1]):
@@ -420,15 +458,8 @@
             copies[-1].start()
         for n, ((c, piece), state) in enumerate(zip(jobs, state_refs, strict=True)):
             at, offset = layout.columns(r, piece, c), later[c][piece][1]
-            k_ref, v_ref, dki_ref, dvi_ref = fields_in[4 * chunks.index(c) : 4 * chunks.index(c) + 4]
-            sums = []
-            for heads in pairs_of(layout.count):
-                here = (piece, slice(None), span(heads))
-                block = diagonal([state[rows_of(h, offset), :] for h in heads])
-                sums.append((heads, here, dot(v_ref[here], block, (1, 1)), dot(k_ref[here], block, (1, 0))))
-            for heads, here, dk, dv in sums:
-                dk_buffer[n, :, span(heads)] = (dki_ref[here] + dk).astype(BF16)
-                dv_buffer[n, :, span(heads)] = (dvi_ref[here] + dv).astype(BF16)
+            here = 4 * chunks.index(c)
+            store_outer(layout, fields_in[here : here + 4], state, offset, piece, dk_buffer, dv_buffer, n)
             copies.append(pltpu.make_async_copy(dk_buffer.at[n], dk_hbm.at[:, at], sems.at[0, n]))
             copies.append(pltpu.make_async_copy(dv_buffer.at[n], dv_hbm.at[:, at], sems.at[1, n]))
             copies[-2].start()
@@ -437,12 +468,11 @@
             copy.wait()
 
     return layout.call(
-        "outer_gradients", body, rank, [], [*fields, *states],
-        [(layout.wide_shape(), HBM_WHOLE)] * 2 + gain_out,
-        into=[(a, n, pltpu.HBM) for n, a in enumerate(into)],
-        macs=2 * layout.size * HD, moved=4 * layout.size, hint=hint,
+        "outer_gradients", body, rank, [], [*fields, *states, queries],
+        [(layout.wide_shape(), HBM_WHOLE)] * 3 + gain_out,
+        into=[(a, n, pltpu.HBM) for n, a in enumerate(into)] + [(query_grad, 2, pltpu.HBM)],
         scratch=[pltpu.VMEM((count, layout.tokens, layout.width), BF16)] * 2
-        + [pltpu.VMEM((heads_all, HD), F32), pltpu.SemaphoreType.DMA((3, count))],
+        + [pltpu.VMEM((heads_all, HD), F32), pltpu.SemaphoreType.DMA((4, count))],
     )
 
 
@@ -592,9 +622,10 @@
     regular = dp & (dp - 1) == 0 and context & (context - 1) == 0
     steps = xor_steps("dp", dp, 1) + xor_steps("context", context, members) if regular else []
 
-    def inner_job(mark, c, part, ready=(), stream=(), hint=0):
+    def inner_job(mark, c, part, hint=0, **beside):
         result = inner_gradients(
-            layout, place, inner[c][4:], inner[c][0], k_kept[c], v_kept[c], d_mixed[c], prior[c], c, part, own[c], mark, ready, stream, hint
+            layout, place, inner[c][4:], inner[c][0], k_kept[c], v_kept[c], d_mixed[c], prior[c], c, part, own[c], mark,
+            hint=hint, **beside,
         )
         *own[c], token = result[:4]
         return [token], result[4:]
@@ -612,22 +643,20 @@
     bases, mark = [], [d_mixed[-1]]
     for c in chunks:
         _, g_c, gain_c = inner[c][:3]
-        normed[c], *gain_grad = normed_output(layout, place, mixed[c], g_c, gain_c, inv, c, gain_grad, mark, NORM_HINTS[c])
+        normed[c], *gain_grad = normed_output(layout, place, mixed[c], g_c, gain_c, inv, c, gain_grad, mark)
         mark = gain_grad
         if c == CHUNKS - 1:
-            mark, _ = inner_job(mark, *jobs.pop(0), hint=JOB_HINTS[0])
+            mark, _ = inner_job(mark, *jobs.pop(0))
             mark = gain_job(mark)
         total = group_total(layout, place, got[c], mark)
         mark = [total]
         bases.append(cross_groups(total, members, context, False))
 
-    written = []
 
     def between(c, mark):
-        nonlocal written
         if jobs:
             job = jobs.pop(0)
-            mark, written = inner_job(mark, *job, () if jobs else [*normed.items()], hint=JOB_HINTS[1 + c])
+            mark, _ = inner_job(mark, *job)
         mark = gain_job(mark)
         while c == CHUNKS - 1 and steps:
             mark = gain_job(mark)
@@ -635,16 +664,14 @@
 
     gain = (lambda: gain_grad[0]) if regular else None
     later, mark = scatter_back(layout, place, got, bases, context, False, mark, between, gain, SPREAD_HINT)
-    for c in chunks[1:]:
-        output, query_grad = written
-        mark, _ = inner_job(mark, c, (0, members), (), [query_grad], JOB_HINTS[3])
-        written = [output, own[c][0]]
-    output, query_grad = written
-    outer = []
-    for group, hint in zip((early, middle + late), OUTER_HINTS, strict=True):
-        if group:
-            extra = regular and group != early
-            *outer, total_gain = [*outer_gradients(layout, place, k_kept, v_kept, own, later, group, outer, extra, hint), None][:3]
+    also = [k_kept[0], v_kept[0], *own[0][1:], *[later[0][k][0] for k in range(far)]]
+    others = [(c, own[c][0]) for c in chunks[:-1]]
+    mark, (output, query_grad, *outer) = inner_job(
+        mark, CHUNKS - 1, (0, members), OUTER_HINT, ready=[*normed.items()], others=others, also=also if far else []
+    )
+    *outer, query_grad, total_gain = [
+        *outer_gradients(layout, place, k_kept, v_kept, own, later, middle + late, outer, regular, own[-1][0], query_grad), None
+    ][:4]
     if not regular:
         total_gain = lax.psum(gain_grad[0], ("dp", "context"))
     return output[None], query_grad[None], outer[0][None], outer[1][None], total_gain.reshape(features)

time: 87 us -> 86.3 us (level)
    pallas_call x29 -> x28, Pallas kernels: 35.6 us -> 34.9 us  [call(): pl.pallas_call(kernel, name=name, grid_spec=pltpu.PrefetchScalarGridSpec(...]
where the time goes in v4:
time: 86.3 us; the launch traced here: 86 us
  starting transfers between devices  42.5 us (49%)
  Pallas kernels  34.9 us (40%)
  waiting for transfers between devices  7.41 us (9%)
  between operations  1.14 us (1%)
    pallas_call x28, Pallas kernels, call(): pl.pallas_call(kernel, name=name, grid_spec=pltpu.PrefetchScalarGridSpec(...  34.9 us
    ppermute x25, starting transfers between devices, swap(): return lax.ppermute(array, axis, [(c, c ^ k) for c in range(size)])  32.7 us
    ppermute x4, starting transfers between devices, cross_groups(): lax.ppermute(total, 'context', up if forward else [(b, a) for a, b in up])  9.83 us
    ppermute x25, waiting for transfers between devices, swap(): return lax.ppermute(array, axis, [(c, c ^ k) for c in range(size)])  7.4 us
  transfers between devices with their start and end apart: 29, of which 7 were waited for; matrix products, arithmetic and copies ran while one was open for 0% of the time, Pallas kernels for 33%

profile of v4, /device:TPU:0, one launch (start us, length us, event | category | flops | bytes accessed | tf_op | source)
XLA Modules:
  0.0 86.0 jit_solution(9476633123704496467)
XLA Ops:
  0.6 2.4 %block_states.3 = (bf16[4,320,512]{2,1,0:T(8,128)(2,1)S(1)}, bf16[4,320,512]{2,1,0:T(8,128)(2,1)S(1)}, bf16[512,128]{1,0:T(8,128)(2,1)S(1)}, bf16[512,128]{1,0:T...) custom-call(s32[1]{0:T(128)} %bitcast.r, bf16[320,4096]{1,0:T(8,128)(2,1)} %bitcast.17, ...), custom_call_target="tpu_custom_call" | custom-call | flops 1 | bytes 1 | tf_op jit(solution)/shard_map/block_states/pallas_call | solution.py:120
  3.0 3.0 %collective-permute-start.3 = (bf16[512,128]{1,0:T(8,128)(2,1)S(1)}, bf16[512,128]{1,0:T(8,128)(2,1)S(1)}, u32[]{:S(2)}, u32[]{:S(2)}) collective-permute-start(bf16[512,128]{1,0:T(8,128)(2,1)S(1)} %get-tuple-element.103), channel_id=1, source_target_pairs={{0,1},{1,0},{2,3},{3,2},{4,5},{5,4},{6,7},{7,6},{8,9},{9,8},{10,11... | collective-permute-start | bytes 393224 | tf_op jit(solution)/shard_map/ppermute | solution.py:480
  6.0 1.6 %collective-permute-start.4 = (bf16[512,128]{1,0:T(8,128)(2,1)S(1)}, bf16[512,128]{1,0:T(8,128)(2,1)S(1)}, u32[]{:S(2)}, u32[]{:S(2)}) collective-permute-start(bf16[512,128]{1,0:T(8,128)(2,1)S(1)} %get-tuple-element.104), channel_id=1, source_target_pairs={{0,2},{1,3},{2,0},{3,1},{4,6},{5,7},{6,4},{7,5},{8,10},{9,11},{10,... | collective-permute-start | bytes 393224 | tf_op jit(solution)/shard_map/ppermute | solution.py:480
  7.6 2.4 %block_states.2 = (bf16[4,320,512]{2,1,0:T(8,128)(2,1)S(1)}, bf16[4,320,512]{2,1,0:T(8,128)(2,1)S(1)}, bf16[512,128]{1,0:T(8,128)(2,1)S(1)}, bf16[512,128]{1,0:T...) custom-call(s32[1]{0:T(128)} %bitcast.r, bf16[320,4096]{1,0:T(8,128)(2,1)} %bitcast.18, ...), custom_call_target="tpu_custom_call" | custom-call | flops 1 | bytes 1 | tf_op jit(solution)/shard_map/block_states/pallas_call | solution.py:120
  10.0 1.9 %collective-permute-start = (bf16[512,128]{1,0:T(8,128)(2,1)S(1)}, bf16[512,128]{1,0:T(8,128)(2,1)S(1)}, u32[]{:S(2)}, u32[]{:S(2)}) collective-permute-start(bf16[512,128]{1,0:T(8,128)(2,1)S(1)} %get-tuple-element.97), channel_id=1, source_target_pairs={{0,1},{1,0},{2,3},{3,2},{4,5},{5,4},{6,7},{7,6},{8,9},{9,8},{10,11... | collective-permute-start | bytes 393224 | tf_op jit(solution)/shard_map/ppermute | solution.py:480
  12.0 1.6 %collective-permute-start.1 = (bf16[512,128]{1,0:T(8,128)(2,1)S(1)}, bf16[512,128]{1,0:T(8,128)(2,1)S(1)}, u32[]{:S(2)}, u32[]{:S(2)}) collective-permute-start(bf16[512,128]{1,0:T(8,128)(2,1)S(1)} %get-tuple-element.98), channel_id=1, source_target_pairs={{0,2},{1,3},{2,0},{3,1},{4,6},{5,7},{6,4},{7,5},{8,10},{9,11},{10,... | collective-permute-start | bytes 393224 | tf_op jit(solution)/shard_map/ppermute | solution.py:480
  13.6 0.5 collective-permute-done.5.refs_3_
  14.2 4.7 %collective-permute-start.7 = (bf16[512,128]{1,0:T(8,128)(2,1)S(1)}, bf16[512,128]{1,0:T(8,128)(2,1)S(1)}, u32[]{:S(2)}, u32[]{:S(2)}) collective-permute-start(bf16[512,128]{1,0:T(8,128)(2,1)S(1)} %group_total.4.refs_5_), channel_id=1, source_target_pairs={{0,4},{1,5},{2,6},{3,7},{8,12},{9,13},{10,14},{11,15},{16,20},{17,... | collective-permute-start | bytes 393224 | tf_op jit(solution)/shard_map/ppermute | solution.py:504
  18.9 3.5 %within_block.2 = (bf16[4,320,512]{2,1,0:T(8,128)(2,1)S(1)}, bf16[4,320,512]{2,1,0:T(8,128)(2,1)S(1)}, f32[4,1,512]{2,1,0:T(1,128)S(1)}, f32[4,320,512]{2,1,0:T(...) custom-call(s32[1]{0:T(128)} %bitcast.r, bf16[320,4096]{1,0:T(8,128)(2,1)} %bitcast.13, ...), custom_call_target="tpu_custom_call" | custom-call | flops 1 | bytes 1 | tf_op jit(solution)/shard_map/within_block/pallas_call | solution.py:120
  22.5 2.3 %collective-permute-start.6 = (bf16[512,128]{1,0:T(8,128)(2,1)S(1)}, bf16[512,128]{1,0:T(8,128)(2,1)S(1)}, u32[]{:S(2)}, u32[]{:S(2)}) collective-permute-start(bf16[512,128]{1,0:T(8,128)(2,1)S(1)} %group_total.5.refs_5_), channel_id=1, source_target_pairs={{0,4},{1,5},{2,6},{3,7},{8,12},{9,13},{10,14},{11,15},{16,20},{17,... | collective-permute-start | bytes 393224 | tf_op jit(solution)/shard_map/ppermute | solution.py:504
  24.8 3.5 %within_block.3 = (bf16[4,320,512]{2,1,0:T(8,128)(2,1)S(1)}, bf16[4,320,512]{2,1,0:T(8,128)(2,1)S(1)}, f32[4,1,512]{2,1,0:T(1,128)S(1)}, f32[4,320,512]{2,1,0:T(...) custom-call(s32[1]{0:T(128)} %bitcast.r, bf16[320,4096]{1,0:T(8,128)(2,1)} %bitcast.14, ...), custom_call_target="tpu_custom_call" | custom-call | flops 1 | bytes 1 | tf_op jit(solution)/shard_map/within_block/pallas_call | solution.py:120
  28.5 1.0 %collective-permute-start.11 = (bf16[512,128]{1,0:T(8,128)(2,1)S(1)}, bf16[512,128]{1,0:T(8,128)(2,1)S(1)}, u32[]{:S(2)}, u32[]{:S(2)}) collective-permute-start(bf16[512,128]{1,0:T(8,128)(2,1)S(1)} %get-tuple-element.122), channel_id=1, source_target_pairs={{0,1},{1,0},{2,3},{3,2},{4,5},{5,4},{6,7},{7,6},{8,9},{9,8},{10,11... | collective-permute-start | bytes 393224 | tf_op jit(solution)/shard_map/ppermute | solution.py:480
  29.5 3.0 %collective-permute-start.12 = (bf16[512,128]{1,0:T(8,128)(2,1)S(1)}, bf16[512,128]{1,0:T(8,128)(2,1)S(1)}, u32[]{:S(2)}, u32[]{:S(2)}) collective-permute-start(bf16[512,128]{1,0:T(8,128)(2,1)S(1)} %get-tuple-element.123), channel_id=1, source_target_pairs={{0,2},{1,3},{2,0},{3,1},{4,6},{5,7},{6,4},{7,5},{8,10},{9,11},{10,... | collective-permute-start | bytes 393224 | tf_op jit(solution)/shard_map/ppermute | solution.py:480
  33.0 3.3 %collective-permute-start.8 = (bf16[1024,128]{1,0:T(8,128)(2,1)S(1)}, bf16[1024,128]{1,0:T(8,128)(2,1)S(1)}, u32[]{:S(2)}, u32[]{:S(2)}) collective-permute-start(bf16[1024,128]{1,0:T(8,128)(2,1)S(1)} %get-tuple-element.118), channel_id=1, source_target_pairs={{0,3},{1,2},{2,1},{3,0},{4,7},{5,6},{6,5},{7,4},{8,11},{9,10},{10,... | collective-permute-start | bytes 786440 | tf_op jit(solution)/shard_map/ppermute | solution.py:480
  36.3 0.6 collective-permute-done.12.refs_6_
  36.9 0.7 mix.3
  37.6 1.8 %collective-permute-done.9.refs_5_.refs_7_ = bf16[512,128]{1,0:T(8,128)(2,1)S(1)} collective-permute-done((bf16[512,128]{1,0:T(8,128)(2,1)S(1)}, bf16[512,128]{1,0:T(8,128)(2,1)S(1)}, u32[]{:S(2)}, u32[]{:S(2)}) %collective-permute-start.9) | collective-permute-done | bytes 131104 | tf_op jit(solution)/shard_map/ppermute | solution.py:480
  39.4 0.7 mix.4
  40.1 2.2 %collective-permute-done.8.refs_8_.refs_9_.refs_7_ = bf16[1024,128]{1,0:T(8,128)(2,1)S(1)} collective-permute-done((bf16[1024,128]{1,0:T(8,128)(2,1)S(1)}, bf16[1024,128]{1,0:T(8,128)(2,1)S(1)}, u32[]{:S(2)}, u32[]{:S(2)}) %collective-permute-start.8) | collective-permute-done | bytes 262176 | tf_op jit(solution)/shard_map/ppermute | solution.py:480
  42.3 0.5 mix.5
  42.9 1.5 %mixed_gradients.3 = (bf16[4,320,512]{2,1,0:T(8,128)(2,1)S(1)}, bf16[512,128]{1,0:T(8,128)(2,1)S(1)}, bf16[512,128]{1,0:T(8,128)(2,1)S(1)}, bf16[512,128]{1,0:T(8,128)(2,1)S(1)}, bf16[512,128]{1,0:T(8,128)(2,1)S(1)}) custom-call(s32[1]{0:T(128)} %bitcast.r, f32[4,320,512]{2,1,0:T(8,128)S(1)} %get-tuple-element.136.refs_0_, ...), custom_call_target="tpu_custom_call" | custom-call | flops 1 | bytes 1 | tf_op jit(solution)/shard_map/mixed_gradients/pallas_call | solution.py:120
  44.4 0.6 collective-permute-start.13
  45.0 1.4 %collective-permute-start.14 = (bf16[512,128]{1,0:T(8,128)(2,1)S(1)}, bf16[512,128]{1,0:T(8,128)(2,1)S(1)}, u32[]{:S(2)}, u32[]{:S(2)}) collective-permute-start(bf16[512,128]{1,0:T(8,128)(2,1)S(1)} %get-tuple-element.140), channel_id=1, source_target_pairs={{0,2},{1,3},{2,0},{3,1},{4,6},{5,7},{6,4},{7,5},{8,10},{9,11},{10,... | collective-permute-start | bytes 393224 | tf_op jit(solution)/shard_map/ppermute | solution.py:480
  46.4 1.6 %collective-permute-start.15 = (bf16[512,128]{1,0:T(8,128)(2,1)S(1)}, bf16[512,128]{1,0:T(8,128)(2,1)S(1)}, u32[]{:S(2)}, u32[]{:S(2)}) collective-permute-start(bf16[512,128]{1,0:T(8,128)(2,1)S(1)} %get-tuple-element.141), channel_id=1, source_target_pairs={{0,3},{1,2},{2,1},{3,0},{4,7},{5,6},{6,5},{7,4},{8,11},{9,10},{10,... | collective-permute-start | bytes 393224 | tf_op jit(solution)/shard_map/ppermute | solution.py:480
  47.9 1.5 %mixed_gradients.2 = (bf16[4,320,512]{2,1,0:T(8,128)(2,1)S(1)}, bf16[512,128]{1,0:T(8,128)(2,1)S(1)}, bf16[512,128]{1,0:T(8,128)(2,1)S(1)}, bf16[512,128]{1,0:T(8,128)(2,1)S(1)}, bf16[512,128]{1,0:T(8,128)(2,1)S(1)}) custom-call(s32[1]{0:T(128)} %bitcast.r, f32[4,320,512]{2,1,0:T(8,128)S(1)} %get-tuple-element.130.refs_0_, ...), custom_call_target="tpu_custom_call" | custom-call | flops 1 | bytes 1 | tf_op jit(solution)/shard_map/mixed_gradients/pallas_call | solution.py:120
  49.5 0.6 collective-permute-start.19
  50.0 1.4 %collective-permute-start.20 = (bf16[512,128]{1,0:T(8,128)(2,1)S(1)}, bf16[512,128]{1,0:T(8,128)(2,1)S(1)}, u32[]{:S(2)}, u32[]{:S(2)}) collective-permute-start(bf16[512,128]{1,0:T(8,128)(2,1)S(1)} %get-tuple-element.151), channel_id=1, source_target_pairs={{0,2},{1,3},{2,0},{3,1},{4,6},{5,7},{6,4},{7,5},{8,10},{9,11},{10,... | collective-permute-start | bytes 393224 | tf_op jit(solution)/shard_map/ppermute | solution.py:480
  51.5 1.6 %collective-permute-start.21 = (bf16[512,128]{1,0:T(8,128)(2,1)S(1)}, bf16[512,128]{1,0:T(8,128)(2,1)S(1)}, u32[]{:S(2)}, u32[]{:S(2)}) collective-permute-start(bf16[512,128]{1,0:T(8,128)(2,1)S(1)} %get-tuple-element.152), channel_id=1, source_target_pairs={{0,3},{1,2},{2,1},{3,0},{4,7},{5,6},{6,5},{7,4},{8,11},{9,10},{10,... | collective-permute-start | bytes 393224 | tf_op jit(solution)/shard_map/ppermute | solution.py:480
  53.0 0.9 %normed_output.2 = (bf16[4,320,512]{2,1,0:T(8,128)(2,1)S(1)}, f32[32,128]{1,0:T(8,128)S(1)}) custom-call(s32[1]{0:T(128)} %bitcast.r, f32[4,320,512]{2,1,0:T(8,128)S(1)} %get-tuple-element.136.refs_0_, bf16[4,320,512]{2,1,0:T(8,128)(2,1)S(1)} %get-tuple-element.111.refs_2_.refs_1_, f32[4,1,512]{2,1,0:T(1,128)S(1)} %get-tuple-element.112.refs_3_.refs_2_, ...), custom_call_target="tpu_custom_call" | custom-call | flops 1 | bytes 1 | tf_op jit(solution)/shard_map/normed_output/pallas_call | solution.py:120
  54.0 1.3 %collective-permute-start.16 = (bf16[512,128]{1,0:T(8,128)(2,1)S(1)}, bf16[512,128]{1,0:T(8,128)(2,1)S(1)}, u32[]{:S(2)}, u32[]{:S(2)}) collective-permute-start(bf16[512,128]{1,0:T(8,128)(2,1)S(1)} %group_total.6.refs_4_), channel_id=1, source_target_pairs={{4,0},{5,1},{6,2},{7,3},{12,8},{13,9},{14,10},{15,11},{20,16},{21,... | collective-permute-start | bytes 393224 | tf_op jit(solution)/shard_map/ppermute | solution.py:504
  55.3 1.0 %normed_output.3 = (bf16[4,320,512]{2,1,0:T(8,128)(2,1)S(1)}, f32[32,128]{1,0:T(8,128)S(1)}) custom-call(s32[1]{0:T(128)} %bitcast.r, f32[4,320,512]{2,1,0:T(8,128)S(1)} %get-tuple-element.130.refs_0_, bf16[4,320,512]{2,1,0:T(8,128)(2,1)S(1)} %get-tuple-element.114.refs_2_.refs_6_.refs_1_, ...), custom_call_target="tpu_custom_call", output_to_operand_aliasing={{1}: (6, {})} | custom-call | flops 1 | bytes 1 | tf_op jit(solution)/shard_map/normed_output/pallas_call | solution.py:120
  56.4 1.5 %inner_gradients.4 = (bf16[4,320,512]{2,1,0:T(8,128)(2,1)S(1)}, f32[4,320,512]{2,1,0:T(8,128)S(1)}, f32[4,320,512]{2,1,0:T(8,128)S(1)}, f32[8,128]{1,0:T(8,128)S(1)}) custom-call(s32[1]{0:T(128)} %bitcast.r, bf16[4,4,320,256]{3,2,1,0:T(8,128)(2,1)S(1)} %get-tuple-element.144.refs_0_, bf16[4,4,64,64]{3,2,1,0:T(8,128)(2,1)S(1)} %get-tuple-element.145.refs_1_, ...), custom_call_target="tpu_custom_call" | custom-call | flops 1 | bytes 1 | tf_op jit(solution)/shard_map/inner_gradients/pallas_call | solution.py:120
  57.9 0.8 collective-permute-done.21.refs_3_
  58.8 1.5 %collective-permute-start.24 = (bf16[512,128]{1,0:T(8,128)(2,1)S(1)}, bf16[512,128]{1,0:T(8,128)(2,1)S(1)}, u32[]{:S(2)}, u32[]{:S(2)}) collective-permute-start(bf16[512,128]{1,0:T(8,128)(2,1)S(1)} %group_total.7.refs_7_), channel_id=1, source_target_pairs={{4,0},{5,1},{6,2},{7,3},{12,8},{13,9},{14,10},{15,11},{20,16},{21,... | collective-permute-start | bytes 393224 | tf_op jit(solution)/shard_map/ppermute | solution.py:504
  60.4 1.6 %collective-permute-start.18 = (f32[32,128]{1,0:T(8,128)S(1)}, f32[32,128]{1,0:T(8,128)S(1)}, u32[]{:S(2)}, u32[]{:S(2)}) collective-permute-start(f32[32,128]{1,0:T(8,128)S(1)} %gain_sum.3.refs_4_.refs_0_), channel_id=1, source_target_pairs={{0,16},{8,24},{16,0},{24,8},{1,17},{9,25},{17,1},{25,9},{2,18},{10... | collective-permute-start | bytes 49160 | tf_op jit(solution)/shard_map/ppermute | solution.py:480
  61.9 1.5 %inner_gradients.5 = (bf16[4,320,512]{2,1,0:T(8,128)(2,1)S(1)}, f32[4,320,512]{2,1,0:T(8,128)S(1)}, f32[4,320,512]{2,1,0:T(8,128)S(1)}, f32[8,128]{1,0:T(8,128)S(1)}) custom-call(s32[1]{0:T(128)} %bitcast.r, bf16[4,4,320,256]{3,2,1,0:T(8,128)(2,1)S(1)} %get-tuple-element.144.refs_0_, ...), custom_call_target="tpu_custom_call", output_to_operand_aliasing={{0}: (9, {}), {1}: (10, {}), {2}: (11, {})} | custom-call | flops 1 | bytes 1 | tf_op jit(solution)/shard_map/inner_gradients/pallas_call | solution.py:120
  63.4 0.8 collective-permute-done.18.refs_1_
  64.2 0.3 spread.6
  64.5 0.6 collective-permute-start.22
  65.0 0.6 collective-permute-start.23
  65.6 3.5 %collective-permute-start.25 = (f32[32,128]{1,0:T(8,128)S(1)}, f32[32,128]{1,0:T(8,128)S(1)}, u32[]{:S(2)}, u32[]{:S(2)}) collective-permute-start(f32[32,128]{1,0:T(8,128)S(1)} %gain_sum.4.refs_5_.refs_0_), channel_id=1, source_target_pairs={{0,4},{1,5},{2,6},{3,7},{4,0},{5,1},{6,2},{7,3},{8,12},{9,13},{10,... | collective-permute-start | bytes 49160 | tf_op jit(solution)/shard_map/ppermute | solution.py:480
  69.2 2.8 %inner_gradients.6 = (bf16[4,320,512]{2,1,0:T(8,128)(2,1)S(1)}, f32[4,320,512]{2,1,0:T(8,128)S(1)}, f32[4,320,512]{2,1,0:T(8,128)S(1)}, f32[8,128]{1,0:T(8,128)S(1)}) custom-call(s32[1]{0:T(128)} %bitcast.r, bf16[4,4,320,256]{3,2,1,0:T(8,128)(2,1)S(1)} %get-tuple-element.144.refs_0_, ...), custom_call_target="tpu_custom_call", output_to_operand_aliasing={{0}: (10, {}), {1}: (11, {}), {2}: (12, {})} | custom-call | flops 1 | bytes 1 | tf_op jit(solution)/shard_map/inner_gradients/pallas_call | solution.py:120
  72.0 0.3 spread.7
  72.3 2.8 %collective-permute-start.28 = (bf16[1088,128]{1,0:T(8,128)(2,1)S(1)}, bf16[1088,128]{1,0:T(8,128)(2,1)S(1)}, u32[]{:S(2)}, u32[]{:S(2)}) collective-permute-start(bf16[1088,128]{1,0:T(8,128)(2,1)S(1)} %get-tuple-element.174), channel_id=1, source_target_pairs={{0,3},{1,2},{2,1},{3,0},{4,7},{5,6},{6,5},{7,4},{8,11},{9,10},{10,... | collective-permute-start | bytes 835592 | tf_op jit(solution)/shard_map/ppermute | solution.py:480
  75.0 0.5 collective-permute-start.26
  75.8 7.1 %inner_gradients.7 = (bf16[4,320,512]{2,1,0:T(8,128)(2,1)S(1)}, f32[4,320,512]{2,1,0:T(8,128)S(1)}, f32[4,320,512]{2,1,0:T(8,128)S(1)}, f32[8,128]{1,0:T(8,128)}...) custom-call(s32[1]{0:T(128)} %bitcast.r, ...), custom_call_target="tpu_custom_call" | custom-call | flops 2000000000 | bytes 7200001 | tf_op jit(solution)/shard_map/inner_gradients/pallas_call | solution.py:120
  82.9 0.7 collective-permute-done.26.refs_9_
  83.6 2.2 %outer_gradients.1 = (bf16[320,4096]{1,0:T(8,128)(2,1)}, bf16[320,4096]{1,0:T(8,128)(2,1)}, bf16[320,4096]{1,0:T(8,128)(2,1)}, f32[32,128]{1,0:T(8,128)}) custom-call(s32[1]{0:T(128)} %bitcast.r, bf16[4,320,512]{2,1,0:T(8,128)(2,1)S(1)} %get-tuple-element.100.refs_3_.refs_13_.refs_0_, ...), custom_call_target="tpu_custom_call", output_to_operand_aliasing={{0}: (15, {}), {1}: (16, {}), {2}: (17, {})} | custom-call | flops 1 | bytes 1 | tf_op jit(solution)/shard_map/outer_gradients/pallas_call | solution.py:120
  (40 shorter events, 1.6 us)
Async XLA Ops:
  3.0 10.6 %collective-permute-start.3 = (bf16[512,128]{1,0:T(8,128)(2,1)S(1)}, bf16[512,128]{1,0:T(8,128)(2,1)S(1)}, u32[]{:S(2)}, u32[]{:S(2)}) collective-permute-start(bf16[512,128]{1,0:T(8,128)(2,1)S(1)} %get-tuple-element.103), channel_id=1, source_target_pairs={{0,1},{1,0},{2,3},{3,2},{4,5},{5,4},{6,7},{7,6},{8,9},{9,8},{10,11... | collective-permute-start | bytes 393224 | tf_op jit(solution)/shard_map/ppermute | solution.py:480
  6.0 7.6 %collective-permute-start.4 = (bf16[512,128]{1,0:T(8,128)(2,1)S(1)}, bf16[512,128]{1,0:T(8,128)(2,1)S(1)}, u32[]{:S(2)}, u32[]{:S(2)}) collective-permute-start(bf16[512,128]{1,0:T(8,128)(2,1)S(1)} %get-tuple-element.104), channel_id=1, source_target_pairs={{0,2},{1,3},{2,0},{3,1},{4,6},{5,7},{6,4},{7,5},{8,10},{9,11},{10,... | collective-permute-start | bytes 393224 | tf_op jit(solution)/shard_map/ppermute | solution.py:480
  7.6 11.3 %copy-start = (f32[4096]{0:T(1024)S(1)}, f32[4096]{0:T(1024)}, u32[]{:S(2)}) copy-start(f32[4096]{0:T(1024)} %param.8) | copy-start | bytes 49156
  7.6 6.4 %collective-permute-start.5 = (bf16[512,128]{1,0:T(8,128)(2,1)S(1)}, bf16[512,128]{1,0:T(8,128)(2,1)S(1)}, u32[]{:S(2)}, u32[]{:S(2)}) collective-permute-start(bf16[512,128]{1,0:T(8,128)(2,1)S(1)} %get-tuple-element.105), channel_id=1, source_target_pairs={{0,3},{1,2},{2,1},{3,0},{4,7},{5,6},{6,5},{7,4},{8,11},{9,10},{10,... | collective-permute-start | bytes 393224 | tf_op jit(solution)/shard_map/ppermute | solution.py:480
  10.0 12.3 %collective-permute-start = (bf16[512,128]{1,0:T(8,128)(2,1)S(1)}, bf16[512,128]{1,0:T(8,128)(2,1)S(1)}, u32[]{:S(2)}, u32[]{:S(2)}) collective-permute-start(bf16[512,128]{1,0:T(8,128)(2,1)S(1)} %get-tuple-element.97), channel_id=1, source_target_pairs={{0,1},{1,0},{2,3},{3,2},{4,5},{5,4},{6,7},{7,6},{8,9},{9,8},{10,11... | collective-permute-start | bytes 393224 | tf_op jit(solution)/shard_map/ppermute | solution.py:480
  12.0 10.4 %collective-permute-start.1 = (bf16[512,128]{1,0:T(8,128)(2,1)S(1)}, bf16[512,128]{1,0:T(8,128)(2,1)S(1)}, u32[]{:S(2)}, u32[]{:S(2)}) collective-permute-start(bf16[512,128]{1,0:T(8,128)(2,1)S(1)} %get-tuple-element.98), channel_id=1, source_target_pairs={{0,2},{1,3},{2,0},{3,1},{4,6},{5,7},{6,4},{7,5},{8,10},{9,11},{10,... | collective-permute-start | bytes 393224 | tf_op jit(solution)/shard_map/ppermute | solution.py:480
  13.6 8.8 %collective-permute-start.2 = (bf16[512,128]{1,0:T(8,128)(2,1)S(1)}, bf16[512,128]{1,0:T(8,128)(2,1)S(1)}, u32[]{:S(2)}, u32[]{:S(2)}) collective-permute-start(bf16[512,128]{1,0:T(8,128)(2,1)S(1)} %get-tuple-element.99), channel_id=1, source_target_pairs={{0,3},{1,2},{2,1},{3,0},{4,7},{5,6},{6,5},{7,4},{8,11},{9,10},{10,... | collective-permute-start | bytes 393224 | tf_op jit(solution)/shard_map/ppermute | solution.py:480
  14.2 14.1 %collective-permute-start.7 = (bf16[512,128]{1,0:T(8,128)(2,1)S(1)}, bf16[512,128]{1,0:T(8,128)(2,1)S(1)}, u32[]{:S(2)}, u32[]{:S(2)}) collective-permute-start(bf16[512,128]{1,0:T(8,128)(2,1)S(1)} %group_total.4.refs_5_), channel_id=1, source_target_pairs={{0,4},{1,5},{2,6},{3,7},{8,12},{9,13},{10,14},{11,15},{16,20},{17,... | collective-permute-start | bytes 393224 | tf_op jit(solution)/shard_map/ppermute | solution.py:504
  22.5 10.0 %collective-permute-start.6 = (bf16[512,128]{1,0:T(8,128)(2,1)S(1)}, bf16[512,128]{1,0:T(8,128)(2,1)S(1)}, u32[]{:S(2)}, u32[]{:S(2)}) collective-permute-start(bf16[512,128]{1,0:T(8,128)(2,1)S(1)} %group_total.5.refs_5_), channel_id=1, source_target_pairs={{0,4},{1,5},{2,6},{3,7},{8,12},{9,13},{10,14},{11,15},{16,20},{17,... | collective-permute-start | bytes 393224 | tf_op jit(solution)/shard_map/ppermute | solution.py:504
  28.5 7.8 %collective-permute-start.11 = (bf16[512,128]{1,0:T(8,128)(2,1)S(1)}, bf16[512,128]{1,0:T(8,128)(2,1)S(1)}, u32[]{:S(2)}, u32[]{:S(2)}) collective-permute-start(bf16[512,128]{1,0:T(8,128)(2,1)S(1)} %get-tuple-element.122), channel_id=1, source_target_pairs={{0,1},{1,0},{2,3},{3,2},{4,5},{5,4},{6,7},{7,6},{8,9},{9,8},{10,11... | collective-permute-start | bytes 393224 | tf_op jit(solution)/shard_map/ppermute | solution.py:480
  29.5 7.4 %collective-permute-start.12 = (bf16[512,128]{1,0:T(8,128)(2,1)S(1)}, bf16[512,128]{1,0:T(8,128)(2,1)S(1)}, u32[]{:S(2)}, u32[]{:S(2)}) collective-permute-start(bf16[512,128]{1,0:T(8,128)(2,1)S(1)} %get-tuple-element.123), channel_id=1, source_target_pairs={{0,2},{1,3},{2,0},{3,1},{4,6},{5,7},{6,4},{7,5},{8,10},{9,11},{10,... | collective-permute-start | bytes 393224 | tf_op jit(solution)/shard_map/ppermute | solution.py:480
  32.8 6.6 %collective-permute-start.9 = (bf16[512,128]{1,0:T(8,128)(2,1)S(1)}, bf16[512,128]{1,0:T(8,128)(2,1)S(1)}, u32[]{:S(2)}, u32[]{:S(2)}) collective-permute-start(bf16[512,128]{1,0:T(8,128)(2,1)S(1)} %get-tuple-element.120), channel_id=1, source_target_pairs={{0,1},{1,0},{2,3},{3,2},{4,5},{5,4},{6,7},{7,6},{8,9},{9,8},{10,11... | collective-permute-start | bytes 393224 | tf_op jit(solution)/shard_map/ppermute | solution.py:480
  32.9 6.5 %collective-permute-start.10 = (bf16[512,128]{1,0:T(8,128)(2,1)S(1)}, bf16[512,128]{1,0:T(8,128)(2,1)S(1)}, u32[]{:S(2)}, u32[]{:S(2)}) collective-permute-start(bf16[512,128]{1,0:T(8,128)(2,1)S(1)} %get-tuple-element.121), channel_id=1, source_target_pairs={{0,2},{1,3},{2,0},{3,1},{4,6},{5,7},{6,4},{7,5},{8,10},{9,11},{10,... | collective-permute-start | bytes 393224 | tf_op jit(solution)/shard_map/ppermute | solution.py:480
  33.0 9.3 %collective-permute-start.8 = (bf16[1024,128]{1,0:T(8,128)(2,1)S(1)}, bf16[1024,128]{1,0:T(8,128)(2,1)S(1)}, u32[]{:S(2)}, u32[]{:S(2)}) collective-permute-start(bf16[1024,128]{1,0:T(8,128)(2,1)S(1)} %get-tuple-element.118), channel_id=1, source_target_pairs={{0,3},{1,2},{2,1},{3,0},{4,7},{5,6},{6,5},{7,4},{8,11},{9,10},{10,... | collective-permute-start | bytes 786440 | tf_op jit(solution)/shard_map/ppermute | solution.py:480
  44.4 7.1 %collective-permute-start.13 = (bf16[512,128]{1,0:T(8,128)(2,1)S(1)}, bf16[512,128]{1,0:T(8,128)(2,1)S(1)}, u32[]{:S(2)}, u32[]{:S(2)}) collective-permute-start(bf16[512,128]{1,0:T(8,128)(2,1)S(1)} %get-tuple-element.139), channel_id=1, source_target_pairs={{0,1},{1,0},{2,3},{3,2},{4,5},{5,4},{6,7},{7,6},{8,9},{9,8},{10,11... | collective-permute-start | bytes 393224 | tf_op jit(solution)/shard_map/ppermute | solution.py:480
  45.0 9.0 %collective-permute-start.14 = (bf16[512,128]{1,0:T(8,128)(2,1)S(1)}, bf16[512,128]{1,0:T(8,128)(2,1)S(1)}, u32[]{:S(2)}, u32[]{:S(2)}) collective-permute-start(bf16[512,128]{1,0:T(8,128)(2,1)S(1)} %get-tuple-element.140), channel_id=1, source_target_pairs={{0,2},{1,3},{2,0},{3,1},{4,6},{5,7},{6,4},{7,5},{8,10},{9,11},{10,... | collective-permute-start | bytes 393224 | tf_op jit(solution)/shard_map/ppermute | solution.py:480
  46.4 7.6 %collective-permute-start.15 = (bf16[512,128]{1,0:T(8,128)(2,1)S(1)}, bf16[512,128]{1,0:T(8,128)(2,1)S(1)}, u32[]{:S(2)}, u32[]{:S(2)}) collective-permute-start(bf16[512,128]{1,0:T(8,128)(2,1)S(1)} %get-tuple-element.141), channel_id=1, source_target_pairs={{0,3},{1,2},{2,1},{3,0},{4,7},{5,6},{6,5},{7,4},{8,11},{9,10},{10,... | collective-permute-start | bytes 393224 | tf_op jit(solution)/shard_map/ppermute | solution.py:480
  49.5 8.4 %collective-permute-start.19 = (bf16[512,128]{1,0:T(8,128)(2,1)S(1)}, bf16[512,128]{1,0:T(8,128)(2,1)S(1)}, u32[]{:S(2)}, u32[]{:S(2)}) collective-permute-start(bf16[512,128]{1,0:T(8,128)(2,1)S(1)} %get-tuple-element.150), channel_id=1, source_target_pairs={{0,1},{1,0},{2,3},{3,2},{4,5},{5,4},{6,7},{7,6},{8,9},{9,8},{10,11... | collective-permute-start | bytes 393224 | tf_op jit(solution)/shard_map/ppermute | solution.py:480
  50.0 7.9 %collective-permute-start.20 = (bf16[512,128]{1,0:T(8,128)(2,1)S(1)}, bf16[512,128]{1,0:T(8,128)(2,1)S(1)}, u32[]{:S(2)}, u32[]{:S(2)}) collective-permute-start(bf16[512,128]{1,0:T(8,128)(2,1)S(1)} %get-tuple-element.151), channel_id=1, source_target_pairs={{0,2},{1,3},{2,0},{3,1},{4,6},{5,7},{6,4},{7,5},{8,10},{9,11},{10,... | collective-permute-start | bytes 393224 | tf_op jit(solution)/shard_map/ppermute | solution.py:480
  51.5 7.3 %collective-permute-start.21 = (bf16[512,128]{1,0:T(8,128)(2,1)S(1)}, bf16[512,128]{1,0:T(8,128)(2,1)S(1)}, u32[]{:S(2)}, u32[]{:S(2)}) collective-permute-start(bf16[512,128]{1,0:T(8,128)(2,1)S(1)} %get-tuple-element.152), channel_id=1, source_target_pairs={{0,3},{1,2},{2,1},{3,0},{4,7},{5,6},{6,5},{7,4},{8,11},{9,10},{10,... | collective-permute-start | bytes 393224 | tf_op jit(solution)/shard_map/ppermute | solution.py:480
  54.0 10.1 %collective-permute-start.16 = (bf16[512,128]{1,0:T(8,128)(2,1)S(1)}, bf16[512,128]{1,0:T(8,128)(2,1)S(1)}, u32[]{:S(2)}, u32[]{:S(2)}) collective-permute-start(bf16[512,128]{1,0:T(8,128)(2,1)S(1)} %group_total.6.refs_4_), channel_id=1, source_target_pairs={{4,0},{5,1},{6,2},{7,3},{12,8},{13,9},{14,10},{15,11},{20,16},{21,... | collective-permute-start | bytes 393224 | tf_op jit(solution)/shard_map/ppermute | solution.py:504
  56.3 1.6 %collective-permute-start.17 = (f32[32,128]{1,0:T(8,128)S(1)}, f32[32,128]{1,0:T(8,128)S(1)}, u32[]{:S(2)}, u32[]{:S(2)}) collective-permute-start(f32[32,128]{1,0:T(8,128)S(1)} %get-tuple-element.147.refs_7_.refs_0_), channel_id=1, source_target_pairs={{0,8},{8,0},{16,24},{24,16},{1,9},{9,1},{17,25},{25,17},{2,10},{10... | collective-permute-start | bytes 49160 | tf_op jit(solution)/shard_map/ppermute | solution.py:480
  58.8 13.1 %collective-permute-start.24 = (bf16[512,128]{1,0:T(8,128)(2,1)S(1)}, bf16[512,128]{1,0:T(8,128)(2,1)S(1)}, u32[]{:S(2)}, u32[]{:S(2)}) collective-permute-start(bf16[512,128]{1,0:T(8,128)(2,1)S(1)} %group_total.7.refs_7_), channel_id=1, source_target_pairs={{4,0},{5,1},{6,2},{7,3},{12,8},{13,9},{14,10},{15,11},{20,16},{21,... | collective-permute-start | bytes 393224 | tf_op jit(solution)/shard_map/ppermute | solution.py:504
  60.4 3.8 %collective-permute-start.18 = (f32[32,128]{1,0:T(8,128)S(1)}, f32[32,128]{1,0:T(8,128)S(1)}, u32[]{:S(2)}, u32[]{:S(2)}) collective-permute-start(f32[32,128]{1,0:T(8,128)S(1)} %gain_sum.3.refs_4_.refs_0_), channel_id=1, source_target_pairs={{0,16},{8,24},{16,0},{24,8},{1,17},{9,25},{17,1},{25,9},{2,18},{10... | collective-permute-start | bytes 49160 | tf_op jit(solution)/shard_map/ppermute | solution.py:480
  64.5 11.4 %collective-permute-start.22 = (bf16[512,128]{1,0:T(8,128)(2,1)S(1)}, bf16[512,128]{1,0:T(8,128)(2,1)S(1)}, u32[]{:S(2)}, u32[]{:S(2)}) collective-permute-start(bf16[512,128]{1,0:T(8,128)(2,1)S(1)} %get-tuple-element.164), channel_id=1, source_target_pairs={{0,1},{1,0},{2,3},{3,2},{4,5},{5,4},{6,7},{7,6},{8,9},{9,8},{10,11... | collective-permute-start | bytes 393224 | tf_op jit(solution)/shard_map/ppermute | solution.py:480
  65.0 10.8 %collective-permute-start.23 = (bf16[512,128]{1,0:T(8,128)(2,1)S(1)}, bf16[512,128]{1,0:T(8,128)(2,1)S(1)}, u32[]{:S(2)}, u32[]{:S(2)}) collective-permute-start(bf16[512,128]{1,0:T(8,128)(2,1)S(1)} %get-tuple-element.165), channel_id=1, source_target_pairs={{0,2},{1,3},{2,0},{3,1},{4,6},{5,7},{6,4},{7,5},{8,10},{9,11},{10,... | collective-permute-start | bytes 393224 | tf_op jit(solution)/shard_map/ppermute | solution.py:480
  65.6 6.3 %collective-permute-start.25 = (f32[32,128]{1,0:T(8,128)S(1)}, f32[32,128]{1,0:T(8,128)S(1)}, u32[]{:S(2)}, u32[]{:S(2)}) collective-permute-start(f32[32,128]{1,0:T(8,128)S(1)} %gain_sum.4.refs_5_.refs_0_), channel_id=1, source_target_pairs={{0,4},{1,5},{2,6},{3,7},{4,0},{5,1},{6,2},{7,3},{8,12},{9,13},{10,... | collective-permute-start | bytes 49160 | tf_op jit(solution)/shard_map/ppermute | solution.py:480
  72.3 11.4 %collective-permute-start.28 = (bf16[1088,128]{1,0:T(8,128)(2,1)S(1)}, bf16[1088,128]{1,0:T(8,128)(2,1)S(1)}, u32[]{:S(2)}, u32[]{:S(2)}) collective-permute-start(bf16[1088,128]{1,0:T(8,128)(2,1)S(1)} %get-tuple-element.174), channel_id=1, source_target_pairs={{0,3},{1,2},{2,1},{3,0},{4,7},{5,6},{6,5},{7,4},{8,11},{9,10},{10,... | collective-permute-start | bytes 835592 | tf_op jit(solution)/shard_map/ppermute | solution.py:480
  75.0 8.6 %collective-permute-start.26 = (bf16[576,128]{1,0:T(8,128)(2,1)S(1)}, bf16[576,128]{1,0:T(8,128)(2,1)S(1)}, u32[]{:S(2)}, u32[]{:S(2)}) collective-permute-start(bf16[576,128]{1,0:T(8,128)(2,1)S(1)} %get-tuple-element.172), channel_id=1, source_target_pairs={{0,1},{1,0},{2,3},{3,2},{4,5},{5,4},{6,7},{7,6},{8,9},{9,8},{10,11... | collective-permute-start | bytes 442376 | tf_op jit(solution)/shard_map/ppermute | solution.py:480
  75.5 8.1 %collective-permute-start.27 = (bf16[576,128]{1,0:T(8,128)(2,1)S(1)}, bf16[576,128]{1,0:T(8,128)(2,1)S(1)}, u32[]{:S(2)}, u32[]{:S(2)}) collective-permute-start(bf16[576,128]{1,0:T(8,128)(2,1)S(1)} %get-tuple-element.173), channel_id=1, source_target_pairs={{0,2},{1,3},{2,0},{3,1},{4,6},{5,7},{6,4},{7,5},{8,10},{9,11},{10,... | collective-permute-start | bytes 442376 | tf_op jit(solution)/shard_map/ppermute | solution.py:480

commit v5 on v4

--- a/solution.py
+++ b/solution.py
@@ -12,7 +12,7 @@
 BF16 = jnp.bfloat16
 F32 = jnp.float32
 CHUNKS = 2
-MIX_HINTS = (10, 10, 10)
+MIX_HINTS = (2, 1, 0)
 OUTER_HINT = 2
 SPREAD_HINT = 0
 VMEM_LIMIT = 14 * 1024 * 1024
@@ -234,7 +234,7 @@
     )
 
 
-def mix(layout, rank, kept, prior, jobs, mixed, sums, hint):
+def mix(layout, rank, kept, prior, jobs, mixed, sums, final, hint):
     chunks = sorted({c for c, _ in jobs})
     fields = [kept[c][n] for c in chunks for n in (3, 0, 1, 2)]
     states = [prior[c][k][0] for c, k in jobs]
@@ -260,6 +260,11 @@
                 m_refs[n][at] = value
                 square = square + value * value
                 cross = cross + gain_ref[piece, :, lanes(h)] * g_ref[at].astype(F32) * value
+        if final:
+            inv = lax.rsqrt(jnp.sum(square, -1, keepdims=True) / layout.features + EPSILON)
+            centered = jnp.sum(cross, -1, keepdims=True) / layout.features
+            square = jnp.broadcast_to(inv, square.shape)
+            cross = jnp.broadcast_to(inv * inv * inv * centered, cross.shape)
         square_ref[...] = square
         cross_ref[...] = cross
 
@@ -269,19 +274,6 @@
         into=[(a, n, pltpu.VMEM) for n, a in old], hint=hint,
     )
     return {**mixed, **dict(zip(chunks, outs, strict=True))}, [square, cross]
-
-
-def norm_factors(layout, rank, square, cross):
-    def body(r, square_ref, cross_ref, inv_ref, factor_ref):
-        mean = jnp.sum(square_ref[...], -1, keepdims=True) / layout.features
-        inv = lax.rsqrt(mean + EPSILON)
-        centered = jnp.sum(cross_ref[...], -1, keepdims=True) / layout.features
-        inv_ref[...] = jnp.broadcast_to(inv, inv_ref.shape)
-        factor_ref[...] = jnp.broadcast_to(inv * inv * inv * centered, factor_ref.shape)
-
-    return layout.call(
-        "norm_factors", body, rank, [], [square, cross], [(layout.narrow(), None)] * 2, moved=layout.tokens * HD * 4
-    )
 
 
 def mixed_gradients(layout, rank, mixed, queries, out_grad, gain, inv, factor):
@@ -603,13 +595,13 @@
     prior, mark = scatter_back(layout, place, got, bases, context, True, mark, lambda c, mark: mark)
     far = members - 1
     early = [(c, k) for c in chunks[:-1] for k in range(far)]
-    middle = [(CHUNKS - 1, k) for k in range(far)]
-    late = [(c, far) for c in chunks]
+    middle = [(CHUNKS - 1, k) for k in range(far)] or [(c, 0) for c in chunks]
+    late = [(c, far) for c in chunks] if far else []
     mixed, sums = {}, []
-    for group, hint in zip((early, middle, late), MIX_HINTS, strict=True):
+    for group, hint in zip((early, late, middle), MIX_HINTS, strict=True):
         if group:
-            mixed, sums = mix(layout, place, inner, prior, group, mixed, sums, hint)
-    inv, factor = norm_factors(layout, place, *sums)
+            mixed, sums = mix(layout, place, inner, prior, group, mixed, sums, group == middle, hint)
+    inv, factor = sums
 
     d_mixed, got = [], []
     for c in chunks:

time: 86.3 us -> 86.1 us (level)
    pallas_call x28 -> x27, Pallas kernels: 34.9 us -> 34.9 us  [call(): pl.pallas_call(kernel, name=name, grid_spec=pltpu.PrefetchScalarGridSpec(...]
  transfers between devices with their start and end apart: 29 -> 29, of which waited for: 7 -> 8; matrix products, arithmetic and copies ran while one was open for 0% -> 0% of each run, Pallas kernels for 33% -> 33%
where the time goes in v5:
time: 86.1 us; the launch traced here: 85.8 us
  starting transfers between devices  42.5 us (49%)
  Pallas kernels  34.9 us (41%)
  waiting for transfers between devices  7.26 us (8%)
  between operations  1.13 us (1%)
    pallas_call x27, Pallas kernels, call(): pl.pallas_call(kernel, name=name, grid_spec=pltpu.PrefetchScalarGridSpec(...  34.9 us
    ppermute x25, starting transfers between devices, swap(): return lax.ppermute(array, axis, [(c, c ^ k) for c in range(size)])  32.7 us
    ppermute x4, starting transfers between devices, cross_groups(): lax.ppermute(total, 'context', up if forward else [(b, a) for a, b in up])  9.83 us
    ppermute x25, waiting for transfers between devices, swap(): return lax.ppermute(array, axis, [(c, c ^ k) for c in range(size)])  7.25 us
  transfers between devices with their start and end apart: 29, of which 8 were waited for; matrix products, arithmetic and copies ran while one was open for 0% of the time, Pallas kernels for 33%

profile of v5, /device:TPU:0, one launch (start us, length us, event | category | flops | bytes accessed | tf_op | source)
XLA Modules:
  0.0 85.8 jit_solution(5045476909596376025)
XLA Ops:
  0.6 2.4 %block_states.3 = (bf16[4,320,512]{2,1,0:T(8,128)(2,1)S(1)}, bf16[4,320,512]{2,1,0:T(8,128)(2,1)S(1)}, bf16[512,128]{1,0:T(8,128)(2,1)S(1)}, bf16[512,128]{1,0:T...) custom-call(s32[1]{0:T(128)} %bitcast.r, bf16[320,4096]{1,0:T(8,128)(2,1)} %bitcast.17, ...), custom_call_target="tpu_custom_call" | custom-call | flops 1 | bytes 1 | tf_op jit(solution)/shard_map/block_states/pallas_call | solution.py:120
  3.0 3.0 %collective-permute-start.3 = (bf16[512,128]{1,0:T(8,128)(2,1)S(1)}, bf16[512,128]{1,0:T(8,128)(2,1)S(1)}, u32[]{:S(2)}, u32[]{:S(2)}) collective-permute-start(bf16[512,128]{1,0:T(8,128)(2,1)S(1)} %get-tuple-element.101), channel_id=1, source_target_pairs={{0,1},{1,0},{2,3},{3,2},{4,5},{5,4},{6,7},{7,6},{8,9},{9,8},{10,11... | collective-permute-start | bytes 393224 | tf_op jit(solution)/shard_map/ppermute | solution.py:472
  6.0 1.6 %collective-permute-start.4 = (bf16[512,128]{1,0:T(8,128)(2,1)S(1)}, bf16[512,128]{1,0:T(8,128)(2,1)S(1)}, u32[]{:S(2)}, u32[]{:S(2)}) collective-permute-start(bf16[512,128]{1,0:T(8,128)(2,1)S(1)} %get-tuple-element.102), channel_id=1, source_target_pairs={{0,2},{1,3},{2,0},{3,1},{4,6},{5,7},{6,4},{7,5},{8,10},{9,11},{10,... | collective-permute-start | bytes 393224 | tf_op jit(solution)/shard_map/ppermute | solution.py:472
  7.6 2.4 %block_states.2 = (bf16[4,320,512]{2,1,0:T(8,128)(2,1)S(1)}, bf16[4,320,512]{2,1,0:T(8,128)(2,1)S(1)}, bf16[512,128]{1,0:T(8,128)(2,1)S(1)}, bf16[512,128]{1,0:T...) custom-call(s32[1]{0:T(128)} %bitcast.r, bf16[320,4096]{1,0:T(8,128)(2,1)} %bitcast.18, ...), custom_call_target="tpu_custom_call" | custom-call | flops 1 | bytes 1 | tf_op jit(solution)/shard_map/block_states/pallas_call | solution.py:120
  10.0 1.9 %collective-permute-start = (bf16[512,128]{1,0:T(8,128)(2,1)S(1)}, bf16[512,128]{1,0:T(8,128)(2,1)S(1)}, u32[]{:S(2)}, u32[]{:S(2)}) collective-permute-start(bf16[512,128]{1,0:T(8,128)(2,1)S(1)} %get-tuple-element.95), channel_id=1, source_target_pairs={{0,1},{1,0},{2,3},{3,2},{4,5},{5,4},{6,7},{7,6},{8,9},{9,8},{10,11... | collective-permute-start | bytes 393224 | tf_op jit(solution)/shard_map/ppermute | solution.py:472
  12.0 1.6 %collective-permute-start.1 = (bf16[512,128]{1,0:T(8,128)(2,1)S(1)}, bf16[512,128]{1,0:T(8,128)(2,1)S(1)}, u32[]{:S(2)}, u32[]{:S(2)}) collective-permute-start(bf16[512,128]{1,0:T(8,128)(2,1)S(1)} %get-tuple-element.96), channel_id=1, source_target_pairs={{0,2},{1,3},{2,0},{3,1},{4,6},{5,7},{6,4},{7,5},{8,10},{9,11},{10,... | collective-permute-start | bytes 393224 | tf_op jit(solution)/shard_map/ppermute | solution.py:472
  13.6 0.5 collective-permute-done.5.refs_3_
  14.2 4.7 %collective-permute-start.7 = (bf16[512,128]{1,0:T(8,128)(2,1)S(1)}, bf16[512,128]{1,0:T(8,128)(2,1)S(1)}, u32[]{:S(2)}, u32[]{:S(2)}) collective-permute-start(bf16[512,128]{1,0:T(8,128)(2,1)S(1)} %group_total.4.refs_5_), channel_id=1, source_target_pairs={{0,4},{1,5},{2,6},{3,7},{8,12},{9,13},{10,14},{11,15},{16,20},{17,... | collective-permute-start | bytes 393224 | tf_op jit(solution)/shard_map/ppermute | solution.py:496
  18.9 3.5 %within_block.2 = (bf16[4,320,512]{2,1,0:T(8,128)(2,1)S(1)}, bf16[4,320,512]{2,1,0:T(8,128)(2,1)S(1)}, f32[4,1,512]{2,1,0:T(1,128)S(1)}, f32[4,320,512]{2,1,0:T(...) custom-call(s32[1]{0:T(128)} %bitcast.r, bf16[320,4096]{1,0:T(8,128)(2,1)} %bitcast.13, ...), custom_call_target="tpu_custom_call" | custom-call | flops 1 | bytes 1 | tf_op jit(solution)/shard_map/within_block/pallas_call | solution.py:120
  22.5 2.3 %collective-permute-start.6 = (bf16[512,128]{1,0:T(8,128)(2,1)S(1)}, bf16[512,128]{1,0:T(8,128)(2,1)S(1)}, u32[]{:S(2)}, u32[]{:S(2)}) collective-permute-start(bf16[512,128]{1,0:T(8,128)(2,1)S(1)} %group_total.5.refs_5_), channel_id=1, source_target_pairs={{0,4},{1,5},{2,6},{3,7},{8,12},{9,13},{10,14},{11,15},{16,20},{17,... | collective-permute-start | bytes 393224 | tf_op jit(solution)/shard_map/ppermute | solution.py:496
  24.8 3.5 %within_block.3 = (bf16[4,320,512]{2,1,0:T(8,128)(2,1)S(1)}, bf16[4,320,512]{2,1,0:T(8,128)(2,1)S(1)}, f32[4,1,512]{2,1,0:T(1,128)S(1)}, f32[4,320,512]{2,1,0:T(...) custom-call(s32[1]{0:T(128)} %bitcast.r, bf16[320,4096]{1,0:T(8,128)(2,1)} %bitcast.14, ...), custom_call_target="tpu_custom_call" | custom-call | flops 1 | bytes 1 | tf_op jit(solution)/shard_map/within_block/pallas_call | solution.py:120
  28.5 1.0 %collective-permute-start.11 = (bf16[512,128]{1,0:T(8,128)(2,1)S(1)}, bf16[512,128]{1,0:T(8,128)(2,1)S(1)}, u32[]{:S(2)}, u32[]{:S(2)}) collective-permute-start(bf16[512,128]{1,0:T(8,128)(2,1)S(1)} %get-tuple-element.120), channel_id=1, source_target_pairs={{0,1},{1,0},{2,3},{3,2},{4,5},{5,4},{6,7},{7,6},{8,9},{9,8},{10,11... | collective-permute-start | bytes 393224 | tf_op jit(solution)/shard_map/ppermute | solution.py:472
  29.5 3.0 %collective-permute-start.12 = (bf16[512,128]{1,0:T(8,128)(2,1)S(1)}, bf16[512,128]{1,0:T(8,128)(2,1)S(1)}, u32[]{:S(2)}, u32[]{:S(2)}) collective-permute-start(bf16[512,128]{1,0:T(8,128)(2,1)S(1)} %get-tuple-element.121), channel_id=1, source_target_pairs={{0,2},{1,3},{2,0},{3,1},{4,6},{5,7},{6,4},{7,5},{8,10},{9,11},{10,... | collective-permute-start | bytes 393224 | tf_op jit(solution)/shard_map/ppermute | solution.py:472
  32.9 1.5 %collective-permute-start.8 = (bf16[512,128]{1,0:T(8,128)(2,1)S(1)}, bf16[512,128]{1,0:T(8,128)(2,1)S(1)}, u32[]{:S(2)}, u32[]{:S(2)}) collective-permute-start(bf16[512,128]{1,0:T(8,128)(2,1)S(1)} %get-tuple-element.114), channel_id=1, source_target_pairs={{0,1},{1,0},{2,3},{3,2},{4,5},{5,4},{6,7},{7,6},{8,9},{9,8},{10,11... | collective-permute-start | bytes 393224 | tf_op jit(solution)/shard_map/ppermute | solution.py:472
  34.3 2.0 %collective-permute-start.9 = (bf16[512,128]{1,0:T(8,128)(2,1)S(1)}, bf16[512,128]{1,0:T(8,128)(2,1)S(1)}, u32[]{:S(2)}, u32[]{:S(2)}) collective-permute-start(bf16[512,128]{1,0:T(8,128)(2,1)S(1)} %get-tuple-element.115), channel_id=1, source_target_pairs={{0,2},{1,3},{2,0},{3,1},{4,6},{5,7},{6,4},{7,5},{8,10},{9,11},{10,... | collective-permute-start | bytes 393224 | tf_op jit(solution)/shard_map/ppermute | solution.py:472
  36.3 1.7 %collective-permute-done.11.refs_5_.refs_6_ = bf16[512,128]{1,0:T(8,128)(2,1)S(1)} collective-permute-done((bf16[512,128]{1,0:T(8,128)(2,1)S(1)}, bf16[512,128]{1,0:T(8,128)(2,1)S(1)}, u32[]{:S(2)}, u32[]{:S(2)}) %collective-permute-start.11) | collective-permute-done | bytes 131104 | tf_op jit(solution)/shard_map/ppermute | solution.py:472
  38.1 0.6 mix.3
  38.7 1.9 %collective-permute-done.10.refs_8_.refs_9_.refs_7_ = bf16[1024,128]{1,0:T(8,128)(2,1)S(1)} collective-permute-done((bf16[1024,128]{1,0:T(8,128)(2,1)S(1)}, bf16[1024,128]{1,0:T(8,128)(2,1)S(1)}, u32[]{:S(2)}, u32[]{:S(2)}) %collective-permute-start.10) | collective-permute-done | bytes 262176 | tf_op jit(solution)/shard_map/ppermute | solution.py:472
  40.6 0.5 mix.4
  41.2 0.8 collective-permute-done.8.refs_5_.refs_7_
  41.9 0.8 mix.5
  42.7 1.4 %mixed_gradients.3 = (bf16[4,320,512]{2,1,0:T(8,128)(2,1)S(1)}, bf16[512,128]{1,0:T(8,128)(2,1)S(1)}, bf16[512,128]{1,0:T(8,128)(2,1)S(1)}, bf16[512,128]{1,0:T(8,128)(2,1)S(1)}, bf16[512,128]{1,0:T(8,128)(2,1)S(1)}) custom-call(s32[1]{0:T(128)} %bitcast.r, f32[4,320,512]{2,1,0:T(8,128)S(1)} %get-tuple-element.132.refs_0_, ...), custom_call_target="tpu_custom_call" | custom-call | flops 1 | bytes 1 | tf_op jit(solution)/shard_map/mixed_gradients/pallas_call | solution.py:120
  44.1 0.7 collective-permute-start.13
  44.8 1.3 %collective-permute-start.14 = (bf16[512,128]{1,0:T(8,128)(2,1)S(1)}, bf16[512,128]{1,0:T(8,128)(2,1)S(1)}, u32[]{:S(2)}, u32[]{:S(2)}) collective-permute-start(bf16[512,128]{1,0:T(8,128)(2,1)S(1)} %get-tuple-element.136), channel_id=1, source_target_pairs={{0,2},{1,3},{2,0},{3,1},{4,6},{5,7},{6,4},{7,5},{8,10},{9,11},{10,... | collective-permute-start | bytes 393224 | tf_op jit(solution)/shard_map/ppermute | solution.py:472
  46.1 1.5 %collective-permute-start.15 = (bf16[512,128]{1,0:T(8,128)(2,1)S(1)}, bf16[512,128]{1,0:T(8,128)(2,1)S(1)}, u32[]{:S(2)}, u32[]{:S(2)}) collective-permute-start(bf16[512,128]{1,0:T(8,128)(2,1)S(1)} %get-tuple-element.137), channel_id=1, source_target_pairs={{0,3},{1,2},{2,1},{3,0},{4,7},{5,6},{6,5},{7,4},{8,11},{9,10},{10,... | collective-permute-start | bytes 393224 | tf_op jit(solution)/shard_map/ppermute | solution.py:472
  47.7 1.5 %mixed_gradients.2 = (bf16[4,320,512]{2,1,0:T(8,128)(2,1)S(1)}, bf16[512,128]{1,0:T(8,128)(2,1)S(1)}, bf16[512,128]{1,0:T(8,128)(2,1)S(1)}, bf16[512,128]{1,0:T(8,128)(2,1)S(1)}, bf16[512,128]{1,0:T(8,128)(2,1)S(1)}) custom-call(s32[1]{0:T(128)} %bitcast.r, f32[4,320,512]{2,1,0:T(8,128)S(1)} %get-tuple-element.128.refs_0_, ...), custom_call_target="tpu_custom_call" | custom-call | flops 1 | bytes 1 | tf_op jit(solution)/shard_map/mixed_gradients/pallas_call | solution.py:120
  49.2 0.7 collective-permute-start.19
  49.9 1.3 %collective-permute-start.20 = (bf16[512,128]{1,0:T(8,128)(2,1)S(1)}, bf16[512,128]{1,0:T(8,128)(2,1)S(1)}, u32[]{:S(2)}, u32[]{:S(2)}) collective-permute-start(bf16[512,128]{1,0:T(8,128)(2,1)S(1)} %get-tuple-element.147), channel_id=1, source_target_pairs={{0,2},{1,3},{2,0},{3,1},{4,6},{5,7},{6,4},{7,5},{8,10},{9,11},{10,... | collective-permute-start | bytes 393224 | tf_op jit(solution)/shard_map/ppermute | solution.py:472
  51.2 1.5 %collective-permute-start.21 = (bf16[512,128]{1,0:T(8,128)(2,1)S(1)}, bf16[512,128]{1,0:T(8,128)(2,1)S(1)}, u32[]{:S(2)}, u32[]{:S(2)}) collective-permute-start(bf16[512,128]{1,0:T(8,128)(2,1)S(1)} %get-tuple-element.148), channel_id=1, source_target_pairs={{0,3},{1,2},{2,1},{3,0},{4,7},{5,6},{6,5},{7,4},{8,11},{9,10},{10,... | collective-permute-start | bytes 393224 | tf_op jit(solution)/shard_map/ppermute | solution.py:472
  52.8 0.9 %normed_output.2 = (bf16[4,320,512]{2,1,0:T(8,128)(2,1)S(1)}, f32[32,128]{1,0:T(8,128)S(1)}) custom-call(s32[1]{0:T(128)} %bitcast.r, f32[4,320,512]{2,1,0:T(8,128)S(1)} %get-tuple-element.132.refs_0_, bf16[4,320,512]{2,1,0:T(8,128)(2,1)S(1)} %get-tuple-element.117.refs_2_.refs_1_, f32[4,1,512]{2,1,0:T(1,128)S(1)} %get-tuple-element.118.refs_3_.refs_2_, ...), custom_call_target="tpu_custom_call" | custom-call | flops 1 | bytes 1 | tf_op jit(solution)/shard_map/normed_output/pallas_call | solution.py:120
  53.7 0.5 collective-permute-done.15.refs_3_
  54.3 1.3 %collective-permute-start.16 = (bf16[512,128]{1,0:T(8,128)(2,1)S(1)}, bf16[512,128]{1,0:T(8,128)(2,1)S(1)}, u32[]{:S(2)}, u32[]{:S(2)}) collective-permute-start(bf16[512,128]{1,0:T(8,128)(2,1)S(1)} %group_total.6.refs_4_), channel_id=1, source_target_pairs={{4,0},{5,1},{6,2},{7,3},{12,8},{13,9},{14,10},{15,11},{20,16},{21,... | collective-permute-start | bytes 393224 | tf_op jit(solution)/shard_map/ppermute | solution.py:496
  55.6 0.9 %normed_output.3 = (bf16[4,320,512]{2,1,0:T(8,128)(2,1)S(1)}, f32[32,128]{1,0:T(8,128)S(1)}) custom-call(s32[1]{0:T(128)} %bitcast.r, f32[4,320,512]{2,1,0:T(8,128)S(1)} %get-tuple-element.128.refs_0_, bf16[4,320,512]{2,1,0:T(8,128)(2,1)S(1)} %get-tuple-element.109.refs_6_.refs_2_.refs_1_, ...), custom_call_target="tpu_custom_call", output_to_operand_aliasing={{1}: (6, {})} | custom-call | flops 1 | bytes 1 | tf_op jit(solution)/shard_map/normed_output/pallas_call | solution.py:120
  56.6 1.5 %inner_gradients.4 = (bf16[4,320,512]{2,1,0:T(8,128)(2,1)S(1)}, f32[4,320,512]{2,1,0:T(8,128)S(1)}, f32[4,320,512]{2,1,0:T(8,128)S(1)}, f32[8,128]{1,0:T(8,128)S(1)}) custom-call(s32[1]{0:T(128)} %bitcast.r, bf16[4,4,320,256]{3,2,1,0:T(8,128)(2,1)S(1)} %get-tuple-element.140.refs_0_, bf16[4,4,64,64]{3,2,1,0:T(8,128)(2,1)S(1)} %get-tuple-element.141.refs_1_, ...), custom_call_target="tpu_custom_call" | custom-call | flops 1 | bytes 1 | tf_op jit(solution)/shard_map/inner_gradients/pallas_call | solution.py:120
  58.1 0.4 collective-permute-done.21.refs_3_
  58.6 1.5 %collective-permute-start.24 = (bf16[512,128]{1,0:T(8,128)(2,1)S(1)}, bf16[512,128]{1,0:T(8,128)(2,1)S(1)}, u32[]{:S(2)}, u32[]{:S(2)}) collective-permute-start(bf16[512,128]{1,0:T(8,128)(2,1)S(1)} %group_total.7.refs_7_), channel_id=1, source_target_pairs={{4,0},{5,1},{6,2},{7,3},{12,8},{13,9},{14,10},{15,11},{20,16},{21,... | collective-permute-start | bytes 393224 | tf_op jit(solution)/shard_map/ppermute | solution.py:496
  60.1 1.6 %collective-permute-start.18 = (f32[32,128]{1,0:T(8,128)S(1)}, f32[32,128]{1,0:T(8,128)S(1)}, u32[]{:S(2)}, u32[]{:S(2)}) collective-permute-start(f32[32,128]{1,0:T(8,128)S(1)} %gain_sum.3.refs_4_.refs_0_), channel_id=1, source_target_pairs={{0,16},{8,24},{16,0},{24,8},{1,17},{9,25},{17,1},{25,9},{2,18},{10... | collective-permute-start | bytes 49160 | tf_op jit(solution)/shard_map/ppermute | solution.py:472
  61.7 1.5 %inner_gradients.5 = (bf16[4,320,512]{2,1,0:T(8,128)(2,1)S(1)}, f32[4,320,512]{2,1,0:T(8,128)S(1)}, f32[4,320,512]{2,1,0:T(8,128)S(1)}, f32[8,128]{1,0:T(8,128)S(1)}) custom-call(s32[1]{0:T(128)} %bitcast.r, bf16[4,4,320,256]{3,2,1,0:T(8,128)(2,1)S(1)} %get-tuple-element.140.refs_0_, ...), custom_call_target="tpu_custom_call", output_to_operand_aliasing={{0}: (9, {}), {1}: (10, {}), {2}: (11, {})} | custom-call | flops 1 | bytes 1 | tf_op jit(solution)/shard_map/inner_gradients/pallas_call | solution.py:120
  63.2 0.7 collective-permute-done.18.refs_1_
  64.2 0.7 collective-permute-start.22
  64.9 0.5 collective-permute-start.23
  65.4 3.5 %collective-permute-start.25 = (f32[32,128]{1,0:T(8,128)S(1)}, f32[32,128]{1,0:T(8,128)S(1)}, u32[]{:S(2)}, u32[]{:S(2)}) collective-permute-start(f32[32,128]{1,0:T(8,128)S(1)} %gain_sum.4.refs_5_.refs_0_), channel_id=1, source_target_pairs={{0,4},{1,5},{2,6},{3,7},{4,0},{5,1},{6,2},{7,3},{8,12},{9,13},{10,... | collective-permute-start | bytes 49160 | tf_op jit(solution)/shard_map/ppermute | solution.py:472
  68.9 2.8 %inner_gradients.6 = (bf16[4,320,512]{2,1,0:T(8,128)(2,1)S(1)}, f32[4,320,512]{2,1,0:T(8,128)S(1)}, f32[4,320,512]{2,1,0:T(8,128)S(1)}, f32[8,128]{1,0:T(8,128)S(1)}) custom-call(s32[1]{0:T(128)} %bitcast.r, bf16[4,4,320,256]{3,2,1,0:T(8,128)(2,1)S(1)} %get-tuple-element.140.refs_0_, ...), custom_call_target="tpu_custom_call", output_to_operand_aliasing={{0}: (10, {}), {1}: (11, {}), {2}: (12, {})} | custom-call | flops 1 | bytes 1 | tf_op jit(solution)/shard_map/inner_gradients/pallas_call | solution.py:120
  72.0 2.7 %collective-permute-start.28 = (bf16[1088,128]{1,0:T(8,128)(2,1)S(1)}, bf16[1088,128]{1,0:T(8,128)(2,1)S(1)}, u32[]{:S(2)}, u32[]{:S(2)}) collective-permute-start(bf16[1088,128]{1,0:T(8,128)(2,1)S(1)} %get-tuple-element.170), channel_id=1, source_target_pairs={{0,3},{1,2},{2,1},{3,0},{4,7},{5,6},{6,5},{7,4},{8,11},{9,10},{10,... | collective-permute-start | bytes 835592 | tf_op jit(solution)/shard_map/ppermute | solution.py:472
  74.8 0.6 collective-permute-start.26
  75.6 7.1 %inner_gradients.7 = (bf16[4,320,512]{2,1,0:T(8,128)(2,1)S(1)}, f32[4,320,512]{2,1,0:T(8,128)S(1)}, f32[4,320,512]{2,1,0:T(8,128)S(1)}, f32[8,128]{1,0:T(8,128)}...) custom-call(s32[1]{0:T(128)} %bitcast.r, ...), custom_call_target="tpu_custom_call" | custom-call | flops 2000000000 | bytes 7200001 | tf_op jit(solution)/shard_map/inner_gradients/pallas_call | solution.py:120
  82.7 0.7 collective-permute-done.26.refs_9_
  83.4 2.2 %outer_gradients.1 = (bf16[320,4096]{1,0:T(8,128)(2,1)}, bf16[320,4096]{1,0:T(8,128)(2,1)}, bf16[320,4096]{1,0:T(8,128)(2,1)}, f32[32,128]{1,0:T(8,128)}) custom-call(s32[1]{0:T(128)} %bitcast.r, bf16[4,320,512]{2,1,0:T(8,128)(2,1)S(1)} %get-tuple-element.98.refs_3_.refs_13_.refs_0_, ...), custom_call_target="tpu_custom_call", output_to_operand_aliasing={{0}: (15, {}), {1}: (16, {}), {2}: (17, {})} | custom-call | flops 1 | bytes 1 | tf_op jit(solution)/shard_map/outer_gradients/pallas_call | solution.py:120
  (39 shorter events, 1.8 us)
Async XLA Ops:
  3.0 10.6 %collective-permute-start.3 = (bf16[512,128]{1,0:T(8,128)(2,1)S(1)}, bf16[512,128]{1,0:T(8,128)(2,1)S(1)}, u32[]{:S(2)}, u32[]{:S(2)}) collective-permute-start(bf16[512,128]{1,0:T(8,128)(2,1)S(1)} %get-tuple-element.101), channel_id=1, source_target_pairs={{0,1},{1,0},{2,3},{3,2},{4,5},{5,4},{6,7},{7,6},{8,9},{9,8},{10,11... | collective-permute-start | bytes 393224 | tf_op jit(solution)/shard_map/ppermute | solution.py:472
  6.0 7.6 %collective-permute-start.4 = (bf16[512,128]{1,0:T(8,128)(2,1)S(1)}, bf16[512,128]{1,0:T(8,128)(2,1)S(1)}, u32[]{:S(2)}, u32[]{:S(2)}) collective-permute-start(bf16[512,128]{1,0:T(8,128)(2,1)S(1)} %get-tuple-element.102), channel_id=1, source_target_pairs={{0,2},{1,3},{2,0},{3,1},{4,6},{5,7},{6,4},{7,5},{8,10},{9,11},{10,... | collective-permute-start | bytes 393224 | tf_op jit(solution)/shard_map/ppermute | solution.py:472
  7.6 11.3 %copy-start = (f32[4096]{0:T(1024)S(1)}, f32[4096]{0:T(1024)}, u32[]{:S(2)}) copy-start(f32[4096]{0:T(1024)} %param.8) | copy-start | bytes 49156
  7.6 6.4 %collective-permute-start.5 = (bf16[512,128]{1,0:T(8,128)(2,1)S(1)}, bf16[512,128]{1,0:T(8,128)(2,1)S(1)}, u32[]{:S(2)}, u32[]{:S(2)}) collective-permute-start(bf16[512,128]{1,0:T(8,128)(2,1)S(1)} %get-tuple-element.103), channel_id=1, source_target_pairs={{0,3},{1,2},{2,1},{3,0},{4,7},{5,6},{6,5},{7,4},{8,11},{9,10},{10,... | collective-permute-start | bytes 393224 | tf_op jit(solution)/shard_map/ppermute | solution.py:472
  10.0 12.3 %collective-permute-start = (bf16[512,128]{1,0:T(8,128)(2,1)S(1)}, bf16[512,128]{1,0:T(8,128)(2,1)S(1)}, u32[]{:S(2)}, u32[]{:S(2)}) collective-permute-start(bf16[512,128]{1,0:T(8,128)(2,1)S(1)} %get-tuple-element.95), channel_id=1, source_target_pairs={{0,1},{1,0},{2,3},{3,2},{4,5},{5,4},{6,7},{7,6},{8,9},{9,8},{10,11... | collective-permute-start | bytes 393224 | tf_op jit(solution)/shard_map/ppermute | solution.py:472
  12.0 10.4 %collective-permute-start.1 = (bf16[512,128]{1,0:T(8,128)(2,1)S(1)}, bf16[512,128]{1,0:T(8,128)(2,1)S(1)}, u32[]{:S(2)}, u32[]{:S(2)}) collective-permute-start(bf16[512,128]{1,0:T(8,128)(2,1)S(1)} %get-tuple-element.96), channel_id=1, source_target_pairs={{0,2},{1,3},{2,0},{3,1},{4,6},{5,7},{6,4},{7,5},{8,10},{9,11},{10,... | collective-permute-start | bytes 393224 | tf_op jit(solution)/shard_map/ppermute | solution.py:472
  13.6 8.8 %collective-permute-start.2 = (bf16[512,128]{1,0:T(8,128)(2,1)S(1)}, bf16[512,128]{1,0:T(8,128)(2,1)S(1)}, u32[]{:S(2)}, u32[]{:S(2)}) collective-permute-start(bf16[512,128]{1,0:T(8,128)(2,1)S(1)} %get-tuple-element.97), channel_id=1, source_target_pairs={{0,3},{1,2},{2,1},{3,0},{4,7},{5,6},{6,5},{7,4},{8,11},{9,10},{10,... | collective-permute-start | bytes 393224 | tf_op jit(solution)/shard_map/ppermute | solution.py:472
  14.2 14.1 %collective-permute-start.7 = (bf16[512,128]{1,0:T(8,128)(2,1)S(1)}, bf16[512,128]{1,0:T(8,128)(2,1)S(1)}, u32[]{:S(2)}, u32[]{:S(2)}) collective-permute-start(bf16[512,128]{1,0:T(8,128)(2,1)S(1)} %group_total.4.refs_5_), channel_id=1, source_target_pairs={{0,4},{1,5},{2,6},{3,7},{8,12},{9,13},{10,14},{11,15},{16,20},{17,... | collective-permute-start | bytes 393224 | tf_op jit(solution)/shard_map/ppermute | solution.py:496
  22.5 10.0 %collective-permute-start.6 = (bf16[512,128]{1,0:T(8,128)(2,1)S(1)}, bf16[512,128]{1,0:T(8,128)(2,1)S(1)}, u32[]{:S(2)}, u32[]{:S(2)}) collective-permute-start(bf16[512,128]{1,0:T(8,128)(2,1)S(1)} %group_total.5.refs_5_), channel_id=1, source_target_pairs={{0,4},{1,5},{2,6},{3,7},{8,12},{9,13},{10,14},{11,15},{16,20},{17,... | collective-permute-start | bytes 393224 | tf_op jit(solution)/shard_map/ppermute | solution.py:496
  28.5 9.5 %collective-permute-start.11 = (bf16[512,128]{1,0:T(8,128)(2,1)S(1)}, bf16[512,128]{1,0:T(8,128)(2,1)S(1)}, u32[]{:S(2)}, u32[]{:S(2)}) collective-permute-start(bf16[512,128]{1,0:T(8,128)(2,1)S(1)} %get-tuple-element.120), channel_id=1, source_target_pairs={{0,1},{1,0},{2,3},{3,2},{4,5},{5,4},{6,7},{7,6},{8,9},{9,8},{10,11... | collective-permute-start | bytes 393224 | tf_op jit(solution)/shard_map/ppermute | solution.py:472
  29.5 8.6 %collective-permute-start.12 = (bf16[512,128]{1,0:T(8,128)(2,1)S(1)}, bf16[512,128]{1,0:T(8,128)(2,1)S(1)}, u32[]{:S(2)}, u32[]{:S(2)}) collective-permute-start(bf16[512,128]{1,0:T(8,128)(2,1)S(1)} %get-tuple-element.121), channel_id=1, source_target_pairs={{0,2},{1,3},{2,0},{3,1},{4,6},{5,7},{6,4},{7,5},{8,10},{9,11},{10,... | collective-permute-start | bytes 393224 | tf_op jit(solution)/shard_map/ppermute | solution.py:472
  32.8 7.9 %collective-permute-start.10 = (bf16[1024,128]{1,0:T(8,128)(2,1)S(1)}, bf16[1024,128]{1,0:T(8,128)(2,1)S(1)}, u32[]{:S(2)}, u32[]{:S(2)}) collective-permute-start(bf16[1024,128]{1,0:T(8,128)(2,1)S(1)} %get-tuple-element.119), channel_id=1, source_target_pairs={{0,3},{1,2},{2,1},{3,0},{4,7},{5,6},{6,5},{7,4},{8,11},{9,10},{10,... | collective-permute-start | bytes 786440 | tf_op jit(solution)/shard_map/ppermute | solution.py:472
  32.9 9.1 %collective-permute-start.8 = (bf16[512,128]{1,0:T(8,128)(2,1)S(1)}, bf16[512,128]{1,0:T(8,128)(2,1)S(1)}, u32[]{:S(2)}, u32[]{:S(2)}) collective-permute-start(bf16[512,128]{1,0:T(8,128)(2,1)S(1)} %get-tuple-element.114), channel_id=1, source_target_pairs={{0,1},{1,0},{2,3},{3,2},{4,5},{5,4},{6,7},{7,6},{8,9},{9,8},{10,11... | collective-permute-start | bytes 393224 | tf_op jit(solution)/shard_map/ppermute | solution.py:472
  34.3 7.6 %collective-permute-start.9 = (bf16[512,128]{1,0:T(8,128)(2,1)S(1)}, bf16[512,128]{1,0:T(8,128)(2,1)S(1)}, u32[]{:S(2)}, u32[]{:S(2)}) collective-permute-start(bf16[512,128]{1,0:T(8,128)(2,1)S(1)} %get-tuple-element.115), channel_id=1, source_target_pairs={{0,2},{1,3},{2,0},{3,1},{4,6},{5,7},{6,4},{7,5},{8,10},{9,11},{10,... | collective-permute-start | bytes 393224 | tf_op jit(solution)/shard_map/ppermute | solution.py:472
  44.1 7.1 %collective-permute-start.13 = (bf16[512,128]{1,0:T(8,128)(2,1)S(1)}, bf16[512,128]{1,0:T(8,128)(2,1)S(1)}, u32[]{:S(2)}, u32[]{:S(2)}) collective-permute-start(bf16[512,128]{1,0:T(8,128)(2,1)S(1)} %get-tuple-element.135), channel_id=1, source_target_pairs={{0,1},{1,0},{2,3},{3,2},{4,5},{5,4},{6,7},{7,6},{8,9},{9,8},{10,11... | collective-permute-start | bytes 393224 | tf_op jit(solution)/shard_map/ppermute | solution.py:472
  44.8 8.9 %collective-permute-start.14 = (bf16[512,128]{1,0:T(8,128)(2,1)S(1)}, bf16[512,128]{1,0:T(8,128)(2,1)S(1)}, u32[]{:S(2)}, u32[]{:S(2)}) collective-permute-start(bf16[512,128]{1,0:T(8,128)(2,1)S(1)} %get-tuple-element.136), channel_id=1, source_target_pairs={{0,2},{1,3},{2,0},{3,1},{4,6},{5,7},{6,4},{7,5},{8,10},{9,11},{10,... | collective-permute-start | bytes 393224 | tf_op jit(solution)/shard_map/ppermute | solution.py:472
  46.1 8.0 %collective-permute-start.15 = (bf16[512,128]{1,0:T(8,128)(2,1)S(1)}, bf16[512,128]{1,0:T(8,128)(2,1)S(1)}, u32[]{:S(2)}, u32[]{:S(2)}) collective-permute-start(bf16[512,128]{1,0:T(8,128)(2,1)S(1)} %get-tuple-element.137), channel_id=1, source_target_pairs={{0,3},{1,2},{2,1},{3,0},{4,7},{5,6},{6,5},{7,4},{8,11},{9,10},{10,... | collective-permute-start | bytes 393224 | tf_op jit(solution)/shard_map/ppermute | solution.py:472
  49.2 8.9 %collective-permute-start.19 = (bf16[512,128]{1,0:T(8,128)(2,1)S(1)}, bf16[512,128]{1,0:T(8,128)(2,1)S(1)}, u32[]{:S(2)}, u32[]{:S(2)}) collective-permute-start(bf16[512,128]{1,0:T(8,128)(2,1)S(1)} %get-tuple-element.146), channel_id=1, source_target_pairs={{0,1},{1,0},{2,3},{3,2},{4,5},{5,4},{6,7},{7,6},{8,9},{9,8},{10,11... | collective-permute-start | bytes 393224 | tf_op jit(solution)/shard_map/ppermute | solution.py:472
  49.9 8.2 %collective-permute-start.20 = (bf16[512,128]{1,0:T(8,128)(2,1)S(1)}, bf16[512,128]{1,0:T(8,128)(2,1)S(1)}, u32[]{:S(2)}, u32[]{:S(2)}) collective-permute-start(bf16[512,128]{1,0:T(8,128)(2,1)S(1)} %get-tuple-element.147), channel_id=1, source_target_pairs={{0,2},{1,3},{2,0},{3,1},{4,6},{5,7},{6,4},{7,5},{8,10},{9,11},{10,... | collective-permute-start | bytes 393224 | tf_op jit(solution)/shard_map/ppermute | solution.py:472
  51.2 7.3 %collective-permute-start.21 = (bf16[512,128]{1,0:T(8,128)(2,1)S(1)}, bf16[512,128]{1,0:T(8,128)(2,1)S(1)}, u32[]{:S(2)}, u32[]{:S(2)}) collective-permute-start(bf16[512,128]{1,0:T(8,128)(2,1)S(1)} %get-tuple-element.148), channel_id=1, source_target_pairs={{0,3},{1,2},{2,1},{3,0},{4,7},{5,6},{6,5},{7,4},{8,11},{9,10},{10,... | collective-permute-start | bytes 393224 | tf_op jit(solution)/shard_map/ppermute | solution.py:472
  54.3 9.7 %collective-permute-start.16 = (bf16[512,128]{1,0:T(8,128)(2,1)S(1)}, bf16[512,128]{1,0:T(8,128)(2,1)S(1)}, u32[]{:S(2)}, u32[]{:S(2)}) collective-permute-start(bf16[512,128]{1,0:T(8,128)(2,1)S(1)} %group_total.6.refs_4_), channel_id=1, source_target_pairs={{4,0},{5,1},{6,2},{7,3},{12,8},{13,9},{14,10},{15,11},{20,16},{21,... | collective-permute-start | bytes 393224 | tf_op jit(solution)/shard_map/ppermute | solution.py:496
  56.5 1.6 %collective-permute-start.17 = (f32[32,128]{1,0:T(8,128)S(1)}, f32[32,128]{1,0:T(8,128)S(1)}, u32[]{:S(2)}, u32[]{:S(2)}) collective-permute-start(f32[32,128]{1,0:T(8,128)S(1)} %get-tuple-element.143.refs_7_.refs_0_), channel_id=1, source_target_pairs={{0,8},{8,0},{16,24},{24,16},{1,9},{9,1},{17,25},{25,17},{2,10},{10... | collective-permute-start | bytes 49160 | tf_op jit(solution)/shard_map/ppermute | solution.py:472
  58.6 13.2 %collective-permute-start.24 = (bf16[512,128]{1,0:T(8,128)(2,1)S(1)}, bf16[512,128]{1,0:T(8,128)(2,1)S(1)}, u32[]{:S(2)}, u32[]{:S(2)}) collective-permute-start(bf16[512,128]{1,0:T(8,128)(2,1)S(1)} %group_total.7.refs_7_), channel_id=1, source_target_pairs={{4,0},{5,1},{6,2},{7,3},{12,8},{13,9},{14,10},{15,11},{20,16},{21,... | collective-permute-start | bytes 393224 | tf_op jit(solution)/shard_map/ppermute | solution.py:496
  60.1 3.8 %collective-permute-start.18 = (f32[32,128]{1,0:T(8,128)S(1)}, f32[32,128]{1,0:T(8,128)S(1)}, u32[]{:S(2)}, u32[]{:S(2)}) collective-permute-start(f32[32,128]{1,0:T(8,128)S(1)} %gain_sum.3.refs_4_.refs_0_), channel_id=1, source_target_pairs={{0,16},{8,24},{16,0},{24,8},{1,17},{9,25},{17,1},{25,9},{2,18},{10... | collective-permute-start | bytes 49160 | tf_op jit(solution)/shard_map/ppermute | solution.py:472
  64.2 11.4 %collective-permute-start.22 = (bf16[512,128]{1,0:T(8,128)(2,1)S(1)}, bf16[512,128]{1,0:T(8,128)(2,1)S(1)}, u32[]{:S(2)}, u32[]{:S(2)}) collective-permute-start(bf16[512,128]{1,0:T(8,128)(2,1)S(1)} %get-tuple-element.160), channel_id=1, source_target_pairs={{0,1},{1,0},{2,3},{3,2},{4,5},{5,4},{6,7},{7,6},{8,9},{9,8},{10,11... | collective-permute-start | bytes 393224 | tf_op jit(solution)/shard_map/ppermute | solution.py:472
  64.9 10.7 %collective-permute-start.23 = (bf16[512,128]{1,0:T(8,128)(2,1)S(1)}, bf16[512,128]{1,0:T(8,128)(2,1)S(1)}, u32[]{:S(2)}, u32[]{:S(2)}) collective-permute-start(bf16[512,128]{1,0:T(8,128)(2,1)S(1)} %get-tuple-element.161), channel_id=1, source_target_pairs={{0,2},{1,3},{2,0},{3,1},{4,6},{5,7},{6,4},{7,5},{8,10},{9,11},{10,... | collective-permute-start | bytes 393224 | tf_op jit(solution)/shard_map/ppermute | solution.py:472
  65.4 6.3 %collective-permute-start.25 = (f32[32,128]{1,0:T(8,128)S(1)}, f32[32,128]{1,0:T(8,128)S(1)}, u32[]{:S(2)}, u32[]{:S(2)}) collective-permute-start(f32[32,128]{1,0:T(8,128)S(1)} %gain_sum.4.refs_5_.refs_0_), channel_id=1, source_target_pairs={{0,4},{1,5},{2,6},{3,7},{4,0},{5,1},{6,2},{7,3},{8,12},{9,13},{10,... | collective-permute-start | bytes 49160 | tf_op jit(solution)/shard_map/ppermute | solution.py:472
  72.0 11.4 %collective-permute-start.28 = (bf16[1088,128]{1,0:T(8,128)(2,1)S(1)}, bf16[1088,128]{1,0:T(8,128)(2,1)S(1)}, u32[]{:S(2)}, u32[]{:S(2)}) collective-permute-start(bf16[1088,128]{1,0:T(8,128)(2,1)S(1)} %get-tuple-element.170), channel_id=1, source_target_pairs={{0,3},{1,2},{2,1},{3,0},{4,7},{5,6},{6,5},{7,4},{8,11},{9,10},{10,... | collective-permute-start | bytes 835592 | tf_op jit(solution)/shard_map/ppermute | solution.py:472
  74.8 8.6 %collective-permute-start.26 = (bf16[576,128]{1,0:T(8,128)(2,1)S(1)}, bf16[576,128]{1,0:T(8,128)(2,1)S(1)}, u32[]{:S(2)}, u32[]{:S(2)}) collective-permute-start(bf16[576,128]{1,0:T(8,128)(2,1)S(1)} %get-tuple-element.168), channel_id=1, source_target_pairs={{0,1},{1,0},{2,3},{3,2},{4,5},{5,4},{6,7},{7,6},{8,9},{9,8},{10,11... | collective-permute-start | bytes 442376 | tf_op jit(solution)/shard_map/ppermute | solution.py:472
  75.4 8.0 %collective-permute-start.27 = (bf16[576,128]{1,0:T(8,128)(2,1)S(1)}, bf16[576,128]{1,0:T(8,128)(2,1)S(1)}, u32[]{:S(2)}, u32[]{:S(2)}) collective-permute-start(bf16[576,128]{1,0:T(8,128)(2,1)S(1)} %get-tuple-element.169), channel_id=1, source_target_pairs={{0,2},{1,3},{2,0},{3,1},{4,6},{5,7},{6,4},{7,5},{8,10},{9,11},{10,... | collective-permute-start | bytes 442376 | tf_op jit(solution)/shard_map/ppermute | solution.py:472

commit v6 on v5

--- a/solution.py
+++ b/solution.py
@@ -473,7 +473,7 @@
 
 
 def gather_home(pieces, context):
-    order = range(len(pieces) - 1, 0, -1)
+    order = [*range(1, len(pieces))][-1:] + [*range(1, len(pieces) - 1)]
     got = {k: swap(pieces[k], "context", context, k) for k in order}
     return [pieces[0]] + [got[k] for k in range(1, len(pieces))]
 

time: 86.1 us -> 86.1 us (level)
  no operation moved by 1% of the time
where the time goes in v6:
time: 86.1 us; the launch traced here: 85.8 us
  starting transfers between devices  42.5 us (49%)
  Pallas kernels  34.9 us (41%)
  waiting for transfers between devices  7.26 us (8%)
  between operations  1.13 us (1%)
    pallas_call x27, Pallas kernels, call(): pl.pallas_call(kernel, name=name, grid_spec=pltpu.PrefetchScalarGridSpec(...  34.9 us
    ppermute x25, starting transfers between devices, swap(): return lax.ppermute(array, axis, [(c, c ^ k) for c in range(size)])  32.7 us
    ppermute x4, starting transfers between devices, cross_groups(): lax.ppermute(total, 'context', up if forward else [(b, a) for a, b in up])  9.83 us
    ppermute x25, waiting for transfers between devices, swap(): return lax.ppermute(array, axis, [(c, c ^ k) for c in range(size)])  7.25 us
  transfers between devices with their start and end apart: 29, of which 8 were waited for; matrix products, arithmetic and copies ran while one was open for 0% of the time, Pallas kernels for 33%

profile of v6, /device:TPU:0, one launch (start us, length us, event | category | flops | bytes accessed | tf_op | source)
XLA Modules:
  0.0 85.8 jit_solution(5045476909596376025)
XLA Ops:
  0.6 2.4 %block_states.3 = (bf16[4,320,512]{2,1,0:T(8,128)(2,1)S(1)}, bf16[4,320,512]{2,1,0:T(8,128)(2,1)S(1)}, bf16[512,128]{1,0:T(8,128)(2,1)S(1)}, bf16[512,128]{1,0:T...) custom-call(s32[1]{0:T(128)} %bitcast.r, bf16[320,4096]{1,0:T(8,128)(2,1)} %bitcast.17, ...), custom_call_target="tpu_custom_call" | custom-call | flops 1 | bytes 1 | tf_op jit(solution)/shard_map/block_states/pallas_call | solution.py:120
  3.0 3.0 %collective-permute-start.3 = (bf16[512,128]{1,0:T(8,128)(2,1)S(1)}, bf16[512,128]{1,0:T(8,128)(2,1)S(1)}, u32[]{:S(2)}, u32[]{:S(2)}) collective-permute-start(bf16[512,128]{1,0:T(8,128)(2,1)S(1)} %get-tuple-element.101), channel_id=1, source_target_pairs={{0,1},{1,0},{2,3},{3,2},{4,5},{5,4},{6,7},{7,6},{8,9},{9,8},{10,11... | collective-permute-start | bytes 393224 | tf_op jit(solution)/shard_map/ppermute | solution.py:472
  6.0 1.6 %collective-permute-start.4 = (bf16[512,128]{1,0:T(8,128)(2,1)S(1)}, bf16[512,128]{1,0:T(8,128)(2,1)S(1)}, u32[]{:S(2)}, u32[]{:S(2)}) collective-permute-start(bf16[512,128]{1,0:T(8,128)(2,1)S(1)} %get-tuple-element.102), channel_id=1, source_target_pairs={{0,2},{1,3},{2,0},{3,1},{4,6},{5,7},{6,4},{7,5},{8,10},{9,11},{10,... | collective-permute-start | bytes 393224 | tf_op jit(solution)/shard_map/ppermute | solution.py:472
  7.6 2.4 %block_states.2 = (bf16[4,320,512]{2,1,0:T(8,128)(2,1)S(1)}, bf16[4,320,512]{2,1,0:T(8,128)(2,1)S(1)}, bf16[512,128]{1,0:T(8,128)(2,1)S(1)}, bf16[512,128]{1,0:T...) custom-call(s32[1]{0:T(128)} %bitcast.r, bf16[320,4096]{1,0:T(8,128)(2,1)} %bitcast.18, ...), custom_call_target="tpu_custom_call" | custom-call | flops 1 | bytes 1 | tf_op jit(solution)/shard_map/block_states/pallas_call | solution.py:120
  10.0 1.9 %collective-permute-start = (bf16[512,128]{1,0:T(8,128)(2,1)S(1)}, bf16[512,128]{1,0:T(8,128)(2,1)S(1)}, u32[]{:S(2)}, u32[]{:S(2)}) collective-permute-start(bf16[512,128]{1,0:T(8,128)(2,1)S(1)} %get-tuple-element.95), channel_id=1, source_target_pairs={{0,1},{1,0},{2,3},{3,2},{4,5},{5,4},{6,7},{7,6},{8,9},{9,8},{10,11... | collective-permute-start | bytes 393224 | tf_op jit(solution)/shard_map/ppermute | solution.py:472
  12.0 1.6 %collective-permute-start.1 = (bf16[512,128]{1,0:T(8,128)(2,1)S(1)}, bf16[512,128]{1,0:T(8,128)(2,1)S(1)}, u32[]{:S(2)}, u32[]{:S(2)}) collective-permute-start(bf16[512,128]{1,0:T(8,128)(2,1)S(1)} %get-tuple-element.96), channel_id=1, source_target_pairs={{0,2},{1,3},{2,0},{3,1},{4,6},{5,7},{6,4},{7,5},{8,10},{9,11},{10,... | collective-permute-start | bytes 393224 | tf_op jit(solution)/shard_map/ppermute | solution.py:472
  13.6 0.5 collective-permute-done.5.refs_3_
  14.2 4.7 %collective-permute-start.7 = (bf16[512,128]{1,0:T(8,128)(2,1)S(1)}, bf16[512,128]{1,0:T(8,128)(2,1)S(1)}, u32[]{:S(2)}, u32[]{:S(2)}) collective-permute-start(bf16[512,128]{1,0:T(8,128)(2,1)S(1)} %group_total.4.refs_5_), channel_id=1, source_target_pairs={{0,4},{1,5},{2,6},{3,7},{8,12},{9,13},{10,14},{11,15},{16,20},{17,... | collective-permute-start | bytes 393224 | tf_op jit(solution)/shard_map/ppermute | solution.py:496
  18.9 3.5 %within_block.2 = (bf16[4,320,512]{2,1,0:T(8,128)(2,1)S(1)}, bf16[4,320,512]{2,1,0:T(8,128)(2,1)S(1)}, f32[4,1,512]{2,1,0:T(1,128)S(1)}, f32[4,320,512]{2,1,0:T(...) custom-call(s32[1]{0:T(128)} %bitcast.r, bf16[320,4096]{1,0:T(8,128)(2,1)} %bitcast.13, ...), custom_call_target="tpu_custom_call" | custom-call | flops 1 | bytes 1 | tf_op jit(solution)/shard_map/within_block/pallas_call | solution.py:120
  22.5 2.3 %collective-permute-start.6 = (bf16[512,128]{1,0:T(8,128)(2,1)S(1)}, bf16[512,128]{1,0:T(8,128)(2,1)S(1)}, u32[]{:S(2)}, u32[]{:S(2)}) collective-permute-start(bf16[512,128]{1,0:T(8,128)(2,1)S(1)} %group_total.5.refs_5_), channel_id=1, source_target_pairs={{0,4},{1,5},{2,6},{3,7},{8,12},{9,13},{10,14},{11,15},{16,20},{17,... | collective-permute-start | bytes 393224 | tf_op jit(solution)/shard_map/ppermute | solution.py:496
  24.8 3.5 %within_block.3 = (bf16[4,320,512]{2,1,0:T(8,128)(2,1)S(1)}, bf16[4,320,512]{2,1,0:T(8,128)(2,1)S(1)}, f32[4,1,512]{2,1,0:T(1,128)S(1)}, f32[4,320,512]{2,1,0:T(...) custom-call(s32[1]{0:T(128)} %bitcast.r, bf16[320,4096]{1,0:T(8,128)(2,1)} %bitcast.14, ...), custom_call_target="tpu_custom_call" | custom-call | flops 1 | bytes 1 | tf_op jit(solution)/shard_map/within_block/pallas_call | solution.py:120
  28.5 1.0 %collective-permute-start.11 = (bf16[512,128]{1,0:T(8,128)(2,1)S(1)}, bf16[512,128]{1,0:T(8,128)(2,1)S(1)}, u32[]{:S(2)}, u32[]{:S(2)}) collective-permute-start(bf16[512,128]{1,0:T(8,128)(2,1)S(1)} %get-tuple-element.120), channel_id=1, source_target_pairs={{0,1},{1,0},{2,3},{3,2},{4,5},{5,4},{6,7},{7,6},{8,9},{9,8},{10,11... | collective-permute-start | bytes 393224 | tf_op jit(solution)/shard_map/ppermute | solution.py:472
  29.5 3.0 %collective-permute-start.12 = (bf16[512,128]{1,0:T(8,128)(2,1)S(1)}, bf16[512,128]{1,0:T(8,128)(2,1)S(1)}, u32[]{:S(2)}, u32[]{:S(2)}) collective-permute-start(bf16[512,128]{1,0:T(8,128)(2,1)S(1)} %get-tuple-element.121), channel_id=1, source_target_pairs={{0,2},{1,3},{2,0},{3,1},{4,6},{5,7},{6,4},{7,5},{8,10},{9,11},{10,... | collective-permute-start | bytes 393224 | tf_op jit(solution)/shard_map/ppermute | solution.py:472
  32.9 1.5 %collective-permute-start.8 = (bf16[512,128]{1,0:T(8,128)(2,1)S(1)}, bf16[512,128]{1,0:T(8,128)(2,1)S(1)}, u32[]{:S(2)}, u32[]{:S(2)}) collective-permute-start(bf16[512,128]{1,0:T(8,128)(2,1)S(1)} %get-tuple-element.114), channel_id=1, source_target_pairs={{0,1},{1,0},{2,3},{3,2},{4,5},{5,4},{6,7},{7,6},{8,9},{9,8},{10,11... | collective-permute-start | bytes 393224 | tf_op jit(solution)/shard_map/ppermute | solution.py:472
  34.3 2.0 %collective-permute-start.9 = (bf16[512,128]{1,0:T(8,128)(2,1)S(1)}, bf16[512,128]{1,0:T(8,128)(2,1)S(1)}, u32[]{:S(2)}, u32[]{:S(2)}) collective-permute-start(bf16[512,128]{1,0:T(8,128)(2,1)S(1)} %get-tuple-element.115), channel_id=1, source_target_pairs={{0,2},{1,3},{2,0},{3,1},{4,6},{5,7},{6,4},{7,5},{8,10},{9,11},{10,... | collective-permute-start | bytes 393224 | tf_op jit(solution)/shard_map/ppermute | solution.py:472
  36.3 1.7 %collective-permute-done.11.refs_5_.refs_6_ = bf16[512,128]{1,0:T(8,128)(2,1)S(1)} collective-permute-done((bf16[512,128]{1,0:T(8,128)(2,1)S(1)}, bf16[512,128]{1,0:T(8,128)(2,1)S(1)}, u32[]{:S(2)}, u32[]{:S(2)}) %collective-permute-start.11) | collective-permute-done | bytes 131104 | tf_op jit(solution)/shard_map/ppermute | solution.py:472
  38.1 0.6 mix.3
  38.7 1.9 %collective-permute-done.10.refs_8_.refs_9_.refs_7_ = bf16[1024,128]{1,0:T(8,128)(2,1)S(1)} collective-permute-done((bf16[1024,128]{1,0:T(8,128)(2,1)S(1)}, bf16[1024,128]{1,0:T(8,128)(2,1)S(1)}, u32[]{:S(2)}, u32[]{:S(2)}) %collective-permute-start.10) | collective-permute-done | bytes 262176 | tf_op jit(solution)/shard_map/ppermute | solution.py:472
  40.6 0.5 mix.4
  41.2 0.8 collective-permute-done.8.refs_5_.refs_7_
  41.9 0.8 mix.5
  42.7 1.4 %mixed_gradients.3 = (bf16[4,320,512]{2,1,0:T(8,128)(2,1)S(1)}, bf16[512,128]{1,0:T(8,128)(2,1)S(1)}, bf16[512,128]{1,0:T(8,128)(2,1)S(1)}, bf16[512,128]{1,0:T(8,128)(2,1)S(1)}, bf16[512,128]{1,0:T(8,128)(2,1)S(1)}) custom-call(s32[1]{0:T(128)} %bitcast.r, f32[4,320,512]{2,1,0:T(8,128)S(1)} %get-tuple-element.132.refs_0_, ...), custom_call_target="tpu_custom_call" | custom-call | flops 1 | bytes 1 | tf_op jit(solution)/shard_map/mixed_gradients/pallas_call | solution.py:120
  44.1 0.7 collective-permute-start.13
  44.8 1.3 %collective-permute-start.14 = (bf16[512,128]{1,0:T(8,128)(2,1)S(1)}, bf16[512,128]{1,0:T(8,128)(2,1)S(1)}, u32[]{:S(2)}, u32[]{:S(2)}) collective-permute-start(bf16[512,128]{1,0:T(8,128)(2,1)S(1)} %get-tuple-element.136), channel_id=1, source_target_pairs={{0,2},{1,3},{2,0},{3,1},{4,6},{5,7},{6,4},{7,5},{8,10},{9,11},{10,... | collective-permute-start | bytes 393224 | tf_op jit(solution)/shard_map/ppermute | solution.py:472
  46.1 1.5 %collective-permute-start.15 = (bf16[512,128]{1,0:T(8,128)(2,1)S(1)}, bf16[512,128]{1,0:T(8,128)(2,1)S(1)}, u32[]{:S(2)}, u32[]{:S(2)}) collective-permute-start(bf16[512,128]{1,0:T(8,128)(2,1)S(1)} %get-tuple-element.137), channel_id=1, source_target_pairs={{0,3},{1,2},{2,1},{3,0},{4,7},{5,6},{6,5},{7,4},{8,11},{9,10},{10,... | collective-permute-start | bytes 393224 | tf_op jit(solution)/shard_map/ppermute | solution.py:472
  47.7 1.5 %mixed_gradients.2 = (bf16[4,320,512]{2,1,0:T(8,128)(2,1)S(1)}, bf16[512,128]{1,0:T(8,128)(2,1)S(1)}, bf16[512,128]{1,0:T(8,128)(2,1)S(1)}, bf16[512,128]{1,0:T(8,128)(2,1)S(1)}, bf16[512,128]{1,0:T(8,128)(2,1)S(1)}) custom-call(s32[1]{0:T(128)} %bitcast.r, f32[4,320,512]{2,1,0:T(8,128)S(1)} %get-tuple-element.128.refs_0_, ...), custom_call_target="tpu_custom_call" | custom-call | flops 1 | bytes 1 | tf_op jit(solution)/shard_map/mixed_gradients/pallas_call | solution.py:120
  49.2 0.7 collective-permute-start.19
  49.9 1.3 %collective-permute-start.20 = (bf16[512,128]{1,0:T(8,128)(2,1)S(1)}, bf16[512,128]{1,0:T(8,128)(2,1)S(1)}, u32[]{:S(2)}, u32[]{:S(2)}) collective-permute-start(bf16[512,128]{1,0:T(8,128)(2,1)S(1)} %get-tuple-element.147), channel_id=1, source_target_pairs={{0,2},{1,3},{2,0},{3,1},{4,6},{5,7},{6,4},{7,5},{8,10},{9,11},{10,... | collective-permute-start | bytes 393224 | tf_op jit(solution)/shard_map/ppermute | solution.py:472
  51.2 1.5 %collective-permute-start.21 = (bf16[512,128]{1,0:T(8,128)(2,1)S(1)}, bf16[512,128]{1,0:T(8,128)(2,1)S(1)}, u32[]{:S(2)}, u32[]{:S(2)}) collective-permute-start(bf16[512,128]{1,0:T(8,128)(2,1)S(1)} %get-tuple-element.148), channel_id=1, source_target_pairs={{0,3},{1,2},{2,1},{3,0},{4,7},{5,6},{6,5},{7,4},{8,11},{9,10},{10,... | collective-permute-start | bytes 393224 | tf_op jit(solution)/shard_map/ppermute | solution.py:472
  52.8 0.9 %normed_output.2 = (bf16[4,320,512]{2,1,0:T(8,128)(2,1)S(1)}, f32[32,128]{1,0:T(8,128)S(1)}) custom-call(s32[1]{0:T(128)} %bitcast.r, f32[4,320,512]{2,1,0:T(8,128)S(1)} %get-tuple-element.132.refs_0_, bf16[4,320,512]{2,1,0:T(8,128)(2,1)S(1)} %get-tuple-element.117.refs_2_.refs_1_, f32[4,1,512]{2,1,0:T(1,128)S(1)} %get-tuple-element.118.refs_3_.refs_2_, ...), custom_call_target="tpu_custom_call" | custom-call | flops 1 | bytes 1 | tf_op jit(solution)/shard_map/normed_output/pallas_call | solution.py:120
  53.7 0.5 collective-permute-done.15.refs_3_
  54.3 1.3 %collective-permute-start.16 = (bf16[512,128]{1,0:T(8,128)(2,1)S(1)}, bf16[512,128]{1,0:T(8,128)(2,1)S(1)}, u32[]{:S(2)}, u32[]{:S(2)}) collective-permute-start(bf16[512,128]{1,0:T(8,128)(2,1)S(1)} %group_total.6.refs_4_), channel_id=1, source_target_pairs={{4,0},{5,1},{6,2},{7,3},{12,8},{13,9},{14,10},{15,11},{20,16},{21,... | collective-permute-start | bytes 393224 | tf_op jit(solution)/shard_map/ppermute | solution.py:496
  55.6 0.9 %normed_output.3 = (bf16[4,320,512]{2,1,0:T(8,128)(2,1)S(1)}, f32[32,128]{1,0:T(8,128)S(1)}) custom-call(s32[1]{0:T(128)} %bitcast.r, f32[4,320,512]{2,1,0:T(8,128)S(1)} %get-tuple-element.128.refs_0_, bf16[4,320,512]{2,1,0:T(8,128)(2,1)S(1)} %get-tuple-element.109.refs_6_.refs_2_.refs_1_, ...), custom_call_target="tpu_custom_call", output_to_operand_aliasing={{1}: (6, {})} | custom-call | flops 1 | bytes 1 | tf_op jit(solution)/shard_map/normed_output/pallas_call | solution.py:120
  56.6 1.5 %inner_gradients.4 = (bf16[4,320,512]{2,1,0:T(8,128)(2,1)S(1)}, f32[4,320,512]{2,1,0:T(8,128)S(1)}, f32[4,320,512]{2,1,0:T(8,128)S(1)}, f32[8,128]{1,0:T(8,128)S(1)}) custom-call(s32[1]{0:T(128)} %bitcast.r, bf16[4,4,320,256]{3,2,1,0:T(8,128)(2,1)S(1)} %get-tuple-element.140.refs_0_, bf16[4,4,64,64]{3,2,1,0:T(8,128)(2,1)S(1)} %get-tuple-element.141.refs_1_, ...), custom_call_target="tpu_custom_call" | custom-call | flops 1 | bytes 1 | tf_op jit(solution)/shard_map/inner_gradients/pallas_call | solution.py:120
  58.1 0.4 collective-permute-done.21.refs_3_
  58.6 1.5 %collective-permute-start.24 = (bf16[512,128]{1,0:T(8,128)(2,1)S(1)}, bf16[512,128]{1,0:T(8,128)(2,1)S(1)}, u32[]{:S(2)}, u32[]{:S(2)}) collective-permute-start(bf16[512,128]{1,0:T(8,128)(2,1)S(1)} %group_total.7.refs_7_), channel_id=1, source_target_pairs={{4,0},{5,1},{6,2},{7,3},{12,8},{13,9},{14,10},{15,11},{20,16},{21,... | collective-permute-start | bytes 393224 | tf_op jit(solution)/shard_map/ppermute | solution.py:496
  60.1 1.6 %collective-permute-start.18 = (f32[32,128]{1,0:T(8,128)S(1)}, f32[32,128]{1,0:T(8,128)S(1)}, u32[]{:S(2)}, u32[]{:S(2)}) collective-permute-start(f32[32,128]{1,0:T(8,128)S(1)} %gain_sum.3.refs_4_.refs_0_), channel_id=1, source_target_pairs={{0,16},{8,24},{16,0},{24,8},{1,17},{9,25},{17,1},{25,9},{2,18},{10... | collective-permute-start | bytes 49160 | tf_op jit(solution)/shard_map/ppermute | solution.py:472
  61.7 1.5 %inner_gradients.5 = (bf16[4,320,512]{2,1,0:T(8,128)(2,1)S(1)}, f32[4,320,512]{2,1,0:T(8,128)S(1)}, f32[4,320,512]{2,1,0:T(8,128)S(1)}, f32[8,128]{1,0:T(8,128)S(1)}) custom-call(s32[1]{0:T(128)} %bitcast.r, bf16[4,4,320,256]{3,2,1,0:T(8,128)(2,1)S(1)} %get-tuple-element.140.refs_0_, ...), custom_call_target="tpu_custom_call", output_to_operand_aliasing={{0}: (9, {}), {1}: (10, {}), {2}: (11, {})} | custom-call | flops 1 | bytes 1 | tf_op jit(solution)/shard_map/inner_gradients/pallas_call | solution.py:120
  63.2 0.7 collective-permute-done.18.refs_1_
  64.2 0.7 collective-permute-start.22
  64.9 0.5 collective-permute-start.23
  65.4 3.5 %collective-permute-start.25 = (f32[32,128]{1,0:T(8,128)S(1)}, f32[32,128]{1,0:T(8,128)S(1)}, u32[]{:S(2)}, u32[]{:S(2)}) collective-permute-start(f32[32,128]{1,0:T(8,128)S(1)} %gain_sum.4.refs_5_.refs_0_), channel_id=1, source_target_pairs={{0,4},{1,5},{2,6},{3,7},{4,0},{5,1},{6,2},{7,3},{8,12},{9,13},{10,... | collective-permute-start | bytes 49160 | tf_op jit(solution)/shard_map/ppermute | solution.py:472
  68.9 2.8 %inner_gradients.6 = (bf16[4,320,512]{2,1,0:T(8,128)(2,1)S(1)}, f32[4,320,512]{2,1,0:T(8,128)S(1)}, f32[4,320,512]{2,1,0:T(8,128)S(1)}, f32[8,128]{1,0:T(8,128)S(1)}) custom-call(s32[1]{0:T(128)} %bitcast.r, bf16[4,4,320,256]{3,2,1,0:T(8,128)(2,1)S(1)} %get-tuple-element.140.refs_0_, ...), custom_call_target="tpu_custom_call", output_to_operand_aliasing={{0}: (10, {}), {1}: (11, {}), {2}: (12, {})} | custom-call | flops 1 | bytes 1 | tf_op jit(solution)/shard_map/inner_gradients/pallas_call | solution.py:120
  72.0 2.7 %collective-permute-start.28 = (bf16[1088,128]{1,0:T(8,128)(2,1)S(1)}, bf16[1088,128]{1,0:T(8,128)(2,1)S(1)}, u32[]{:S(2)}, u32[]{:S(2)}) collective-permute-start(bf16[1088,128]{1,0:T(8,128)(2,1)S(1)} %get-tuple-element.170), channel_id=1, source_target_pairs={{0,3},{1,2},{2,1},{3,0},{4,7},{5,6},{6,5},{7,4},{8,11},{9,10},{10,... | collective-permute-start | bytes 835592 | tf_op jit(solution)/shard_map/ppermute | solution.py:472
  74.8 0.6 collective-permute-start.26
  75.6 7.1 %inner_gradients.7 = (bf16[4,320,512]{2,1,0:T(8,128)(2,1)S(1)}, f32[4,320,512]{2,1,0:T(8,128)S(1)}, f32[4,320,512]{2,1,0:T(8,128)S(1)}, f32[8,128]{1,0:T(8,128)}...) custom-call(s32[1]{0:T(128)} %bitcast.r, ...), custom_call_target="tpu_custom_call" | custom-call | flops 2000000000 | bytes 7200001 | tf_op jit(solution)/shard_map/inner_gradients/pallas_call | solution.py:120
  82.7 0.7 collective-permute-done.26.refs_9_
  83.4 2.2 %outer_gradients.1 = (bf16[320,4096]{1,0:T(8,128)(2,1)}, bf16[320,4096]{1,0:T(8,128)(2,1)}, bf16[320,4096]{1,0:T(8,128)(2,1)}, f32[32,128]{1,0:T(8,128)}) custom-call(s32[1]{0:T(128)} %bitcast.r, bf16[4,320,512]{2,1,0:T(8,128)(2,1)S(1)} %get-tuple-element.98.refs_3_.refs_13_.refs_0_, ...), custom_call_target="tpu_custom_call", output_to_operand_aliasing={{0}: (15, {}), {1}: (16, {}), {2}: (17, {})} | custom-call | flops 1 | bytes 1 | tf_op jit(solution)/shard_map/outer_gradients/pallas_call | solution.py:120
  (39 shorter events, 1.8 us)
Async XLA Ops:
  3.0 10.6 %collective-permute-start.3 = (bf16[512,128]{1,0:T(8,128)(2,1)S(1)}, bf16[512,128]{1,0:T(8,128)(2,1)S(1)}, u32[]{:S(2)}, u32[]{:S(2)}) collective-permute-start(bf16[512,128]{1,0:T(8,128)(2,1)S(1)} %get-tuple-element.101), channel_id=1, source_target_pairs={{0,1},{1,0},{2,3},{3,2},{4,5},{5,4},{6,7},{7,6},{8,9},{9,8},{10,11... | collective-permute-start | bytes 393224 | tf_op jit(solution)/shard_map/ppermute | solution.py:472
  6.0 7.6 %collective-permute-start.4 = (bf16[512,128]{1,0:T(8,128)(2,1)S(1)}, bf16[512,128]{1,0:T(8,128)(2,1)S(1)}, u32[]{:S(2)}, u32[]{:S(2)}) collective-permute-start(bf16[512,128]{1,0:T(8,128)(2,1)S(1)} %get-tuple-element.102), channel_id=1, source_target_pairs={{0,2},{1,3},{2,0},{3,1},{4,6},{5,7},{6,4},{7,5},{8,10},{9,11},{10,... | collective-permute-start | bytes 393224 | tf_op jit(solution)/shard_map/ppermute | solution.py:472
  7.6 11.3 %copy-start = (f32[4096]{0:T(1024)S(1)}, f32[4096]{0:T(1024)}, u32[]{:S(2)}) copy-start(f32[4096]{0:T(1024)} %param.8) | copy-start | bytes 49156
  7.6 6.4 %collective-permute-start.5 = (bf16[512,128]{1,0:T(8,128)(2,1)S(1)}, bf16[512,128]{1,0:T(8,128)(2,1)S(1)}, u32[]{:S(2)}, u32[]{:S(2)}) collective-permute-start(bf16[512,128]{1,0:T(8,128)(2,1)S(1)} %get-tuple-element.103), channel_id=1, source_target_pairs={{0,3},{1,2},{2,1},{3,0},{4,7},{5,6},{6,5},{7,4},{8,11},{9,10},{10,... | collective-permute-start | bytes 393224 | tf_op jit(solution)/shard_map/ppermute | solution.py:472
  10.0 12.3 %collective-permute-start = (bf16[512,128]{1,0:T(8,128)(2,1)S(1)}, bf16[512,128]{1,0:T(8,128)(2,1)S(1)}, u32[]{:S(2)}, u32[]{:S(2)}) collective-permute-start(bf16[512,128]{1,0:T(8,128)(2,1)S(1)} %get-tuple-element.95), channel_id=1, source_target_pairs={{0,1},{1,0},{2,3},{3,2},{4,5},{5,4},{6,7},{7,6},{8,9},{9,8},{10,11... | collective-permute-start | bytes 393224 | tf_op jit(solution)/shard_map/ppermute | solution.py:472
  12.0 10.4 %collective-permute-start.1 = (bf16[512,128]{1,0:T(8,128)(2,1)S(1)}, bf16[512,128]{1,0:T(8,128)(2,1)S(1)}, u32[]{:S(2)}, u32[]{:S(2)}) collective-permute-start(bf16[512,128]{1,0:T(8,128)(2,1)S(1)} %get-tuple-element.96), channel_id=1, source_target_pairs={{0,2},{1,3},{2,0},{3,1},{4,6},{5,7},{6,4},{7,5},{8,10},{9,11},{10,... | collective-permute-start | bytes 393224 | tf_op jit(solution)/shard_map/ppermute | solution.py:472
  13.6 8.8 %collective-permute-start.2 = (bf16[512,128]{1,0:T(8,128)(2,1)S(1)}, bf16[512,128]{1,0:T(8,128)(2,1)S(1)}, u32[]{:S(2)}, u32[]{:S(2)}) collective-permute-start(bf16[512,128]{1,0:T(8,128)(2,1)S(1)} %get-tuple-element.97), channel_id=1, source_target_pairs={{0,3},{1,2},{2,1},{3,0},{4,7},{5,6},{6,5},{7,4},{8,11},{9,10},{10,... | collective-permute-start | bytes 393224 | tf_op jit(solution)/shard_map/ppermute | solution.py:472
  14.2 14.1 %collective-permute-start.7 = (bf16[512,128]{1,0:T(8,128)(2,1)S(1)}, bf16[512,128]{1,0:T(8,128)(2,1)S(1)}, u32[]{:S(2)}, u32[]{:S(2)}) collective-permute-start(bf16[512,128]{1,0:T(8,128)(2,1)S(1)} %group_total.4.refs_5_), channel_id=1, source_target_pairs={{0,4},{1,5},{2,6},{3,7},{8,12},{9,13},{10,14},{11,15},{16,20},{17,... | collective-permute-start | bytes 393224 | tf_op jit(solution)/shard_map/ppermute | solution.py:496
  22.5 10.0 %collective-permute-start.6 = (bf16[512,128]{1,0:T(8,128)(2,1)S(1)}, bf16[512,128]{1,0:T(8,128)(2,1)S(1)}, u32[]{:S(2)}, u32[]{:S(2)}) collective-permute-start(bf16[512,128]{1,0:T(8,128)(2,1)S(1)} %group_total.5.refs_5_), channel_id=1, source_target_pairs={{0,4},{1,5},{2,6},{3,7},{8,12},{9,13},{10,14},{11,15},{16,20},{17,... | collective-permute-start | bytes 393224 | tf_op jit(solution)/shard_map/ppermute | solution.py:496
  28.5 9.5 %collective-permute-start.11 = (bf16[512,128]{1,0:T(8,128)(2,1)S(1)}, bf16[512,128]{1,0:T(8,128)(2,1)S(1)}, u32[]{:S(2)}, u32[]{:S(2)}) collective-permute-start(bf16[512,128]{1,0:T(8,128)(2,1)S(1)} %get-tuple-element.120), channel_id=1, source_target_pairs={{0,1},{1,0},{2,3},{3,2},{4,5},{5,4},{6,7},{7,6},{8,9},{9,8},{10,11... | collective-permute-start | bytes 393224 | tf_op jit(solution)/shard_map/ppermute | solution.py:472
  29.5 8.6 %collective-permute-start.12 = (bf16[512,128]{1,0:T(8,128)(2,1)S(1)}, bf16[512,128]{1,0:T(8,128)(2,1)S(1)}, u32[]{:S(2)}, u32[]{:S(2)}) collective-permute-start(bf16[512,128]{1,0:T(8,128)(2,1)S(1)} %get-tuple-element.121), channel_id=1, source_target_pairs={{0,2},{1,3},{2,0},{3,1},{4,6},{5,7},{6,4},{7,5},{8,10},{9,11},{10,... | collective-permute-start | bytes 393224 | tf_op jit(solution)/shard_map/ppermute | solution.py:472
  32.8 7.9 %collective-permute-start.10 = (bf16[1024,128]{1,0:T(8,128)(2,1)S(1)}, bf16[1024,128]{1,0:T(8,128)(2,1)S(1)}, u32[]{:S(2)}, u32[]{:S(2)}) collective-permute-start(bf16[1024,128]{1,0:T(8,128)(2,1)S(1)} %get-tuple-element.119), channel_id=1, source_target_pairs={{0,3},{1,2},{2,1},{3,0},{4,7},{5,6},{6,5},{7,4},{8,11},{9,10},{10,... | collective-permute-start | bytes 786440 | tf_op jit(solution)/shard_map/ppermute | solution.py:472
  32.9 9.1 %collective-permute-start.8 = (bf16[512,128]{1,0:T(8,128)(2,1)S(1)}, bf16[512,128]{1,0:T(8,128)(2,1)S(1)}, u32[]{:S(2)}, u32[]{:S(2)}) collective-permute-start(bf16[512,128]{1,0:T(8,128)(2,1)S(1)} %get-tuple-element.114), channel_id=1, source_target_pairs={{0,1},{1,0},{2,3},{3,2},{4,5},{5,4},{6,7},{7,6},{8,9},{9,8},{10,11... | collective-permute-start | bytes 393224 | tf_op jit(solution)/shard_map/ppermute | solution.py:472
  34.3 7.6 %collective-permute-start.9 = (bf16[512,128]{1,0:T(8,128)(2,1)S(1)}, bf16[512,128]{1,0:T(8,128)(2,1)S(1)}, u32[]{:S(2)}, u32[]{:S(2)}) collective-permute-start(bf16[512,128]{1,0:T(8,128)(2,1)S(1)} %get-tuple-element.115), channel_id=1, source_target_pairs={{0,2},{1,3},{2,0},{3,1},{4,6},{5,7},{6,4},{7,5},{8,10},{9,11},{10,... | collective-permute-start | bytes 393224 | tf_op jit(solution)/shard_map/ppermute | solution.py:472
  44.1 7.1 %collective-permute-start.13 = (bf16[512,128]{1,0:T(8,128)(2,1)S(1)}, bf16[512,128]{1,0:T(8,128)(2,1)S(1)}, u32[]{:S(2)}, u32[]{:S(2)}) collective-permute-start(bf16[512,128]{1,0:T(8,128)(2,1)S(1)} %get-tuple-element.135), channel_id=1, source_target_pairs={{0,1},{1,0},{2,3},{3,2},{4,5},{5,4},{6,7},{7,6},{8,9},{9,8},{10,11... | collective-permute-start | bytes 393224 | tf_op jit(solution)/shard_map/ppermute | solution.py:472
  44.8 8.9 %collective-permute-start.14 = (bf16[512,128]{1,0:T(8,128)(2,1)S(1)}, bf16[512,128]{1,0:T(8,128)(2,1)S(1)}, u32[]{:S(2)}, u32[]{:S(2)}) collective-permute-start(bf16[512,128]{1,0:T(8,128)(2,1)S(1)} %get-tuple-element.136), channel_id=1, source_target_pairs={{0,2},{1,3},{2,0},{3,1},{4,6},{5,7},{6,4},{7,5},{8,10},{9,11},{10,... | collective-permute-start | bytes 393224 | tf_op jit(solution)/shard_map/ppermute | solution.py:472
  46.1 8.0 %collective-permute-start.15 = (bf16[512,128]{1,0:T(8,128)(2,1)S(1)}, bf16[512,128]{1,0:T(8,128)(2,1)S(1)}, u32[]{:S(2)}, u32[]{:S(2)}) collective-permute-start(bf16[512,128]{1,0:T(8,128)(2,1)S(1)} %get-tuple-element.137), channel_id=1, source_target_pairs={{0,3},{1,2},{2,1},{3,0},{4,7},{5,6},{6,5},{7,4},{8,11},{9,10},{10,... | collective-permute-start | bytes 393224 | tf_op jit(solution)/shard_map/ppermute | solution.py:472
  49.2 8.9 %collective-permute-start.19 = (bf16[512,128]{1,0:T(8,128)(2,1)S(1)}, bf16[512,128]{1,0:T(8,128)(2,1)S(1)}, u32[]{:S(2)}, u32[]{:S(2)}) collective-permute-start(bf16[512,128]{1,0:T(8,128)(2,1)S(1)} %get-tuple-element.146), channel_id=1, source_target_pairs={{0,1},{1,0},{2,3},{3,2},{4,5},{5,4},{6,7},{7,6},{8,9},{9,8},{10,11... | collective-permute-start | bytes 393224 | tf_op jit(solution)/shard_map/ppermute | solution.py:472
  49.9 8.2 %collective-permute-start.20 = (bf16[512,128]{1,0:T(8,128)(2,1)S(1)}, bf16[512,128]{1,0:T(8,128)(2,1)S(1)}, u32[]{:S(2)}, u32[]{:S(2)}) collective-permute-start(bf16[512,128]{1,0:T(8,128)(2,1)S(1)} %get-tuple-element.147), channel_id=1, source_target_pairs={{0,2},{1,3},{2,0},{3,1},{4,6},{5,7},{6,4},{7,5},{8,10},{9,11},{10,... | collective-permute-start | bytes 393224 | tf_op jit(solution)/shard_map/ppermute | solution.py:472
  51.2 7.3 %collective-permute-start.21 = (bf16[512,128]{1,0:T(8,128)(2,1)S(1)}, bf16[512,128]{1,0:T(8,128)(2,1)S(1)}, u32[]{:S(2)}, u32[]{:S(2)}) collective-permute-start(bf16[512,128]{1,0:T(8,128)(2,1)S(1)} %get-tuple-element.148), channel_id=1, source_target_pairs={{0,3},{1,2},{2,1},{3,0},{4,7},{5,6},{6,5},{7,4},{8,11},{9,10},{10,... | collective-permute-start | bytes 393224 | tf_op jit(solution)/shard_map/ppermute | solution.py:472
  54.3 9.7 %collective-permute-start.16 = (bf16[512,128]{1,0:T(8,128)(2,1)S(1)}, bf16[512,128]{1,0:T(8,128)(2,1)S(1)}, u32[]{:S(2)}, u32[]{:S(2)}) collective-permute-start(bf16[512,128]{1,0:T(8,128)(2,1)S(1)} %group_total.6.refs_4_), channel_id=1, source_target_pairs={{4,0},{5,1},{6,2},{7,3},{12,8},{13,9},{14,10},{15,11},{20,16},{21,... | collective-permute-start | bytes 393224 | tf_op jit(solution)/shard_map/ppermute | solution.py:496
  56.5 1.6 %collective-permute-start.17 = (f32[32,128]{1,0:T(8,128)S(1)}, f32[32,128]{1,0:T(8,128)S(1)}, u32[]{:S(2)}, u32[]{:S(2)}) collective-permute-start(f32[32,128]{1,0:T(8,128)S(1)} %get-tuple-element.143.refs_7_.refs_0_), channel_id=1, source_target_pairs={{0,8},{8,0},{16,24},{24,16},{1,9},{9,1},{17,25},{25,17},{2,10},{10... | collective-permute-start | bytes 49160 | tf_op jit(solution)/shard_map/ppermute | solution.py:472
  58.6 13.2 %collective-permute-start.24 = (bf16[512,128]{1,0:T(8,128)(2,1)S(1)}, bf16[512,128]{1,0:T(8,128)(2,1)S(1)}, u32[]{:S(2)}, u32[]{:S(2)}) collective-permute-start(bf16[512,128]{1,0:T(8,128)(2,1)S(1)} %group_total.7.refs_7_), channel_id=1, source_target_pairs={{4,0},{5,1},{6,2},{7,3},{12,8},{13,9},{14,10},{15,11},{20,16},{21,... | collective-permute-start | bytes 393224 | tf_op jit(solution)/shard_map/ppermute | solution.py:496
  60.1 3.8 %collective-permute-start.18 = (f32[32,128]{1,0:T(8,128)S(1)}, f32[32,128]{1,0:T(8,128)S(1)}, u32[]{:S(2)}, u32[]{:S(2)}) collective-permute-start(f32[32,128]{1,0:T(8,128)S(1)} %gain_sum.3.refs_4_.refs_0_), channel_id=1, source_target_pairs={{0,16},{8,24},{16,0},{24,8},{1,17},{9,25},{17,1},{25,9},{2,18},{10... | collective-permute-start | bytes 49160 | tf_op jit(solution)/shard_map/ppermute | solution.py:472
  64.2 11.4 %collective-permute-start.22 = (bf16[512,128]{1,0:T(8,128)(2,1)S(1)}, bf16[512,128]{1,0:T(8,128)(2,1)S(1)}, u32[]{:S(2)}, u32[]{:S(2)}) collective-permute-start(bf16[512,128]{1,0:T(8,128)(2,1)S(1)} %get-tuple-element.160), channel_id=1, source_target_pairs={{0,1},{1,0},{2,3},{3,2},{4,5},{5,4},{6,7},{7,6},{8,9},{9,8},{10,11... | collective-permute-start | bytes 393224 | tf_op jit(solution)/shard_map/ppermute | solution.py:472
  64.9 10.7 %collective-permute-start.23 = (bf16[512,128]{1,0:T(8,128)(2,1)S(1)}, bf16[512,128]{1,0:T(8,128)(2,1)S(1)}, u32[]{:S(2)}, u32[]{:S(2)}) collective-permute-start(bf16[512,128]{1,0:T(8,128)(2,1)S(1)} %get-tuple-element.161), channel_id=1, source_target_pairs={{0,2},{1,3},{2,0},{3,1},{4,6},{5,7},{6,4},{7,5},{8,10},{9,11},{10,... | collective-permute-start | bytes 393224 | tf_op jit(solution)/shard_map/ppermute | solution.py:472
  65.4 6.3 %collective-permute-start.25 = (f32[32,128]{1,0:T(8,128)S(1)}, f32[32,128]{1,0:T(8,128)S(1)}, u32[]{:S(2)}, u32[]{:S(2)}) collective-permute-start(f32[32,128]{1,0:T(8,128)S(1)} %gain_sum.4.refs_5_.refs_0_), channel_id=1, source_target_pairs={{0,4},{1,5},{2,6},{3,7},{4,0},{5,1},{6,2},{7,3},{8,12},{9,13},{10,... | collective-permute-start | bytes 49160 | tf_op jit(solution)/shard_map/ppermute | solution.py:472
  72.0 11.4 %collective-permute-start.28 = (bf16[1088,128]{1,0:T(8,128)(2,1)S(1)}, bf16[1088,128]{1,0:T(8,128)(2,1)S(1)}, u32[]{:S(2)}, u32[]{:S(2)}) collective-permute-start(bf16[1088,128]{1,0:T(8,128)(2,1)S(1)} %get-tuple-element.170), channel_id=1, source_target_pairs={{0,3},{1,2},{2,1},{3,0},{4,7},{5,6},{6,5},{7,4},{8,11},{9,10},{10,... | collective-permute-start | bytes 835592 | tf_op jit(solution)/shard_map/ppermute | solution.py:472
  74.8 8.6 %collective-permute-start.26 = (bf16[576,128]{1,0:T(8,128)(2,1)S(1)}, bf16[576,128]{1,0:T(8,128)(2,1)S(1)}, u32[]{:S(2)}, u32[]{:S(2)}) collective-permute-start(bf16[576,128]{1,0:T(8,128)(2,1)S(1)} %get-tuple-element.168), channel_id=1, source_target_pairs={{0,1},{1,0},{2,3},{3,2},{4,5},{5,4},{6,7},{7,6},{8,9},{9,8},{10,11... | collective-permute-start | bytes 442376 | tf_op jit(solution)/shard_map/ppermute | solution.py:472
  75.4 8.0 %collective-permute-start.27 = (bf16[576,128]{1,0:T(8,128)(2,1)S(1)}, bf16[576,128]{1,0:T(8,128)(2,1)S(1)}, u32[]{:S(2)}, u32[]{:S(2)}) collective-permute-start(bf16[576,128]{1,0:T(8,128)(2,1)S(1)} %get-tuple-element.169), channel_id=1, source_target_pairs={{0,2},{1,3},{2,0},{3,1},{4,6},{5,7},{6,4},{7,5},{8,10},{9,11},{10,... | collective-permute-start | bytes 442376 | tf_op jit(solution)/shard_map/ppermute | solution.py:472
